TPU v7x, 32 devices: a whole 2x2x4 slice. The times are simulated.
32 devices in a mesh: dp: 2 (over x), row: 8 (over z, y), col: 2 (over core).
Axes of the slice: x: 2, y: 2, z: 4, core: 2. Of those that a mesh axis runs over, the one named last changes fastest.
Arguments:
- tokens_in: bfloat16 [32768, 1024], P(('dp', 'row', 'col'))
- grad_out: bfloat16 [32768, 1024], P(('dp', 'row', 'col')), may hold values from -6 to 6
- gain_attn: bfloat16 [1024], P(('row', 'col')), may hold values from 0.099609375 to 1.8984375
- gain_ffn: bfloat16 [1024], P(('row', 'col')), may hold values from 0.099609375 to 1.8984375
- w_query: bfloat16 [1024, 1024], P('row', 'col'), may hold values from -0.1875 to 0.1875
- w_key: bfloat16 [1024, 1024], P('row', 'col'), may hold values from -0.1875 to 0.1875
- w_value: bfloat16 [1024, 1024], P('row', 'col'), may hold values from -0.1875 to 0.1875
- w_gate: bfloat16 [1024, 1024], P('row', 'col'), may hold values from -0.1875 to 0.1875
- w_out: bfloat16 [1024, 1024], P('row', 'col'), may hold values from -0.375 to 0.375
- w_ffn_gate: bfloat16 [1024, 2816], P('row', 'col'), may hold values from -0.1875 to 0.1875
- w_ffn_up: bfloat16 [1024, 2816], P('row', 'col'), may hold values from -0.1875 to 0.1875
- w_ffn_down: bfloat16 [2816, 1024], P('row', 'col'), may hold values from -0.109375 to 0.109375
- persist_key: bfloat16 [16, 1024], P(None, ('row', 'col')), may hold values from -6 to 6
- persist_value: bfloat16 [16, 1024], P(None, ('row', 'col')), may hold values from -6 to 6
- mem_rate: float32 [16, 8], P(None, 'col'), may hold values from 0.05 to 0.5
- mem_momentum: float32 [16, 8], P(None, 'col'), may hold values from 0.2 to 0.9
- mem_forget: float32 [16, 8], P(None, 'col'), may hold values from 0.002 to 0.5
- segment_ids: int32 [32768], P(('dp', 'row')), may hold values from 0 to 31, as said below
- decay_index: int32 [512], P(('dp', 'row')), may hold values from 0 to 15
Outputs:
- out: bfloat16 [32768, 1024], P(('dp', 'row', 'col'))
- grad_in: bfloat16 [32768, 1024], P(('dp', 'row', 'col'))
- g_query: float32 [1024, 1024], P('row', 'col')
- g_key: float32 [1024, 1024], P('row', 'col')
- g_value: float32 [1024, 1024], P('row', 'col')
- g_gate: float32 [1024, 1024], P('row', 'col')
- g_out: float32 [1024, 1024], P('row', 'col')
- g_ffn_gate: float32 [1024, 2816], P('row', 'col')
- g_ffn_up: float32 [1024, 2816], P('row', 'col')
- g_ffn_down: float32 [2816, 1024], P('row', 'col')
- g_gain_attn: float32 [1024], P(('row', 'col'))
- g_gain_ffn: float32 [1024], P(('row', 'col'))
- g_persist_key: float32 [16, 1024], P(None, ('row', 'col'))
- g_persist_value: float32 [16, 1024], P(None, ('row', 'col'))
- rms_stats: float32 [3], replicated
Inputs may be any that keep to these rules, and one draw needn't show every extreme that they name: `segment_ids`: within each aligned sequence of 2048 tokens the ids start at 0, never fall, and change exactly at document starts; the last document of every sequence has id 2048 // 64 - 1. Documents cover whole aligned blocks of 64 tokens, and every sequence holds two documents or more.
All inputs are finite; a program needn't handle non-finite values.
Results may differ from a plain program's by a relative error of at most 0.015.
Values may be sent and summed in bfloat16 or wider, within the bound.
A program may use at most 256 MiB of HBM per device.

v0:
```python
import jax
import jax.numpy as jnp
from jax import lax
from jax.sharding import PartitionSpec as P

HD = 128
P_SIZE = 16
SEG = 1024
CH = 64
SEQ = 2048


EPS = 1e-06
NEG = -1e30
HIGH = lax.Precision.HIGHEST


def plain_dot(first_op, second_op):
    return jnp.dot(first_op, second_op, preferred_element_type=jnp.float32)


def dot_trans_right(first_op, second_op):
    return lax.dot_general(
        first_op, second_op, (((1,), (1,)), ((), ())), preferred_element_type=jnp.float32
    )


def dot_trans_left(first_op, second_op):
    return lax.dot_general(
        first_op, second_op, (((0,), (0,)), ((), ())), preferred_element_type=jnp.float32
    )


def norm_forward(values, gain_vec):
    inverse = lax.rsqrt(jnp.mean(values * values, axis=-1, keepdims=True) + EPS)
    return (values * inverse * gain_vec, inverse)


def norm_backward(values, inverse, gain_vec, upstream):
    weighted = upstream * gain_vec
    row_inner = jnp.mean(weighted * values, axis=-1, keepdims=True)
    grad_values = weighted * inverse - values * (inverse * inverse * inverse) * row_inner
    grad_gain = jnp.sum(upstream * values * inverse, axis=0)
    return (grad_values, grad_gain)


def fetch_first(params):
    col_section = (
        lax.all_gather(params[0], "col", axis=1, tiled=True),
        lax.all_gather(params[1], "col", axis=1, tiled=True),
        lax.all_gather(params[2], "col", axis=1, tiled=True),
        lax.all_gather(params[3], "col", axis=1, tiled=True),
        lax.all_gather(params[4], "col", axis=1, tiled=True),
        lax.all_gather(params[5], "col", axis=1, tiled=True),
        lax.all_gather(params[6], "col", axis=1, tiled=True),
        lax.all_gather(params[7], "col", axis=1, tiled=True),
        lax.all_gather(params[8], "col", axis=0, tiled=True),
        lax.all_gather(params[9], "col", axis=0, tiled=True),
        lax.all_gather(params[10], "col", axis=1, tiled=True),
        lax.all_gather(params[11], "col", axis=1, tiled=True),
    )
    return (
        lax.all_gather(col_section[0], "row", axis=0, tiled=True),
        lax.all_gather(col_section[1], "row", axis=0, tiled=True),
        lax.all_gather(col_section[2], "row", axis=0, tiled=True),
        lax.all_gather(col_section[3], "row", axis=0, tiled=True),
        lax.all_gather(col_section[4], "row", axis=0, tiled=True),
        lax.all_gather(col_section[5], "row", axis=0, tiled=True),
        lax.all_gather(col_section[6], "row", axis=0, tiled=True),
        lax.all_gather(col_section[7], "row", axis=0, tiled=True),
        lax.all_gather(col_section[8], "row", axis=0, tiled=True),
        lax.all_gather(col_section[9], "row", axis=0, tiled=True),
        lax.all_gather(col_section[10], "row", axis=1, tiled=True),
        lax.all_gather(col_section[11], "row", axis=1, tiled=True),
    )


def fetch_again(params):
    col_section = (
        lax.all_gather(params[0], "col", axis=1, tiled=True),
        lax.all_gather(params[1], "col", axis=1, tiled=True),
        lax.all_gather(params[2], "col", axis=1, tiled=True),
        lax.all_gather(params[3], "col", axis=1, tiled=True),
        lax.all_gather(params[4], "col", axis=1, tiled=True),
        lax.all_gather(params[5], "col", axis=1, tiled=True),
        lax.all_gather(params[6], "col", axis=1, tiled=True),
        lax.all_gather(params[7], "col", axis=1, tiled=True),
        lax.all_gather(params[8], "col", axis=0, tiled=True),
        lax.all_gather(params[9], "col", axis=0, tiled=True),
        lax.all_gather(params[10], "col", axis=1, tiled=True),
        lax.all_gather(params[11], "col", axis=1, tiled=True),
    )
    return (
        lax.all_gather(col_section[0], "row", axis=0, tiled=True),
        lax.all_gather(col_section[1], "row", axis=0, tiled=True),
        lax.all_gather(col_section[2], "row", axis=0, tiled=True),
        lax.all_gather(col_section[3], "row", axis=0, tiled=True),
        lax.all_gather(col_section[4], "row", axis=0, tiled=True),
        lax.all_gather(col_section[5], "row", axis=0, tiled=True),
        lax.all_gather(col_section[6], "row", axis=0, tiled=True),
        lax.all_gather(col_section[7], "row", axis=0, tiled=True),
        lax.all_gather(col_section[8], "row", axis=0, tiled=True),
        lax.all_gather(col_section[9], "row", axis=0, tiled=True),
        lax.all_gather(col_section[10], "row", axis=1, tiled=True),
        lax.all_gather(col_section[11], "row", axis=1, tiled=True),
    )


def block_scores(query_rows, key_rows, fixed_keys, seg_ids, score_scale):
    tok_scores = (
        jnp.einsum("qhd,khd->hqk", query_rows, key_rows, preferred_element_type=jnp.float32)
        * score_scale
    )
    per_scores = (
        jnp.einsum("qhd,phd->hqp", query_rows, fixed_keys, preferred_element_type=jnp.float32)
        * score_scale
    )
    places = jnp.arange(query_rows.shape[0])
    allowed = (places[None, :] <= places[:, None]) & (seg_ids[None, :] == seg_ids[:, None])
    return (jnp.where(allowed[None, :, :], tok_scores, NEG), per_scores)


def attend_forward(inputs, fixed_keys, fixed_values, score_scale):
    query_rows, key_rows, value_rows, seg_ids = inputs
    tok_scores, per_scores = block_scores(query_rows, key_rows, fixed_keys, seg_ids, score_scale)
    row_top = jnp.maximum(
        jnp.max(tok_scores, axis=-1, keepdims=True), jnp.max(per_scores, axis=-1, keepdims=True)
    )
    tok_exp = jnp.exp(tok_scores - row_top)
    per_exp = jnp.exp(per_scores - row_top)
    row_total = jnp.sum(tok_exp, axis=-1, keepdims=True) + jnp.sum(per_exp, axis=-1, keepdims=True)
    tok_prob = (tok_exp / row_total).astype(jnp.bfloat16)
    per_prob = (per_exp / row_total).astype(jnp.bfloat16)
    output = jnp.einsum(
        "hqk,khd->qhd", tok_prob, value_rows, preferred_element_type=jnp.float32
    ) + jnp.einsum("hqp,phd->qhd", per_prob, fixed_values, preferred_element_type=jnp.float32)
    return (output, row_top + jnp.log(row_total))


def attend_backward(inputs, fixed_keys, fixed_values, score_scale):
    query_rows, key_rows, value_rows, seg_ids, log_total, upstream = inputs
    tok_scores, per_scores = block_scores(query_rows, key_rows, fixed_keys, seg_ids, score_scale)
    tok_prob = jnp.exp(tok_scores - log_total)
    per_prob = jnp.exp(per_scores - log_total)
    tok_dp = jnp.einsum("qhd,khd->hqk", upstream, value_rows, preferred_element_type=jnp.float32)
    per_dp = jnp.einsum("qhd,phd->hqp", upstream, fixed_values, preferred_element_type=jnp.float32)
    row_inner = jnp.sum(tok_prob * tok_dp, axis=-1, keepdims=True) + jnp.sum(
        per_prob * per_dp, axis=-1, keepdims=True
    )
    tok_ds = (tok_prob * (tok_dp - row_inner)).astype(jnp.bfloat16)
    per_ds = (per_prob * (per_dp - row_inner)).astype(jnp.bfloat16)
    grad_query = (
        jnp.einsum("hqk,khd->qhd", tok_ds, key_rows, preferred_element_type=jnp.float32)
        + jnp.einsum("hqp,phd->qhd", per_ds, fixed_keys, preferred_element_type=jnp.float32)
    ) * score_scale
    grad_key = (
        jnp.einsum("hqk,qhd->khd", tok_ds, query_rows, preferred_element_type=jnp.float32)
        * score_scale
    )
    grad_value = jnp.einsum(
        "hqk,qhd->khd", tok_prob.astype(jnp.bfloat16), upstream, preferred_element_type=jnp.float32
    )
    grad_fixed_key = (
        jnp.einsum("hqp,qhd->phd", per_ds, query_rows, preferred_element_type=jnp.float32)
        * score_scale
    )
    grad_fixed_value = jnp.einsum(
        "hqp,qhd->phd", per_prob.astype(jnp.bfloat16), upstream, preferred_element_type=jnp.float32
    )
    return (grad_query, grad_key, grad_value, grad_fixed_key, grad_fixed_value)


def memory_scan(query_rows, key_rows, value_rows, rate_rows, moment_rows, forget_rows, keep_flags):

    def advance(carry, inputs):
        memory, moment = carry
        span_query, span_key, span_value, span_rate, span_moment, span_forget, span_keep = inputs
        keep_now = span_keep[:, None, None]
        memory = memory * keep_now
        moment = moment * keep_now
        span_read = jnp.einsum("bcd,bde->bce", span_query, memory, precision=HIGH)
        misfit = jnp.einsum("bcd,bde->bce", span_key, memory, precision=HIGH) - span_value
        span_slope = jnp.einsum("bcd,bce->bde", span_key, misfit, precision=HIGH)
        moment = span_moment[:, None, None] * moment - span_rate[:, None, None] * span_slope
        memory = (1.0 - span_forget[:, None, None]) * memory + moment
        return ((memory, moment), span_read)

    empty_state = jnp.zeros(
        (query_rows.shape[1], query_rows.shape[3], query_rows.shape[3]), jnp.float32
    )
    ignored, memory_reads = lax.scan(
        advance,
        (empty_state, empty_state),
        (query_rows, key_rows, value_rows, rate_rows, moment_rows, forget_rows, keep_flags),
        unroll=4,
    )
    return memory_reads


def local(
    tokens_in,
    grad_out,
    gain_attn,
    gain_ffn,
    w_query,
    w_key,
    w_value,
    w_gate,
    w_out,
    w_ffn_gate,
    w_ffn_up,
    w_ffn_down,
    persist_key,
    persist_value,
    mem_rate,
    mem_momentum,
    mem_forget,
    segment_ids,
    decay_index,
):
    params = (
        w_query,
        w_key,
        w_value,
        w_gate,
        w_out,
        w_ffn_gate,
        w_ffn_up,
        w_ffn_down,
        gain_attn,
        gain_ffn,
        persist_key,
        persist_value,
    )
    weights = fetch_first(params)
    (
        full_query,
        full_key,
        full_value,
        full_gate,
        full_out,
        full_fgate,
        full_fup,
        full_fdown,
        full_gain_a,
        full_gain_f,
        full_pkey,
        full_pvalue,
    ) = weights
    gain_a = full_gain_a.astype(jnp.float32)
    gain_f = full_gain_f.astype(jnp.float32)
    inputs = tokens_in.astype(jnp.float32)
    normed_pre, inverse_a = norm_forward(inputs, gain_a)
    normed = normed_pre.astype(jnp.bfloat16)
    query_tok = plain_dot(normed, full_query).astype(jnp.bfloat16)
    key_tok = plain_dot(normed, full_key).astype(jnp.bfloat16)
    value_tok = plain_dot(normed, full_value).astype(jnp.bfloat16)
    gate_tok = plain_dot(normed, full_gate).astype(jnp.bfloat16)
    query_heads, key_heads, value_heads, gate_heads = (
        lax.all_to_all(query_tok, "col", split_axis=1, concat_axis=0, tiled=True),
        lax.all_to_all(key_tok, "col", split_axis=1, concat_axis=0, tiled=True),
        lax.all_to_all(value_tok, "col", split_axis=1, concat_axis=0, tiled=True),
        lax.all_to_all(gate_tok, "col", split_axis=1, concat_axis=0, tiled=True),
    )
    total_tok = query_heads.shape[0]
    head_count = mem_rate.shape[1]
    head_width = head_count * HD
    col_index = lax.axis_index("col")
    fixed_keys = lax.dynamic_slice_in_dim(full_pkey, col_index * head_width, head_width, 1).reshape(
        P_SIZE, head_count, HD
    )
    fixed_values = lax.dynamic_slice_in_dim(
        full_pvalue, col_index * head_width, head_width, 1
    ).reshape(P_SIZE, head_count, HD)
    score_scale = HD ** (-0.5)
    segments = total_tok // SEG

    def split_seg(values):
        return values.reshape(segments, SEG, head_count, HD)

    seg_blocks = segment_ids.reshape(segments, SEG)

    def attend_one(inputs_seg):
        return attend_forward(inputs_seg, fixed_keys, fixed_values, score_scale)

    attention, log_total = lax.map(
        attend_one,
        (split_seg(query_heads), split_seg(key_heads), split_seg(value_heads), seg_blocks),
    )
    attention_flat = attention.reshape(total_tok, head_width)
    sequences = total_tok // SEQ
    per_seq = SEQ // CH
    span_segs = segment_ids.reshape(sequences, per_seq, CH)
    same_doc = (span_segs[:, 1:, 0] == span_segs[:, :-1, CH - 1]).astype(jnp.float32)
    keep_seq = jnp.concatenate([jnp.zeros((sequences, 1), jnp.float32), same_doc], axis=1)
    keep_flags = jnp.broadcast_to(keep_seq.T[:, :, None], (per_seq, sequences, head_count)).reshape(
        per_seq, sequences * head_count
    )
    choose = (decay_index[:, None] == jnp.arange(mem_rate.shape[0])[None, :]).astype(jnp.float32)

    def table_rows(decay_table):
        picked = jnp.dot(choose, decay_table, precision=HIGH)
        return (
            picked.reshape(sequences, per_seq, head_count)
            .transpose(1, 0, 2)
            .reshape(per_seq, sequences * head_count)
        )

    def to_scan(values):
        return (
            values.reshape(sequences, per_seq, CH, head_count, HD)
            .transpose(1, 0, 3, 2, 4)
            .reshape(per_seq, sequences * head_count, CH, HD)
        )

    def from_scan(values):
        return (
            values.reshape(per_seq, sequences, head_count, CH, HD)
            .transpose(1, 0, 3, 2, 4)
            .reshape(total_tok, head_width)
        )

    rate_rows = table_rows(mem_rate)
    moment_rows = table_rows(mem_momentum)
    forget_rows = table_rows(mem_forget)

    def run_memory(query_scan, key_scan, value_scan):
        return memory_scan(
            query_scan, key_scan, value_scan, rate_rows, moment_rows, forget_rows, keep_flags
        )

    reads_scan, memory_pullback = jax.vjp(
        run_memory,
        to_scan(query_heads.astype(jnp.float32)) * score_scale,
        to_scan(key_heads.astype(jnp.float32)) * score_scale,
        to_scan(value_heads.astype(jnp.float32)),
    )
    memory_reads = from_scan(reads_scan)
    gate_sig = jax.nn.sigmoid(gate_heads.astype(jnp.float32))
    combined = (attention_flat + gate_sig * memory_reads).astype(jnp.bfloat16)
    combined_tok = lax.all_to_all(combined, "col", split_axis=0, concat_axis=1, tiled=True)
    branch = plain_dot(combined_tok, full_out)
    middle = inputs + branch
    normed2_pre, inverse_f = norm_forward(middle, gain_f)
    normed2 = normed2_pre.astype(jnp.bfloat16)
    ffn_gate = plain_dot(normed2, full_fgate)
    ffn_up = plain_dot(normed2, full_fup)
    gate_sigmoid = jax.nn.sigmoid(ffn_gate)
    silu_gate = ffn_gate * gate_sigmoid
    hidden = (silu_gate * ffn_up).astype(jnp.bfloat16)
    ffn_out = plain_dot(hidden, full_fdown)
    final_rows = middle + ffn_out
    result = final_rows.astype(jnp.bfloat16)
    sum_input, sum_branch, sum_final = lax.psum(
        (jnp.sum(inputs * inputs), jnp.sum(branch * branch), jnp.sum(final_rows * final_rows)),
        ("dp", "row", "col"),
    )
    entry_count = (
        tokens_in.shape[0]
        * tokens_in.shape[1]
        * lax.axis_size("dp")
        * lax.axis_size("row")
        * lax.axis_size("col")
    )
    rms_stats = jnp.sqrt(jnp.stack([sum_input, sum_branch, sum_final]) / entry_count)
    weights_back = fetch_again(params)
    back_query, back_key, back_value, back_gate, back_out, back_fgate, back_fup, back_fdown = (
        weights_back[:8]
    )
    grad_hidden = dot_trans_right(grad_out, back_fdown)
    g_ffn_down = dot_trans_left(hidden, grad_out)
    silu_slope = gate_sigmoid * (1.0 + ffn_gate * (1.0 - gate_sigmoid))
    grad_fgate = (grad_hidden * ffn_up * silu_slope).astype(jnp.bfloat16)
    grad_fup = (grad_hidden * silu_gate).astype(jnp.bfloat16)
    g_ffn_gate = dot_trans_left(normed2, grad_fgate)
    g_ffn_up = dot_trans_left(normed2, grad_fup)
    grad_normed2 = dot_trans_right(grad_fgate, back_fgate) + dot_trans_right(grad_fup, back_fup)
    grad_mid_norm, g_gain_f = norm_backward(middle, inverse_f, gain_f, grad_normed2)
    grad_middle = grad_out.astype(jnp.float32) + grad_mid_norm
    grad_branch = grad_middle.astype(jnp.bfloat16)
    g_out = dot_trans_left(combined_tok, grad_branch)
    grad_comb_tok = dot_trans_right(grad_branch, back_out).astype(jnp.bfloat16)
    grad_comb = lax.all_to_all(grad_comb_tok, "col", split_axis=1, concat_axis=0, tiled=True)
    grad_comb_f = grad_comb.astype(jnp.float32)
    grad_reads = grad_comb_f * gate_sig
    grad_gate = (grad_comb_f * memory_reads * gate_sig * (1.0 - gate_sig)).astype(jnp.bfloat16)

    def attend_back(inputs_seg):
        return attend_backward(inputs_seg, fixed_keys, fixed_values, score_scale)

    grad_q_att, grad_k_att, grad_v_att, grad_pk_seg, grad_pv_seg = lax.map(
        attend_back,
        (
            split_seg(query_heads),
            split_seg(key_heads),
            split_seg(value_heads),
            seg_blocks,
            log_total,
            split_seg(grad_comb),
        ),
    )
    grad_q_mem, grad_k_mem, grad_v_mem = memory_pullback(to_scan(grad_reads))
    grad_query = (
        grad_q_att.reshape(total_tok, head_width) + from_scan(grad_q_mem) * score_scale
    ).astype(jnp.bfloat16)
    grad_key = (
        grad_k_att.reshape(total_tok, head_width) + from_scan(grad_k_mem) * score_scale
    ).astype(jnp.bfloat16)
    grad_value = (grad_v_att.reshape(total_tok, head_width) + from_scan(grad_v_mem)).astype(
        jnp.bfloat16
    )
    grad_q_tok, grad_k_tok, grad_v_tok, grad_g_tok = (
        lax.all_to_all(grad_query, "col", split_axis=0, concat_axis=1, tiled=True),
        lax.all_to_all(grad_key, "col", split_axis=0, concat_axis=1, tiled=True),
        lax.all_to_all(grad_value, "col", split_axis=0, concat_axis=1, tiled=True),
        lax.all_to_all(grad_gate, "col", split_axis=0, concat_axis=1, tiled=True),
    )
    g_query = dot_trans_left(normed, grad_q_tok)
    g_key = dot_trans_left(normed, grad_k_tok)
    g_value = dot_trans_left(normed, grad_v_tok)
    g_gate = dot_trans_left(normed, grad_g_tok)
    grad_normed = (
        dot_trans_right(grad_q_tok, back_query)
        + dot_trans_right(grad_k_tok, back_key)
        + dot_trans_right(grad_v_tok, back_value)
        + dot_trans_right(grad_g_tok, back_gate)
    )
    grad_in_norm, g_gain_a = norm_backward(inputs, inverse_a, gain_a, grad_normed)
    grad_in = (grad_middle + grad_in_norm).astype(jnp.bfloat16)
    full_width = full_pkey.shape[1]
    g_pkey_full = lax.dynamic_update_slice_in_dim(
        jnp.zeros((P_SIZE, full_width), jnp.float32),
        jnp.sum(grad_pk_seg, axis=0).reshape(P_SIZE, head_width),
        col_index * head_width,
        1,
    )
    g_pvalue_full = lax.dynamic_update_slice_in_dim(
        jnp.zeros((P_SIZE, full_width), jnp.float32),
        jnp.sum(grad_pv_seg, axis=0).reshape(P_SIZE, head_width),
        col_index * head_width,
        1,
    )
    row_section = (
        lax.psum_scatter(g_query, "row", scatter_dimension=0, tiled=True),
        lax.psum_scatter(g_key, "row", scatter_dimension=0, tiled=True),
        lax.psum_scatter(g_value, "row", scatter_dimension=0, tiled=True),
        lax.psum_scatter(g_gate, "row", scatter_dimension=0, tiled=True),
        lax.psum_scatter(g_out, "row", scatter_dimension=0, tiled=True),
        lax.psum_scatter(g_ffn_gate, "row", scatter_dimension=0, tiled=True),
        lax.psum_scatter(g_ffn_up, "row", scatter_dimension=0, tiled=True),
        lax.psum_scatter(g_ffn_down, "row", scatter_dimension=0, tiled=True),
        lax.psum_scatter(g_gain_a, "row", scatter_dimension=0, tiled=True),
        lax.psum_scatter(g_gain_f, "row", scatter_dimension=0, tiled=True),
        lax.psum_scatter(g_pkey_full, "row", scatter_dimension=1, tiled=True),
        lax.psum_scatter(g_pvalue_full, "row", scatter_dimension=1, tiled=True),
    )
    blocks = (
        lax.psum_scatter(
            row_section[0].astype(jnp.bfloat16), "col", scatter_dimension=1, tiled=True
        ).astype(jnp.float32),
        lax.psum_scatter(
            row_section[1].astype(jnp.bfloat16), "col", scatter_dimension=1, tiled=True
        ).astype(jnp.float32),
        lax.psum_scatter(
            row_section[2].astype(jnp.bfloat16), "col", scatter_dimension=1, tiled=True
        ).astype(jnp.float32),
        lax.psum_scatter(
            row_section[3].astype(jnp.bfloat16), "col", scatter_dimension=1, tiled=True
        ).astype(jnp.float32),
        lax.psum_scatter(
            row_section[4].astype(jnp.bfloat16), "col", scatter_dimension=1, tiled=True
        ).astype(jnp.float32),
        lax.psum_scatter(
            row_section[5].astype(jnp.bfloat16), "col", scatter_dimension=1, tiled=True
        ).astype(jnp.float32),
        lax.psum_scatter(
            row_section[6].astype(jnp.bfloat16), "col", scatter_dimension=1, tiled=True
        ).astype(jnp.float32),
        lax.psum_scatter(
            row_section[7].astype(jnp.bfloat16), "col", scatter_dimension=1, tiled=True
        ).astype(jnp.float32),
        lax.psum_scatter(
            row_section[8].astype(jnp.bfloat16), "col", scatter_dimension=0, tiled=True
        ).astype(jnp.float32),
        lax.psum_scatter(
            row_section[9].astype(jnp.bfloat16), "col", scatter_dimension=0, tiled=True
        ).astype(jnp.float32),
        lax.psum_scatter(
            row_section[10].astype(jnp.bfloat16), "col", scatter_dimension=1, tiled=True
        ).astype(jnp.float32),
        lax.psum_scatter(
            row_section[11].astype(jnp.bfloat16), "col", scatter_dimension=1, tiled=True
        ).astype(jnp.float32),
    )
    totals = (
        lax.psum(blocks[0].astype(jnp.bfloat16), "dp").astype(jnp.float32),
        lax.psum(blocks[1].astype(jnp.bfloat16), "dp").astype(jnp.float32),
        lax.psum(blocks[2].astype(jnp.bfloat16), "dp").astype(jnp.float32),
        lax.psum(blocks[3].astype(jnp.bfloat16), "dp").astype(jnp.float32),
        lax.psum(blocks[4].astype(jnp.bfloat16), "dp").astype(jnp.float32),
        lax.psum(blocks[5].astype(jnp.bfloat16), "dp").astype(jnp.float32),
        lax.psum(blocks[6].astype(jnp.bfloat16), "dp").astype(jnp.float32),
        lax.psum(blocks[7].astype(jnp.bfloat16), "dp").astype(jnp.float32),
        lax.psum(blocks[8].astype(jnp.bfloat16), "dp").astype(jnp.float32),
        lax.psum(blocks[9].astype(jnp.bfloat16), "dp").astype(jnp.float32),
        lax.psum(blocks[10].astype(jnp.bfloat16), "dp").astype(jnp.float32),
        lax.psum(blocks[11].astype(jnp.bfloat16), "dp").astype(jnp.float32),
    )
    return (
        result,
        grad_in,
        totals[0],
        totals[1],
        totals[2],
        totals[3],
        totals[4],
        totals[5],
        totals[6],
        totals[7],
        totals[8],
        totals[9],
        totals[10],
        totals[11],
        rms_stats,
    )


def solution(mesh):
    placed = (
        P(("dp", "row", "col"), None),
        P(("dp", "row", "col"), None),
        P(("row", "col")),
        P(("row", "col")),
        P("row", "col"),
        P("row", "col"),
        P("row", "col"),
        P("row", "col"),
        P("row", "col"),
        P("row", "col"),
        P("row", "col"),
        P("row", "col"),
        P(None, ("row", "col")),
        P(None, ("row", "col")),
        P(None, "col"),
        P(None, "col"),
        P(None, "col"),
        P(("dp", "row")),
        P(("dp", "row")),
    )
    return jax.shard_map(
        local,
        mesh=mesh,
        in_specs=placed,
        out_specs=(
            P(("dp", "row", "col"), None),
            P(("dp", "row", "col"), None),
            P("row", "col"),
            P("row", "col"),
            P("row", "col"),
            P("row", "col"),
            P("row", "col"),
            P("row", "col"),
            P("row", "col"),
            P("row", "col"),
            P(("row", "col")),
            P(("row", "col")),
            P(None, ("row", "col")),
            P(None, ("row", "col")),
            P(),
        ),
        check_vma=False,
    )
```

profile of v0, /device:TPU:0, one launch (start us, length us, event | category | flops | bytes accessed | tf_op | source)
XLA Modules:
  0.0 2142.1 jit_solution(5757432867934067230)
XLA Ops:
  44.5 22.1 %all-gather = bf16[8,1,128]{2,1,0:T(2,128)(2,1)S(1)} all-gather(bf16[1,1,128]{2,1,0:T(2,128)(2,1)S(1)} %bitcast.977), channel_id=1, replica_groups=mesh['dp'=2,'row'=8,'col'=2] {'row'}, dimensions={0}, use_global_device_ids=true | all-gather | bytes 2304 | tf_op jit(solution)/shard_map/all_gather | solution.py:71
  68.6 26.1 %all_gather.99 = bf16[16,1024]{1,0:T(8,128)(2,1)S(1)} all-gather(bf16[16,128]{1,0:T(8,128)(2,1)S(1)} %bitcast.962), channel_id=1, replica_groups=mesh['dp'=2,'row'=8,'col'=2] {'row'}, dimensions={1}, use_global_device_ids=true | all-gather | bytes 36864 | tf_op jit(solution)/shard_map/all_gather | solution.py:74
  96.5 26.1 %all_gather.97 = bf16[16,1024]{1,0:T(8,128)(2,1)S(1)} all-gather(bf16[16,128]{1,0:T(8,128)(2,1)S(1)} %bitcast.963), channel_id=1, replica_groups=mesh['dp'=2,'row'=8,'col'=2] {'row'}, dimensions={1}, use_global_device_ids=true | all-gather | bytes 36864 | tf_op jit(solution)/shard_map/all_gather | solution.py:73
  123.5 16.2 all-gather.3
  144.8 6.3 all_to_all.157
  159.4 6.5 all_to_all.158
  236.6 170.0 %while.82 = (s32[]{:T(128)}, f32[4,128,128]{2,1,0:T(8,128)S(1)}, f32[4,128,128]{2,1,0:T(8,128)S(1)}, f32[8,4,4,64,128]{4,3,2,1,0:T(8,128)}, f32[8,4,4,1,1]{2,1,4...) while((s32[]{:T(128)}, f32[4,128,128]{2,1,0:T(8,128)S(1)}, ...), condition=%wide.region_8.9_spmd.clone, body=%wide.region_7.8_spmd.clone.sunk | while | flops 607912192 | bytes 15747738 | solution.py:191
  409.2 39.9 %while.80 = (s32[]{:T(128)}, f32[2,1024,4,128]{1,3,2,0:T(8,128)}, f32[2,4,1024,1]{2,1,3,0:T(4,128)S(1)}, bf16[2,1024,4,128]{1,3,2,0:T(8,128)(2,1)}, s32[2,1024]{...) while((s32[]{:T(128)}, f32[2,1024,4,128]{1,3,2,0:T(8,128)}, ...), condition=%wide.region_6.7_spmd, body=%wide.region_1.6_spmd.sunk | while | flops 2235494400 | bytes 99695264 | solution.py:286
  420.5 6.7 bitcast_dynamic-update-slice_fusion.13
  440.4 6.7 bitcast_dynamic-update-slice_fusion.13
  454.9 7.8 copy.403
  477.9 7.0 all_to_all.159
  489.4 6.5 all_to_all.160
  509.8 11.6 fusion.215
  521.4 12.0 fusion.216
  533.4 9.5 all-gather.27.cloned.1.call-done
  542.9 21.6 %multiply_convert_fusion.2 = (bf16[1024,2816]{1,0:T(8,128)(2,1)}, bf16[1024,2816]{1,0:T(8,128)(2,1)}, bf16[1024,2816]{1,0:T(8,128)(2,1)}) fusion(f32[1024,2816]{1,0:T(8,128)} %fusion.215, f32[1024,2816]{1,0:T(8,128)} %fusion.216, bf16[1024,1024]{1,0:T(8,128)(2,1)S(1)} %copy-done.20, bf16[2816,1024]{1,0:T(8,128)(2,1)} %all-gather.27.cloned.1.call-done), kind=kOutput, calls=%fused_computation.345 | convolution fusion | flops 5948833792 | bytes 48234496 | tf_op jit(solution)/shard_map/dot_general | solution.py:23
  564.5 11.8 fusion.218
  579.5 11.0 fusion.217
  590.6 11.3 multiply_reduce_fusion.4
  608.5 7.3 all_to_all.161
  627.3 12.0 fusion.219
  647.0 342.1 %while.83 = (s32[]{:T(128)}, f32[4,128,128]{2,1,0:T(8,128)S(1)}, f32[4,128,128]{2,1,0:T(8,128)S(1)}, f32[8,4,4,64,128]{4,3,2,1,0:T(8,128)}, f32[8,4,4,64,128]{4,...) while((s32[]{:T(128)}, f32[4,128,128]{2,1,0:T(8,128)S(1)}, ...), condition=%wide.region_16.17_spmd.clone, body=%wide.region_15.16_spmd.clone.sunk | while | flops 1212481536 | bytes 23070024 | solution.py:191
  989.0 7.0 broadcast_multiply_fusion
  1017.0 127.0 %while.81 = (s32[]{:T(128)}, f32[2,1024,4,128]{1,3,2,0:T(8,128)}, f32[2,1024,4,128]{1,3,2,0:T(8,128)}, f32[2,1024,4,128]{1,3,2,0:T(8,128)}, f32[2,16,4,128]{3,1,...) while((s32[]{:T(128)}, f32[2,1024,4,128]{1,3,2,0:T(8,128)}, ...), condition=%wide.region_14.15_spmd, body=%wide.region_11.14_spmd.sunk | while | flops 5495590912 | bytes 269668192 | solution.py:391
  1017.5 9.7 fusion.394
  1027.7 12.6 multiply_reduce_fusion.9
  1043.5 12.0 multiply_convert_fusion.8
  1055.5 6.5 fusion.397
  1062.6 9.4 bitcast_dynamic-update-slice_fusion.15
  1080.7 9.7 fusion.394
  1091.0 12.5 multiply_reduce_fusion.9
  1106.7 12.0 multiply_convert_fusion.8
  1118.7 6.5 fusion.397
  1125.8 9.5 bitcast_dynamic-update-slice_fusion.15
  1153.7 6.4 all_to_all.162
  1170.1 7.3 fusion.189
  1177.5 7.8 copy.402
  1200.6 6.5 all_to_all.163
  1217.1 7.8 copy.400
  1240.0 6.3 all_to_all.164
  1256.4 8.6 all_to_all.165
  1274.9 12.4 fusion.220
  1296.1 50.9 %reduce-scatter.45.cloned.1.call-done = f32[128,1024]{1,0:T(8,128)} async-done(((f32[1024,1024]{1,0:T(8,128)}), f32[128,1024]{1,0:T(8,128)}) %reduce-scatter.45.cloned.1.call-update) | async-done | bytes 524304 | tf_op jit(solution)/shard_map/reduce_scatter | solution.py:448
  1348.9 89.5 %reduce-scatter.29.cloned.1.call-done = f32[128,1024]{1,0:T(8,128)} async-done(((f32[1024,1024]{1,0:T(8,128)}), f32[128,1024]{1,0:T(8,128)}) %reduce-scatter.29.cloned.1.call-update) | async-done | bytes 524304 | tf_op jit(solution)/shard_map/reduce_scatter | solution.py:444
  1440.2 89.8 %reduce-scatter.37.cloned.1.call-done = f32[128,1024]{1,0:T(8,128)} async-done(((f32[1024,1024]{1,0:T(8,128)}), f32[128,1024]{1,0:T(8,128)}) %reduce-scatter.37.cloned.1.call-update) | async-done | bytes 524304 | tf_op jit(solution)/shard_map/reduce_scatter | solution.py:446
  1533.7 87.4 %reduce-scatter.41.cloned.1.call-done = f32[128,1024]{1,0:T(8,128)} async-done(((f32[1024,1024]{1,0:T(8,128)}), f32[128,1024]{1,0:T(8,128)}) %reduce-scatter.41.cloned.1.call-update) | async-done | bytes 524304 | tf_op jit(solution)/shard_map/reduce_scatter | solution.py:447
  1623.0 6.5 fusion.222
  1629.5 187.8 %reduce-scatter.53.cloned.1.call-done = f32[352,1024]{1,0:T(8,128)} async-done(((f32[2816,1024]{1,0:T(8,128)}), f32[352,1024]{1,0:T(8,128)}) %reduce-scatter.53.cloned.1.call-update) | async-done | bytes 1441808 | tf_op jit(solution)/shard_map/reduce_scatter | solution.py:451
  1819.8 12.4 multiply_reduce_fusion.2
  1832.1 41.4 %reduce-scatter.57.cloned.1.call-done = f32[16,128]{1,0:T(8,128)} async-done(((f32[16,1024]{1,0:T(8,128)}), f32[16,128]{1,0:T(8,128)}) %reduce-scatter.57.cloned.1.call-update) | async-done | bytes 8208 | tf_op jit(solution)/shard_map/reduce_scatter | solution.py:454
  1875.0 6.6 fusion.221
  1881.6 48.0 %reduce-scatter.59.cloned.1.call-done = f32[16,128]{1,0:T(8,128)} async-done(((f32[16,1024]{1,0:T(8,128)}), f32[16,128]{1,0:T(8,128)}) %reduce-scatter.59.cloned.1.call-update) | async-done | bytes 8208 | tf_op jit(solution)/shard_map/reduce_scatter | solution.py:455
  1931.2 6.5 fusion.223
  1941.6 10.2 reduce-scatter.63.cloned.1.call-done
  1953.7 9.9 reduce-scatter.35.cloned.1.call-done
  1963.5 11.7 reduce-scatter.47.cloned.1.call-done
  1975.2 11.7 reduce-scatter.31.cloned.1.call-done
  1986.9 11.5 reduce-scatter.39.cloned.1.call-done
  1998.4 11.7 reduce-scatter.43.cloned.1.call-done
  2010.2 12.1 reduce-scatter.55.cloned.1.call-done
  2022.3 11.8 fusion.186
  2034.1 41.1 %all-reduce.6 = (f32[1]{0:T(128)}, f32[1]{0:T(128)}, f32[1]{0:T(128)}) all-reduce(f32[1]{0:T(128)} %bitcast.94, f32[1]{0:T(128)} %bitcast.93, f32[1]{0:T(128)} %bitcast.92), channel_id=1, replica_groups=mesh['dp'=2,'row'=8,'col'=2] {'dp','row','col'}, use_global_device_ids=true, to_apply=%region_63.64 | all-reduce | flops 3 | bytes 24 | tf_op jit(solution)/shard_map/psum | solution.py:354
  2075.2 21.4 %all-reduce.7 = (bf16[1024]{0:T(1024)(128)(2,1)S(1)}, bf16[1024]{0:T(1024)(128)(2,1)S(1)}) all-reduce(f32[1024]{0:T(1024)S(1)} %get-tuple-element.984, f32[1024]{0:T(1024)S(1)} %copy-done.46), channel_id=18, replica_groups=mesh['dp'=2,'row'=8,'col'=2] {'row'}, use_global_device_ids=true, to_apply=%region_43.44.clone | all-reduce | flops 2048 | bytes 12288
  (920 shorter events, 923.9 us)
Async XLA Ops:
  7.2 115.8 %copy-start = (f32[16,4]{0,1:T(4,128)S(1)}, f32[16,4]{0,1:T(4,128)}, u32[]{:S(2)}) copy-start(f32[16,4]{0,1:T(4,128)} %param.43) | copy-start | bytes 772
  7.2 23.7 %copy-start.25 = (bf16[128,1408]{1,0:T(8,128)(2,1)S(1)}, bf16[128,1408]{1,0:T(8,128)(2,1)}, u32[]{:S(2)}) copy-start(bf16[128,1408]{1,0:T(8,128)(2,1)} %param.37) | copy-start | bytes 1081348
  7.2 26.3 %copy-start.26 = (bf16[352,512]{1,0:T(8,128)(2,1)S(1)}, bf16[352,512]{1,0:T(8,128)(2,1)}, u32[]{:S(2)}) copy-start(bf16[352,512]{1,0:T(8,128)(2,1)} %param.38) | copy-start | bytes 1081348
  7.2 133.1 %all-gather.15.cloned.1.call-start = ((), (), s32[]{:S(2)}) async-start(), calls=%async_computation.31 | async-start | bytes 2359296 | tf_op jit(solution)/shard_map/all_gather | solution.py:63
  11.3 24.7 %copy-start.42 = (s32[2048]{0:T(1024)S(1)}, s32[2048]{0:T(1024)}, u32[]{:S(2)}) copy-start(s32[2048]{0:T(1024)} %param.44) | copy-start | bytes 24580
  11.4 143.7 %all-gather.17.cloned.1.call-start = ((), (), s32[]{:S(2)}) async-start(), calls=%async_computation.32 | async-start | bytes 2359296 | tf_op jit(solution)/shard_map/all_gather | solution.py:64
  15.1 154.6 %all-gather.13.cloned.1.call-start = ((), (), s32[]{:S(2)}) async-start(), calls=%async_computation.30 | async-start | bytes 2359296 | tf_op jit(solution)/shard_map/all_gather | solution.py:65
  19.0 449.3 %all-gather.19.cloned.1.call-start = ((), (), s32[]{:S(2)}) async-start(), calls=%async_computation.33 | async-start | bytes 2359296 | tf_op jit(solution)/shard_map/all_gather | solution.py:66
  22.8 477.1 %all-gather.21.cloned.1.call-start = ((), (), s32[]{:S(2)}) async-start(), calls=%async_computation.34 | async-start | bytes 2359296 | tf_op jit(solution)/shard_map/all_gather | solution.py:67
  26.7 481.8 %all-gather.23.cloned.1.call-start = ((), (), s32[]{:S(2)}) async-start(), calls=%async_computation.35 | async-start | bytes 6488064 | tf_op jit(solution)/shard_map/all_gather | solution.py:68
  30.8 490.6 %all-gather.25.cloned.1.call-start = ((), (), s32[]{:S(2)}) async-start(), calls=%async_computation.36 | async-start | bytes 6488064 | tf_op jit(solution)/shard_map/all_gather | solution.py:69
  33.4 8.4 copy-start.52
  33.4 33.3 %copy-start.44 = (bf16[16,64]{1,0:T(8,128)(2,1)S(1)}, bf16[16,64]{1,0:T(8,128)(2,1)}, u32[]{:S(2)}) copy-start(bf16[16,64]{1,0:T(8,128)(2,1)} %param.40) | copy-start | bytes 6148
  33.4 61.2 %copy-start.45 = (bf16[16,64]{1,0:T(8,128)(2,1)S(1)}, bf16[16,64]{1,0:T(8,128)(2,1)}, u32[]{:S(2)}) copy-start(bf16[16,64]{1,0:T(8,128)(2,1)} %param.39) | copy-start | bytes 6148
  33.4 89.5 %copy-start.53 = (s32[32]{0:T(128)S(1)}, s32[32]{0:T(128)}, u32[]{:S(2)}) copy-start(s32[32]{0:T(128)} %param.45) | copy-start | bytes 388
  33.4 89.7 %copy-start.49 = (f32[16,4]{0,1:T(4,128)S(1)}, f32[16,4]{0,1:T(4,128)}, u32[]{:S(2)}) copy-start(f32[16,4]{0,1:T(4,128)} %param.42) | copy-start | bytes 772
  33.4 89.9 %copy-start.50 = (f32[16,4]{0,1:T(4,128)S(1)}, f32[16,4]{0,1:T(4,128)}, u32[]{:S(2)}) copy-start(f32[16,4]{0,1:T(4,128)} %param.41) | copy-start | bytes 772
  33.4 509.4 %all-gather.27.cloned.1.call-start = ((), (), s32[]{:S(2)}) async-start(), calls=%async_computation.37 | async-start | bytes 6488064 | tf_op jit(solution)/shard_map/all_gather | solution.py:70
  39.0 130.8 %copy-start.5 = (bf16[1024,1024]{0,1:T(8,128)(2,1)}, bf16[1024,1024]{0,1:T(8,128)(2,1)S(1)}, u32[]{:S(2)}) copy-start(bf16[1024,1024]{0,1:T(8,128)(2,1)S(1)} %copy.258) | copy-start | bytes 6291460
  40.3 129.5 %copy-start.36 = (f32[1024]{0:T(1024)}, f32[1024]{0:T(1024)S(1)}, u32[]{:S(2)}) copy-start(f32[1024]{0:T(1024)S(1)} %get-tuple-element.1222) | copy-start | bytes 12292
  66.7 103.1 %copy-start.39 = (f32[8,1,128]{2,1,0:T(1,128)}, f32[8,1,128]{2,1,0:T(1,128)S(1)}, u32[]{:S(2)}) copy-start(f32[8,1,128]{2,1,0:T(1,128)S(1)} %convert_element_type.317) | copy-start | bytes 12292
  175.3 41.5 %all-to-all-start = ((bf16[1024,2,512]{0,2,1:T(8,128)(2,1)}), bf16[1024,2,512]{0,2,1:T(8,128)(2,1)}, u32[]{:S(2)}, u32[]{:S(2)}) async-start(bf16[1024,2,512]{0,2,1:T(8,128)(2,1)} %bitcast.934), calls=%async_computation | async-start | bytes 4194304 | tf_op jit(solution)/shard_map/all_to_all | solution.py:262
  180.3 1108.6 %reduce-scatter.49.cloned.1.call-start = ((), (), s32[]{:S(2)}) async-start(), calls=%async_computation.48 | async-start | bytes 12976128 | tf_op jit(solution)/shard_map/reduce_scatter | solution.py:449
  521.4 21.5 %copy-start.20 = (bf16[1024,1024]{1,0:T(8,128)(2,1)S(1)}, bf16[1024,1024]{1,0:T(8,128)(2,1)}, u32[]{:S(2)}) copy-start(bf16[1024,1024]{1,0:T(8,128)(2,1)} %param.28) | copy-start | bytes 6291460
  576.3 715.3 %reduce-scatter.51.cloned.1.call-start = ((), (), s32[]{:S(2)}) async-start(), calls=%async_computation.49 | async-start | bytes 12976128 | tf_op jit(solution)/shard_map/reduce_scatter | solution.py:450
  579.5 11.1 copy-start.17
  639.3 655.0 %reduce-scatter.33.cloned.1.call-start = ((), (), s32[]{:S(2)}) async-start(), calls=%async_computation.40 | async-start | bytes 4718592 | tf_op jit(solution)/shard_map/reduce_scatter | solution.py:445
  1043.4 28.6 %slice-start = ((s8[16777216]{0:T(1024)(128)(4,1)}), s8[4194304]{0:T(1024)(128)(4,1)S(1)}, s32[]{:S(2)}) async-start(s8[16777216]{0:T(1024)(128)(4,1)} %bitcast.889), calls=%async_computation.59 | async-start | bytes 8388608 | tf_op jit(solution)/shard_map/while
  1043.4 28.6 %slice-start.1 = ((s8[16777216]{0:T(1024)(128)(4,1)}), s8[4194304]{0:T(1024)(128)(4,1)S(1)}, s32[]{:S(2)}) async-start(s8[16777216]{0:T(1024)(128)(4,1)} %bitcast.889), calls=%async_computation.60 | async-start | bytes 8388608 | tf_op jit(solution)/shard_map/while
  1043.5 28.6 %slice-start.2 = ((s8[16777216]{0:T(1024)(128)(4,1)}), s8[4194304]{0:T(1024)(128)(4,1)S(1)}, s32[]{:S(2)}) async-start(s8[16777216]{0:T(1024)(128)(4,1)} %bitcast.889), calls=%async_computation.61 | async-start | bytes 8388608 | tf_op jit(solution)/shard_map/while
  1055.5 16.6 slice-start.3
  1062.6 9.5 copy-start.12
  1106.7 28.6 %slice-start = ((s8[16777216]{0:T(1024)(128)(4,1)}), s8[4194304]{0:T(1024)(128)(4,1)S(1)}, s32[]{:S(2)}) async-start(s8[16777216]{0:T(1024)(128)(4,1)} %bitcast.889), calls=%async_computation.59 | async-start | bytes 8388608 | tf_op jit(solution)/shard_map/while
  1106.7 28.6 %slice-start.1 = ((s8[16777216]{0:T(1024)(128)(4,1)}), s8[4194304]{0:T(1024)(128)(4,1)S(1)}, s32[]{:S(2)}) async-start(s8[16777216]{0:T(1024)(128)(4,1)} %bitcast.889), calls=%async_computation.60 | async-start | bytes 8388608 | tf_op jit(solution)/shard_map/while
  1106.7 28.6 %slice-start.2 = ((s8[16777216]{0:T(1024)(128)(4,1)}), s8[4194304]{0:T(1024)(128)(4,1)S(1)}, s32[]{:S(2)}) async-start(s8[16777216]{0:T(1024)(128)(4,1)} %bitcast.889), calls=%async_computation.61 | async-start | bytes 8388608 | tf_op jit(solution)/shard_map/while
  1118.7 16.6 slice-start.3
  1125.8 9.5 copy-start.12
  1153.7 10.5 copy-start.7
  1153.7 10.5 copy-start.38
  1153.7 10.4 copy-start.41
  1170.1 177.0 %reduce-scatter.45.cloned.1.call-start = ((), (), s32[]{:S(2)}) async-start(), calls=%async_computation.46 | async-start | bytes 4718592 | tf_op jit(solution)/shard_map/reduce_scatter | solution.py:448
  1177.4 260.9 %reduce-scatter.29.cloned.1.call-start = ((), (), s32[]{:S(2)}) async-start(), calls=%async_computation.38 | async-start | bytes 4718592 | tf_op jit(solution)/shard_map/reduce_scatter | solution.py:444
  1217.1 312.9 %reduce-scatter.37.cloned.1.call-start = ((), (), s32[]{:S(2)}) async-start(), calls=%async_computation.42 | async-start | bytes 4718592 | tf_op jit(solution)/shard_map/reduce_scatter | solution.py:446
  1256.3 364.8 %reduce-scatter.41.cloned.1.call-start = ((), (), s32[]{:S(2)}) async-start(), calls=%async_computation.44 | async-start | bytes 4718592 | tf_op jit(solution)/shard_map/reduce_scatter | solution.py:447
  1274.8 542.5 %reduce-scatter.53.cloned.1.call-start = ((), (), s32[]{:S(2)}) async-start(), calls=%async_computation.50 | async-start | bytes 12976128 | tf_op jit(solution)/shard_map/reduce_scatter | solution.py:451
  1287.3 586.2 %reduce-scatter.57.cloned.1.call-start = ((), (), s32[]{:S(2)}) async-start(), calls=%async_computation.52 | async-start | bytes 73728 | tf_op jit(solution)/shard_map/reduce_scatter | solution.py:454
  1288.1 641.5 %reduce-scatter.59.cloned.1.call-start = ((), (), s32[]{:S(2)}) async-start(), calls=%async_computation.53 | async-start | bytes 73728 | tf_op jit(solution)/shard_map/reduce_scatter | solution.py:455
  1288.8 650.9 %reduce-scatter.61.cloned.1.call-start = ((), (), s32[]{:S(2)}) async-start(), calls=%async_computation.54 | async-start | bytes 1081344
  1291.5 240.3 %copy-start.54 = (u32[32]{0:T(128)S(1)}, u32[32]{0:T(128)}, u32[]{:S(2)}) copy-start(u32[32]{0:T(128)} %constant.178) | copy-start | bytes 388
  1291.5 660.3 %reduce-scatter.63.cloned.1.call-start = ((), (), s32[]{:S(2)}) async-start(), calls=%async_computation.55 | async-start | bytes 1081344
  1294.2 669.3 %reduce-scatter.35.cloned.1.call-start = ((), (), s32[]{:S(2)}) async-start(), calls=%async_computation.41 | async-start | bytes 393216 | tf_op jit(solution)/shard_map/reduce_scatter | solution.py:461
  1296.1 679.1 %reduce-scatter.47.cloned.1.call-start = ((), (), s32[]{:S(2)}) async-start(), calls=%async_computation.47 | async-start | bytes 393216 | tf_op jit(solution)/shard_map/reduce_scatter | solution.py:470
  1348.8 638.1 %reduce-scatter.31.cloned.1.call-start = ((), (), s32[]{:S(2)}) async-start(), calls=%async_computation.39 | async-start | bytes 393216 | tf_op jit(solution)/shard_map/reduce_scatter | solution.py:458
  1440.1 558.3 %reduce-scatter.39.cloned.1.call-start = ((), (), s32[]{:S(2)}) async-start(), calls=%async_computation.43 | async-start | bytes 393216 | tf_op jit(solution)/shard_map/reduce_scatter | solution.py:464
  1531.8 478.4 %reduce-scatter.43.cloned.1.call-start = ((), (), s32[]{:S(2)}) async-start(), calls=%async_computation.45 | async-start | bytes 393216 | tf_op jit(solution)/shard_map/reduce_scatter | solution.py:467
  1623.0 399.3 %reduce-scatter.55.cloned.1.call-start = ((), (), s32[]{:S(2)}) async-start(), calls=%async_computation.51 | async-start | bytes 1081344 | tf_op jit(solution)/shard_map/reduce_scatter | solution.py:479
  1819.7 294.7 %reduce-scatter.65.cloned.1.call-start = ((), (), s32[]{:S(2)}) async-start(), calls=%async_computation.56 | async-start | bytes 49152
  1875.0 240.2 %reduce-scatter.67.cloned.1.call-start = ((), (), s32[]{:S(2)}) async-start(), calls=%async_computation.57 | async-start | bytes 49152
  1931.0 192.2 %all-reduce.14.cloned.1.call-start = ((), (), s32[]{:S(2)}) async-start(), calls=%async_computation.58 | async-start | bytes 3473408 | tf_op jit(solution)/shard_map/psum | solution.py:496
  2022.3 52.9 %copy-start.46 = (f32[1024]{0:T(1024)S(1)}, f32[1024]{0:T(1024)}, u32[]{:S(2)}) copy-start(f32[1024]{0:T(1024)} %get-tuple-element.982) | copy-start | bytes 12292
  2022.3 77.1 %copy-start.43 = (f32[1024]{0:T(1024)S(1)}, f32[1024]{0:T(1024)}, u32[]{:S(2)}) copy-start(f32[1024]{0:T(1024)} %get-tuple-element.1221) | copy-start | bytes 12292
  2109.3 26.1 %copy-start.1 = (f32[16,4]{0,1:T(4,128)S(1)}, f32[16,4]{0,1:T(4,128)}, u32[]{:S(2)}) copy-start(f32[16,4]{0,1:T(4,128)} %param.43) | copy-start | bytes 772
  2123.3 10.7 copy-start.34
  2123.3 11.4 copy-start.33
  (34 other events, 163.5 us)
Sparse Core Ops, SparseCore 0:
  11.5 51.7 all-gather.14
  65.4 48.1 all-gather.16
  115.7 48.0 all-gather.12
  165.8 47.9 all-gather.18
  215.7 47.7 all-gather.20
  265.6 91.1 all-gather.22
  358.9 90.8 all-gather.24
  452.0 90.8 all-gather.26
  576.4 190.8 reduce-scatter.48
  770.8 191.7 reduce-scatter.50
  1170.2 85.1 reduce-scatter.32
  1259.4 87.6 reduce-scatter.44
  1350.7 87.6 reduce-scatter.28
  1442.3 87.6 reduce-scatter.36
  1533.4 87.6 reduce-scatter.40
  1625.0 192.2 reduce-scatter.52
  1820.6 52.8 reduce-scatter.56
  1876.8 52.7 reduce-scatter.58
  1932.5 7.1 reduce-scatter.60
  1942.4 9.3 reduce-scatter.62
  1954.7 8.8 reduce-scatter.34
  1966.3 8.8 reduce-scatter.46
  1978.1 8.8 reduce-scatter.30
  1989.6 8.8 reduce-scatter.38
  2001.3 8.8 reduce-scatter.42
  2012.9 9.3 reduce-scatter.54
  2024.3 8.5 reduce-scatter.64
  2035.2 8.6 reduce-scatter.66
  2047.4 58.1 all-reduce.13
where the time goes:
time: 2160 us; the launch traced here: 2140 us
  matrix products  757 us (35%)
  waiting for transfers between devices  685 us (32%)
  local copies, waits for them, and re-layouts  265 us (12%)
  blocking collectives  256 us (12%)
  other arithmetic  151 us (7%)
    reduce_scatter x1, waiting for transfers between devices, local(): lax.psum_scatter(g_ffn_down, 'row', scatter_dimension=0, tiled=True)  188 us
    dot_general x96, matrix products, advance(): span_slope = jnp.einsum('bcd,bce->bde', span_key, misfit, precision=HIGH)  143 us
    dot_general x96, matrix products, advance(): span_read = jnp.einsum('bcd,bde->bce', span_query, memory, precision=HIGH)  140 us
    dot_general x96, matrix products, advance(): jnp.einsum('bcd,bde->bce', span_key, memory, precision=HIGH) - span_value  140 us
    reduce_scatter x1, waiting for transfers between devices, local(): lax.psum_scatter(g_value, 'row', scatter_dimension=0, tiled=True)  89.8 us
    reduce_scatter x1, waiting for transfers between devices, local(): lax.psum_scatter(g_query, 'row', scatter_dimension=0, tiled=True)  89.5 us
    reduce_scatter x1, waiting for transfers between devices, local(): lax.psum_scatter(g_gate, 'row', scatter_dimension=0, tiled=True)  87.4 us
    dot_general x8, matrix products, dot_trans_right(): lax.dot_general(first_op, second_op, (((1,), (1,)), ((), ())), preferred_...  77.7 us
  transfers between devices with their start and end apart: 30, of which 16 were waited for; matrix products, arithmetic and copies ran while one was open for 52% of the time, Pallas kernels for 0%

commit v1 on v0

v1 whole, which is shorter than its diff:
```python
import functools
import jax
import jax.numpy as jnp
from jax import lax
from jax.experimental import pallas as pl
from jax.experimental.pallas import tpu as pltpu
from jax.sharding import PartitionSpec as P

HD = 128
P_SIZE = 16
SEG = 1024
CH = 64
SEQ = 2048
TILE = 256
TPS = SEG // TILE
EPS = 1e-06
NEG = -1e30
SCALE = HD ** (-0.5)
LOG2E = 1.4426950408889634
VMEM_MAX = 60 * 1024 * 1024
F32 = jnp.float32
BF = jnp.bfloat16
HIGH = lax.Precision.HIGHEST
MESH = pl.DeviceIdType.MESH


def nn(a, b):
    return lax.dot_general(a, b, (((1,), (0,)), ((), ())), preferred_element_type=F32)


def nt(a, b):
    return lax.dot_general(a, b, (((1,), (1,)), ((), ())), preferred_element_type=F32)


def tn(a, b):
    return lax.dot_general(a, b, (((0,), (0,)), ((), ())), preferred_element_type=F32)


def token_bias(segc, segr, part):
    width = (part + 1) * TILE
    same = segc == segr[:, :width]
    qpos = lax.broadcasted_iota(jnp.int32, (TILE, width), 0) + part * TILE
    kpos = lax.broadcasted_iota(jnp.int32, (TILE, width), 1)
    return jnp.where(same & (kpos <= qpos), 0.0, NEG).astype(F32)


def mix_forward_tile(heads, part, tile, q_ref, k_ref, v_ref, g_ref, pk_ref, pv_ref, segc_ref,
                     segr_ref, coef_ref, comb_ref, lse_ref, reads_ref, m0_ref, err_ref, mem, mom):
    width = (part + 1) * TILE
    base = part * TILE
    bias = token_bias(segc_ref[...], segr_ref[...], part)
    pcol = lax.broadcasted_iota(jnp.int32, (TILE, HD), 1)
    lane = lax.broadcasted_iota(jnp.int32, (TILE, HD), 1)
    lse_all = jnp.zeros((TILE, HD), F32)
    blocks = TILE // CH
    for head in range(heads):
        cols = slice(head * HD, (head + 1) * HD)
        query = q_ref[:, cols]
        state = mem[head]
        speed = mom[head]
        reads = []
        for step in range(blocks):
            rows = slice(step * CH, (step + 1) * CH)
            at = tile * blocks + step
            keep = coef_ref[0, at * heads + head]
            rate = coef_ref[1, at * heads + head]
            moment = coef_ref[2, at * heads + head]
            stay = coef_ref[3, at * heads + head]
            start = state * keep
            low_start = start.astype(BF)
            m0_ref[step, head] = low_start
            rest = (start - low_start.astype(F32)).astype(BF)
            key = k_ref[base + step * CH:base + (step + 1) * CH, cols]
            value = v_ref[base + step * CH:base + (step + 1) * CH, cols]
            both = jnp.concatenate([query[rows], key], axis=0)
            got = nn(both, low_start) + nn(both, rest)
            reads.append(got[:CH] * SCALE)
            err = (got[CH:] * SCALE - value.astype(F32)).astype(BF)
            err_ref[rows, cols] = err
            slope = tn(key, err)
            speed = (moment * keep) * speed - (rate * SCALE) * slope
            state = stay * start + speed
        mem[head] = state
        mom[head] = speed
        read = jnp.concatenate(reads, axis=0)
        reads_ref[:, cols] = read.astype(BF)
        tok = nt(query, k_ref[:width, cols]) * (SCALE * LOG2E) + bias
        per = nt(query, pk_ref[:, cols]) * (SCALE * LOG2E)
        per = jnp.where(pcol < P_SIZE, per, NEG)
        top = jnp.maximum(jnp.max(tok, axis=1, keepdims=True), jnp.max(per, axis=1, keepdims=True))
        tok_e = jnp.exp2(tok - top)
        per_e = jnp.exp2(per - top)
        total = jnp.sum(tok_e, axis=1, keepdims=True) + jnp.sum(per_e, axis=1, keepdims=True)
        att = nn(tok_e.astype(BF), v_ref[:width, cols]) + nn(per_e.astype(BF), pv_ref[:, cols])
        att = att / total
        lse_all = jnp.where(lane == head, top + jnp.log2(total), lse_all)
        gate = jax.nn.sigmoid(g_ref[:, cols].astype(F32))
        comb_ref[:, cols] = (att + gate * read).astype(BF)
    lse_ref[...] = lse_all


def mix_forward_kernel(heads, q_ref, k_ref, v_ref, g_ref, pk_ref, pv_ref, segc_ref, segr_ref,
                       coef_ref, comb_ref, lse_ref, reads_ref, m0_ref, err_ref, mem, mom):
    tile = pl.program_id(0)

    @pl.when(tile == 0)
    def clear():
        mem[...] = jnp.zeros_like(mem)
        mom[...] = jnp.zeros_like(mom)

    for part in range(TPS):
        @pl.when(lax.rem(tile, TPS) == part)
        def work():
            mix_forward_tile(heads, part, tile, q_ref, k_ref, v_ref, g_ref, pk_ref, pv_ref,
                             segc_ref, segr_ref, coef_ref, comb_ref, lse_ref, reads_ref, m0_ref,
                             err_ref, mem, mom)


def mix_forward(qkvg, pkey, pvalue, segc, segr, coef, heads):
    total = qkvg.shape[0]
    width = heads * HD
    tiles = total // TILE
    per = TILE // CH
    return pl.pallas_call(
        functools.partial(mix_forward_kernel, heads),
        grid=(tiles,),
        in_specs=[
            pl.BlockSpec((TILE, width), lambda t: (t, 0)),
            pl.BlockSpec((SEG, width), lambda t: (t // TPS, 1)),
            pl.BlockSpec((SEG, width), lambda t: (t // TPS, 2)),
            pl.BlockSpec((TILE, width), lambda t: (t, 3)),
            pl.BlockSpec((HD, width), lambda t: (0, 0)),
            pl.BlockSpec((HD, width), lambda t: (0, 0)),
            pl.BlockSpec((TILE, 1), lambda t: (t, 0)),
            pl.BlockSpec((1, SEG), lambda t: (0, t // TPS)),
            pl.BlockSpec(memory_space=pltpu.SMEM),
        ],
        out_specs=[
            pl.BlockSpec((TILE, width), lambda t: (t, 0)),
            pl.BlockSpec((TILE, HD), lambda t: (t, 0)),
            pl.BlockSpec((TILE, width), lambda t: (t, 0)),
            pl.BlockSpec((per, heads, HD, HD), lambda t: (t, 0, 0, 0)),
            pl.BlockSpec((TILE, width), lambda t: (t, 0)),
        ],
        out_shape=[
            jax.ShapeDtypeStruct((total, width), BF),
            jax.ShapeDtypeStruct((total, HD), F32),
            jax.ShapeDtypeStruct((total, width), BF),
            jax.ShapeDtypeStruct((total // CH, heads, HD, HD), BF),
            jax.ShapeDtypeStruct((total, width), BF),
        ],
        scratch_shapes=[pltpu.VMEM((heads, HD, HD), F32), pltpu.VMEM((heads, HD, HD), F32)],
        compiler_params=pltpu.CompilerParams(vmem_limit_bytes=VMEM_MAX),
        name="mix_forward",
    )(qkvg, qkvg, qkvg, qkvg, pkey, pvalue, segc, segr, coef)


def mix_backward_tile(heads, part, tile, q_ref, k_ref, v_ref, g_ref, dc_ref, pk_ref, pv_ref,
                      segc_ref, segr_ref, coef_ref, lse_ref, reads_ref, m0_ref, err_ref, dout_ref,
                      dmem, dmom, dk_acc, dv_acc, dpk_acc, dpv_acc):
    width = (part + 1) * TILE
    base = part * TILE
    wide = heads * HD
    bias = token_bias(segc_ref[...], segr_ref[...], part)
    pcol = lax.broadcasted_iota(jnp.int32, (TILE, HD), 1)
    blocks = TILE // CH
    lse_all = lse_ref[...]
    for head in range(heads):
        cols = slice(head * HD, (head + 1) * HD)
        query = q_ref[:, cols]
        up = dc_ref[:, cols]
        upf = up.astype(F32)
        gate = jax.nn.sigmoid(g_ref[:, cols].astype(F32))
        dread = (upf * gate).astype(BF)
        dgate = upf * reads_ref[:, cols].astype(F32) * gate * (1.0 - gate)
        dout_ref[:, 3 * wide + head * HD:3 * wide + (head + 1) * HD] = dgate.astype(BF)
        dstate = dmem[head]
        dspeed = dmom[head]
        dq_mem, dk_mem, dv_mem = [None] * blocks, [None] * blocks, [None] * blocks
        for step in reversed(range(blocks)):
            rows = slice(step * CH, (step + 1) * CH)
            at = tile * blocks + step
            keep = coef_ref[0, at * heads + head]
            rate = coef_ref[1, at * heads + head]
            moment = coef_ref[2, at * heads + head]
            stay = coef_ref[3, at * heads + head]
            key = k_ref[base + step * CH:base + (step + 1) * CH, cols]
            start = m0_ref[step, head]
            err = err_ref[rows, cols]
            dspeed = dspeed + dstate
            dslope = (dspeed * (-rate)).astype(BF)
            derr = nn(key, dslope) * SCALE
            derr_low = derr.astype(BF)
            top = jnp.concatenate([dread[rows], derr_low], axis=0)
            both = jnp.concatenate([query[rows], key], axis=0)
            dstart = stay * dstate + SCALE * tn(both, top)
            back = nt(top, start)
            dq_mem[step] = back[:CH]
            dk_mem[step] = back[CH:] + nt(err, dslope)
            dv_mem[step] = derr
            dspeed = (moment * keep) * dspeed
            dstate = keep * dstart
        dmem[head] = dstate
        dmom[head] = dspeed
        tok = nt(query, k_ref[:width, cols]) * (SCALE * LOG2E) + bias
        per = nt(query, pk_ref[:, cols]) * (SCALE * LOG2E)
        per = jnp.where(pcol < P_SIZE, per, NEG)
        lse = lse_all[:, head:head + 1]
        tok_p = jnp.exp2(tok - lse)
        per_p = jnp.exp2(per - lse)
        tok_dp = nt(up, v_ref[:width, cols])
        per_dp = nt(up, pv_ref[:, cols])
        inner = jnp.sum(tok_p * tok_dp, axis=1, keepdims=True) + jnp.sum(
            per_p * per_dp, axis=1, keepdims=True)
        tok_ds = (tok_p * (tok_dp - inner)).astype(BF)
        per_ds = (per_p * (per_dp - inner)).astype(BF)
        dquery = nn(tok_ds, k_ref[:width, cols]) + nn(per_ds, pk_ref[:, cols])
        dquery = (dquery + jnp.concatenate(dq_mem, axis=0)) * SCALE
        dout_ref[:, cols] = dquery.astype(BF)
        dkey = tn(tok_ds, query)
        dval = tn(tok_p.astype(BF), up)
        dpk_acc[:, cols] += tn(per_ds, query) * SCALE
        dpv_acc[:, cols] += tn(per_p.astype(BF), up)
        own = slice(base, base + TILE)
        if part == TPS - 1:
            dk_acc[:base, cols] = dkey[:base]
            dv_acc[:base, cols] = dval[:base]
            dk_own, dv_own = dkey[base:], dval[base:]
        else:
            if part:
                dk_acc[:base, cols] += dkey[:base]
                dv_acc[:base, cols] += dval[:base]
            dk_own = dk_acc[own, cols] + dkey[base:]
            dv_own = dv_acc[own, cols] + dval[base:]
        dout_ref[:, wide + head * HD:wide + (head + 1) * HD] = (
            (dk_own + jnp.concatenate(dk_mem, axis=0)) * SCALE).astype(BF)
        dout_ref[:, 2 * wide + head * HD:2 * wide + (head + 1) * HD] = (
            dv_own - jnp.concatenate(dv_mem, axis=0)).astype(BF)


def mix_backward_kernel(heads, tiles, q_ref, k_ref, v_ref, g_ref, dc_ref, pk_ref, pv_ref, segc_ref,
                        segr_ref, coef_ref, lse_ref, reads_ref, m0_ref, err_ref, dout_ref, dpk_ref,
                        dpv_ref, dmem, dmom, dk_acc, dv_acc):
    turn = pl.program_id(0)
    tile = tiles - 1 - turn

    @pl.when(turn == 0)
    def clear():
        dmem[...] = jnp.zeros_like(dmem)
        dmom[...] = jnp.zeros_like(dmom)
        dpk_ref[...] = jnp.zeros_like(dpk_ref)
        dpv_ref[...] = jnp.zeros_like(dpv_ref)

    for part in range(TPS):
        @pl.when(lax.rem(tile, TPS) == part)
        def work():
            mix_backward_tile(heads, part, tile, q_ref, k_ref, v_ref, g_ref, dc_ref, pk_ref, pv_ref,
                              segc_ref, segr_ref, coef_ref, lse_ref, reads_ref, m0_ref, err_ref,
                              dout_ref, dmem, dmom, dk_acc, dv_acc, dpk_ref, dpv_ref)


def mix_backward(qkvg, dcomb, pkey, pvalue, segc, segr, coef, lse, reads, m0, err, heads):
    total = qkvg.shape[0]
    width = heads * HD
    tiles = total // TILE
    per = TILE // CH
    last = tiles - 1
    return pl.pallas_call(
        functools.partial(mix_backward_kernel, heads, tiles),
        grid=(tiles,),
        in_specs=[
            pl.BlockSpec((TILE, width), lambda t: (last - t, 0)),
            pl.BlockSpec((SEG, width), lambda t: ((last - t) // TPS, 1)),
            pl.BlockSpec((SEG, width), lambda t: ((last - t) // TPS, 2)),
            pl.BlockSpec((TILE, width), lambda t: (last - t, 3)),
            pl.BlockSpec((TILE, width), lambda t: (last - t, 0)),
            pl.BlockSpec((HD, width), lambda t: (0, 0)),
            pl.BlockSpec((HD, width), lambda t: (0, 0)),
            pl.BlockSpec((TILE, 1), lambda t: (last - t, 0)),
            pl.BlockSpec((1, SEG), lambda t: (0, (last - t) // TPS)),
            pl.BlockSpec(memory_space=pltpu.SMEM),
            pl.BlockSpec((TILE, HD), lambda t: (last - t, 0)),
            pl.BlockSpec((TILE, width), lambda t: (last - t, 0)),
            pl.BlockSpec((per, heads, HD, HD), lambda t: (last - t, 0, 0, 0)),
            pl.BlockSpec((TILE, width), lambda t: (last - t, 0)),
        ],
        out_specs=[
            pl.BlockSpec((TILE, 4 * width), lambda t: (last - t, 0)),
            pl.BlockSpec((HD, width), lambda t: (0, 0)),
            pl.BlockSpec((HD, width), lambda t: (0, 0)),
        ],
        out_shape=[
            jax.ShapeDtypeStruct((total, 4 * width), BF),
            jax.ShapeDtypeStruct((HD, width), F32),
            jax.ShapeDtypeStruct((HD, width), F32),
        ],
        scratch_shapes=[
            pltpu.VMEM((heads, HD, HD), F32),
            pltpu.VMEM((heads, HD, HD), F32),
            pltpu.VMEM((SEG, width), F32),
            pltpu.VMEM((SEG, width), F32),
        ],
        compiler_params=pltpu.CompilerParams(vmem_limit_bytes=VMEM_MAX),
        name="mix_backward",
    )(qkvg, qkvg, qkvg, qkvg, dcomb, pkey, pvalue, segc, segr, coef, lse, reads, m0, err)


def ffn_kernel(tiles, comb_ref, x_ref, dy_ref, wo_ref, wg_ref, wu_ref, wd_ref, gain_ref, out_ref,
               dmid_ref, dcomb_ref, go_ref, gg_ref, gu_ref, gd_ref, dgain_ref, sums_ref, n2, n2t,
               mid, acc_out, acc_dn, hid_all, pair_all):
    turn = pl.program_id(0)
    rows_all, dim = x_ref.shape
    steps = rows_all // TILE
    ft = wg_ref.shape[1]
    gain = gain_ref[...]

    @pl.when(turn == 0)
    def first():
        sums_ref[...] = jnp.zeros_like(sums_ref)
        dgain_ref[...] = jnp.zeros_like(dgain_ref)
        for i in range(steps):
            rows = slice(i * TILE, (i + 1) * TILE)
            xf = x_ref[rows, :].astype(F32)
            branch = nn(comb_ref[rows, :], wo_ref[...])
            middle = xf + branch
            mid[rows, :] = middle
            acc_out[rows, :] = middle
            inv = lax.rsqrt(jnp.mean(middle * middle, axis=1, keepdims=True) + EPS)
            normed = (middle * inv * gain).astype(BF)
            n2[rows, :] = normed
            n2t[:, rows] = normed.T
            acc_dn[rows, :] = jnp.zeros((TILE, dim), F32)
            sums_ref[0:1, :] += jnp.sum(xf * xf, axis=0, keepdims=True)
            sums_ref[1:2, :] += jnp.sum(branch * branch, axis=0, keepdims=True)

    wd = wd_ref[...]
    both = jnp.concatenate([wg_ref[...], wu_ref[...]], axis=1)
    for i in range(steps):
        rows = slice(i * TILE, (i + 1) * TILE)
        gateup = nn(n2[rows, :], both)
        gate, up = gateup[:, :ft], gateup[:, ft:]
        dh = nt(dy_ref[rows, :], wd)
        sig = jax.nn.sigmoid(gate)
        silu = gate * sig
        hid = (silu * up).astype(BF)
        dg = (dh * up * (sig * (1.0 + gate * (1.0 - sig)))).astype(BF)
        du = (dh * silu).astype(BF)
        hid_all[rows, :] = hid
        pair = jnp.concatenate([dg, du], axis=1)
        pair_all[rows, :] = pair
        acc_out[rows, :] += nn(hid, wd)
        acc_dn[rows, :] += nt(pair, both)
    gd_ref[...] = tn(hid_all[...], dy_ref[...]).astype(BF)
    grads = nn(n2t[...], pair_all[...])
    gg_ref[...] = grads[:, :ft].astype(BF)
    gu_ref[...] = grads[:, ft:].astype(BF)

    @pl.when(turn == tiles - 1)
    def last():
        for i in range(steps):
            rows = slice(i * TILE, (i + 1) * TILE)
            final = acc_out[rows, :]
            out_ref[rows, :] = final.astype(BF)
            sums_ref[2:3, :] += jnp.sum(final * final, axis=0, keepdims=True)
            middle = mid[rows, :]
            inv = lax.rsqrt(jnp.mean(middle * middle, axis=1, keepdims=True) + EPS)
            dnorm = acc_dn[rows, :]
            weighted = dnorm * gain
            inner = jnp.mean(weighted * middle, axis=1, keepdims=True)
            dgain_ref[...] += jnp.sum(dnorm * middle * inv, axis=0, keepdims=True)
            dmid = dy_ref[rows, :].astype(F32) + weighted * inv - middle * (inv * inv * inv) * inner
            low = dmid.astype(BF)
            dmid_ref[rows, :] = low
            dcomb_ref[rows, :] = nt(low, wo_ref[...]).astype(BF)
        for i in range(dim // TILE):
            part = slice(i * TILE, (i + 1) * TILE)
            go_ref[part, :] = tn(comb_ref[:, part], dmid_ref[...]).astype(BF)


def whole(shape):
    return pl.BlockSpec(shape, lambda t: (0,) * len(shape), pipeline_mode=pl.Buffered(1))


def ffn_block(comb, x, dy, w_out, w_gate, w_up, w_down, gain):
    rows, dim = x.shape
    hidden = w_gate.shape[1]
    tiles = hidden // TILE
    full = (rows, dim)
    return pl.pallas_call(
        functools.partial(ffn_kernel, tiles),
        grid=(tiles,),
        in_specs=[
            whole(full),
            whole(full),
            whole(full),
            whole((dim, dim)),
            pl.BlockSpec((dim, TILE), lambda t: (0, t)),
            pl.BlockSpec((dim, TILE), lambda t: (0, t)),
            pl.BlockSpec((TILE, dim), lambda t: (t, 0)),
            whole((1, dim)),
        ],
        out_specs=[
            whole(full),
            whole(full),
            whole(full),
            whole((dim, dim)),
            pl.BlockSpec((dim, TILE), lambda t: (0, t)),
            pl.BlockSpec((dim, TILE), lambda t: (0, t)),
            pl.BlockSpec((TILE, dim), lambda t: (t, 0)),
            whole((1, dim)),
            whole((8, dim)),
        ],
        out_shape=[
            jax.ShapeDtypeStruct(full, BF),
            jax.ShapeDtypeStruct(full, BF),
            jax.ShapeDtypeStruct(full, BF),
            jax.ShapeDtypeStruct((dim, dim), BF),
            jax.ShapeDtypeStruct((dim, hidden), BF),
            jax.ShapeDtypeStruct((dim, hidden), BF),
            jax.ShapeDtypeStruct((hidden, dim), BF),
            jax.ShapeDtypeStruct((1, dim), F32),
            jax.ShapeDtypeStruct((8, dim), F32),
        ],
        scratch_shapes=[
            pltpu.VMEM(full, BF),
            pltpu.VMEM((dim, rows), BF),
            pltpu.VMEM(full, F32),
            pltpu.VMEM(full, F32),
            pltpu.VMEM(full, F32),
            pltpu.VMEM((rows, TILE), BF),
            pltpu.VMEM((rows, 2 * TILE), BF),
        ],
        compiler_params=pltpu.CompilerParams(vmem_limit_bytes=VMEM_MAX),
        name="ffn_block",
    )(comb, x, dy, w_out, w_gate, w_up, w_down, gain)


def ring_place(row, n):
    return jnp.where(lax.rem(row, 2) == 0, row // 2, n - 1 - row // 2)


def ring_row(place, n):
    return jnp.where(place < n // 2, 2 * place, 2 * (n - place) - 1)


def split_cols(width, flip):
    tiles = width // HD
    first = (tiles + (0 if flip else 1)) // 2 * HD
    return ((0, first), (first, width - first))


def mod(value, n):
    return lax.rem(value + n, n)


def neighbours(n):
    me = ring_place(lax.axis_index("row"), n)
    return me, ring_row(mod(me + 1, n), n), ring_row(mod(me - 1, n), n)


def greet(n, right, left, use_col, use_dp):
    barrier = pltpu.get_barrier_semaphore()
    count = 2
    for target in (right, left):
        pl.semaphore_signal(barrier, inc=1, device_id={"row": target}, device_id_type=MESH)
    if use_col:
        other = 1 - lax.axis_index("col")
        pl.semaphore_signal(barrier, inc=1, device_id={"col": other}, device_id_type=MESH)
        count += 1
    if use_dp:
        twin = 1 - lax.axis_index("dp")
        pl.semaphore_signal(barrier, inc=1, device_id={"dp": twin}, device_id_type=MESH)
        count += 1
    pl.semaphore_wait(barrier, count)


class Gather:
    def __init__(self, n, items, sems):
        self.n = n
        self.items = items
        self.send, self.recv, self.local, self.csend, self.crecv = sems
        self.me, self.right, self.left = neighbours(n)
        self.row = lax.axis_index("row")
        self.other = 1 - lax.axis_index("col")

    def hop(self, m, d, s):
        block, whole_ref, base, share = self.items[m]
        place = mod(self.me - s, self.n) if d == 0 else mod(self.me + s, self.n)
        owner = ring_row(place, self.n)
        start, size = split_cols(block.shape[1], m % 2)[d]
        spot = whole_ref.at[owner, :, pl.ds(base + start, size)]
        return owner, start, size, spot

    def ring(self, m, d, s, first=False):
        block = self.items[m][0]
        owner, start, size, spot = self.hop(m, d, s)
        source = block.at[:, pl.ds(start, size)] if first else spot
        return pltpu.make_async_remote_copy(
            src_ref=source, dst_ref=spot, send_sem=self.send.at[m, d, s], recv_sem=self.recv.at[m, d, s],
            device_id={"row": self.right if d == 0 else self.left}, device_id_type=MESH)

    def across(self, m, source, spot):
        return pltpu.make_async_remote_copy(
            src_ref=source, dst_ref=spot, send_sem=self.csend.at[m], recv_sem=self.crecv.at[m],
            device_id={"col": self.other}, device_id_type=MESH)

    def keep(self, m):
        block, whole_ref, base, share = self.items[m]
        return pltpu.make_async_copy(
            block, whole_ref.at[self.row, :, pl.ds(base, block.shape[1])], self.local.at[m])

    def begin(self, ms):
        for m in ms:
            for d in (0, 1):
                self.ring(m, d, 0, first=True).start()
        for m in ms:
            block, whole_ref, base, share = self.items[m]
            self.keep(m).start()
            if share:
                self.across(m, block, whole_ref.at[self.row, :, pl.ds(base, block.shape[1])]).start()

    def advance(self, m, s):
        for d in (0, 1):
            self.ring(m, d, s).wait_recv()

            @pl.when(s < self.n - 2)
            def on():
                self.ring(m, d, s + 1).start()

            if self.items[m][3]:
                spot = self.hop(m, d, s + 1)[3]
                self.across(m, spot, spot).start()

    def finish(self, ms):
        for m in ms:
            block, whole_ref, base, share = self.items[m]
            self.keep(m).wait()
            if share:
                spot = whole_ref.at[:, :, pl.ds(base, block.shape[1])]
                theirs = whole_ref.at[:, :, pl.ds(self.other * block.shape[1], block.shape[1])]
                self.across(m, spot, theirs).wait_recv()
                self.across(m, spot, theirs).wait_send()

            def sent(s, carry):
                for d in (0, 1):
                    self.ring(m, d, s).wait_send()
                return carry

            lax.fori_loop(0, self.n - 1, sent, 0)


def gather_sems(n, count):
    return [
        pltpu.SemaphoreType.DMA((count, 2, n - 1)),
        pltpu.SemaphoreType.DMA((count, 2, n - 1)),
        pltpu.SemaphoreType.DMA((count,)),
        pltpu.SemaphoreType.DMA((count,)),
        pltpu.SemaphoreType.DMA((count,)),
    ]


def gather_kernel(n, first, *refs):
    blocks = refs[:8]
    x_ref = refs[8]
    wide, w_out, w_gate, w_up, w_down, pair = refs[9:15]
    sems = refs[15:20]
    xsems = refs[20]
    core = lax.axis_index("col")
    items = [(blocks[m], wide, m * blocks[m].shape[1], False) for m in range(4)]
    items += [(blocks[m], ref, core * blocks[m].shape[1], True)
              for m, ref in zip(range(4, 8), (w_out, w_gate, w_up, w_down))]
    g = Gather(n, items, sems)
    greet(n, g.right, g.left, True, False)
    g.begin(range(4))
    mine = pltpu.make_async_copy(x_ref, pair.at[core], xsems.at[0])
    mine.start()
    theirs = pltpu.make_async_remote_copy(
        src_ref=x_ref, dst_ref=pair.at[core], send_sem=xsems.at[1], recv_sem=xsems.at[2],
        device_id={"col": 1 - core}, device_id_type=MESH)
    theirs.start()
    g.begin(range(4, 8))

    def step(s, carry):
        for m in range(8):
            g.advance(m, s)
        return carry

    lax.fori_loop(0, n - 1, step, 0)
    g.finish(range(8))
    mine.wait()
    theirs.wait()


def gather_all(n, blocks, x):
    rows = [block.shape[0] for block in blocks]
    width = blocks[0].shape[1]
    any_spec = pl.BlockSpec(memory_space=pl.ANY)
    shapes = [(n, rows[0], 4 * width)] + [(n, rows[m], 2 * blocks[m].shape[1]) for m in range(4, 8)]
    shapes.append((2,) + x.shape)
    return pl.pallas_call(
        functools.partial(gather_kernel, n, 4),
        in_specs=[any_spec] * 9,
        out_specs=[any_spec] * 6,
        out_shape=[jax.ShapeDtypeStruct(shape, BF) for shape in shapes],
        scratch_shapes=gather_sems(n, 8) + [pltpu.SemaphoreType.DMA((3,))],
        compiler_params=pltpu.CompilerParams(collective_id=1, has_side_effects=True),
        name="gather_all",
    )(*blocks, x)


class Scatter:
    def __init__(self, n, items, sems):
        self.n = n
        self.items = items
        self.send, self.recv, self.local, self.csend, self.crecv, self.dsend, self.drecv = sems
        self.me, self.right, self.left = neighbours(n)
        self.row = lax.axis_index("row")
        self.core = lax.axis_index("col")
        self.twin = 1 - lax.axis_index("dp")

    def load(self, m):
        whole_ref, base, width, share, own = self.items[m][:5]
        return pltpu.make_async_copy(whole_ref.at[:, :, pl.ds(base, width)], own, self.local.at[m])

    def across(self, m):
        whole_ref, base, width, share, own, sib = self.items[m][:6]
        return pltpu.make_async_remote_copy(
            src_ref=whole_ref.at[:, :, pl.ds((1 - self.core) * width, width)], dst_ref=sib,
            send_sem=self.csend.at[m], recv_sem=self.crecv.at[m],
            device_id={"col": 1 - self.core}, device_id_type=MESH)

    def begin(self, ms):
        for m in ms:
            if self.items[m][3]:
                self.across(m).start()
            self.load(m).start()

    def ready(self, m):
        self.load(m).wait()
        if self.items[m][3]:
            self.across(m).wait_recv()

    def part(self, m, d, s):
        place = mod(self.me - 1 - s, self.n) if d == 0 else mod(self.me + 1 + s, self.n)
        start, size = split_cols(self.items[m][2], m % 2)[d]
        return ring_row(mod(place, self.n), self.n), slice(start, start + size)

    def ring(self, m, d, s):
        own, ring = self.items[m][4], self.items[m][6]
        owner, cols = self.part(m, d, s)
        return pltpu.make_async_remote_copy(
            src_ref=own.at[owner, :, cols], dst_ref=ring.at[s, :, cols],
            send_sem=self.send.at[m, d, s], recv_sem=self.recv.at[m, d, s],
            device_id={"row": self.right if d == 0 else self.left}, device_id_type=MESH)

    def total(self, m, d, s, arrived):
        whole_ref, base, width, share, own, sib, ring = self.items[m][:7]
        owner, cols = self.part(m, d, s)
        value = own[owner, :, cols].astype(F32)
        if share:
            value = value + sib[owner, :, cols].astype(F32)
        if arrived:
            value = value + ring[s - 1, :, cols].astype(F32)
        return owner, cols, value

    def start(self, m):
        for d in (0, 1):
            owner, cols, value = self.total(m, d, 0, False)
            if self.items[m][3]:
                self.items[m][4][owner, :, cols] = value.astype(BF)
            self.ring(m, d, 0).start()

    def advance(self, m, s):
        for d in (0, 1):
            self.ring(m, d, s - 1).wait_recv()
            owner, cols, value = self.total(m, d, s, True)
            self.items[m][4][owner, :, cols] = value.astype(BF)
            self.ring(m, d, s).start()

    def swap(self, m):
        low, twin = self.items[m][7:9]
        return pltpu.make_async_remote_copy(
            src_ref=low, dst_ref=twin, send_sem=self.dsend.at[m], recv_sem=self.drecv.at[m],
            device_id={"dp": self.twin}, device_id_type=MESH)

    def settle(self, m):
        for d in (0, 1):
            self.ring(m, d, self.n - 2).wait_recv()
            owner, cols, value = self.total(m, d, self.n - 1, True)
            self.items[m][7][:, cols] = value.astype(BF)
        self.swap(m).start()

    def finish(self, m):
        low, twin, out = self.items[m][7:10]
        self.swap(m).wait_recv()
        out[...] = low[...].astype(F32) + twin[...].astype(F32)
        self.swap(m).wait_send()
        if self.items[m][3]:
            self.across(m).wait_send()

        def sent(s, carry):
            for d in (0, 1):
                self.ring(m, d, s).wait_send()
            return carry

        lax.fori_loop(0, self.n - 1, sent, 0)


def scatter_sems(n, count):
    return [
        pltpu.SemaphoreType.DMA((count, 2, n - 1)),
        pltpu.SemaphoreType.DMA((count, 2, n - 1)),
    ] + [pltpu.SemaphoreType.DMA((count,))] * 5


def scatter_plan(arrays):
    scratch = []
    for array, width, share in arrays:
        n, rows, full = array.shape
        scratch.append(pltpu.VMEM((n, rows, width), BF))
        scratch.append(pltpu.VMEM((n, rows, width) if share else (1, 16, HD), BF))
        scratch.append(pltpu.VMEM((n - 1, rows, width), BF))
        scratch.append(pltpu.VMEM((rows, width), BF))
        scratch.append(pltpu.VMEM((rows, width), BF))
    return scratch


def scatter_kernel(n, count, *refs):
    wide, go, gg, gu, gd = refs[:5]
    outs = refs[5:5 + count]
    scratch = refs[5 + count:5 + 6 * count]
    sems = refs[5 + 6 * count:]
    core = lax.axis_index("col")
    items = []
    for m in range(count):
        ref = wide if m < 4 else (go, gg, gu, gd)[m - 4]
        width = outs[m].shape[1]
        base = m * width if m < 4 else core * width
        items.append((ref, base, width, m >= 4) + tuple(scratch[5 * m:5 * m + 5]) + (outs[m],))
    g = Scatter(n, items, sems)
    greet(n, g.right, g.left, True, True)
    order = (5, 6, 7, 4, 0, 1, 2, 3)
    g.begin(order)
    for m in order:
        g.ready(m)
        g.start(m)

    def step(s, carry):
        for m in order:
            g.advance(m, s)
        return carry

    lax.fori_loop(1, n - 1, step, 0)
    for m in order:
        g.settle(m)
    for m in order:
        g.finish(m)


def scatter_all(n, wide, go, gg, gu, gd):
    width = wide.shape[2] // 4
    arrays = [(wide, width, False)] * 4 + [(a, a.shape[2] // 2, True) for a in (go, gg, gu, gd)]
    count = len(arrays)
    any_spec = pl.BlockSpec(memory_space=pl.ANY)
    return pl.pallas_call(
        functools.partial(scatter_kernel, n, count),
        in_specs=[any_spec] * 5,
        out_specs=[pl.BlockSpec(memory_space=pltpu.VMEM)] * count,
        out_shape=[jax.ShapeDtypeStruct((a.shape[1], w), F32) for a, w, share in arrays],
        scratch_shapes=scatter_plan(arrays) + scatter_sems(n, count),
        compiler_params=pltpu.CompilerParams(
            collective_id=2, has_side_effects=True, vmem_limit_bytes=VMEM_MAX),
        name="scatter_all",
    )(wide, go, gg, gu, gd)


def local(
    tokens_in,
    grad_out,
    gain_attn,
    gain_ffn,
    w_query,
    w_key,
    w_value,
    w_gate,
    w_out,
    w_ffn_gate,
    w_ffn_up,
    w_ffn_down,
    persist_key,
    persist_value,
    mem_rate,
    mem_momentum,
    mem_forget,
    segment_ids,
    decay_index,
):
    n = lax.axis_size("row")
    core = lax.axis_index("col")
    local_tok, dim = tokens_in.shape
    heads = mem_rate.shape[1]
    width = heads * HD
    piece = gain_attn.shape[0]
    small = jnp.concatenate(
        [persist_key, persist_value, gain_attn[None, :], gain_ffn[None, :]], axis=0)
    small_all = lax.all_gather(small, ("row", "col"), axis=1, tiled=True)
    gain_a = small_all[2 * P_SIZE][None, :].astype(F32)
    gain_f = small_all[2 * P_SIZE + 1][None, :].astype(F32)
    own_small = lax.dynamic_slice_in_dim(small_all, core * width, width, 1)
    pad = ((0, HD - P_SIZE), (0, 0))
    pkey = jnp.pad(own_small[:P_SIZE], pad)
    pvalue = jnp.pad(own_small[P_SIZE:2 * P_SIZE], pad)

    blocks = (w_query, w_key, w_value, w_gate, w_out, w_ffn_gate, w_ffn_up, w_ffn_down)
    wide, full_out, full_gate, full_up, full_down, pair = gather_all(n, blocks, tokens_in)
    wide = wide.reshape(dim, 4 * width)
    full_out, full_gate, full_up = [a.reshape(dim, -1) for a in (full_out, full_gate, full_up)]
    full_down = full_down.reshape(-1, dim)

    inputs = pair.reshape(2 * local_tok, dim).astype(F32)
    inverse_a = lax.rsqrt(jnp.mean(inputs * inputs, axis=-1, keepdims=True) + EPS)
    normed = (inputs * inverse_a * gain_a).astype(BF)
    qkvg = nn(normed, wide).astype(BF)

    total = qkvg.shape[0]
    spans = total // CH
    span_ids = segment_ids.reshape(total // SEQ, SEQ // CH, CH)
    same = (span_ids[:, 1:, 0] == span_ids[:, :-1, CH - 1]).astype(F32)
    keep = jnp.concatenate([jnp.zeros((total // SEQ, 1), F32), same], axis=1).reshape(spans, 1)
    choose = (decay_index[:, None] == jnp.arange(mem_rate.shape[0])[None, :]).astype(F32)
    tables = jnp.concatenate([mem_rate, mem_momentum, 1.0 - mem_forget], axis=1)
    picked = jnp.dot(choose, tables, precision=HIGH)
    coef = jnp.stack(
        [jnp.broadcast_to(keep, (spans, heads))] + [picked[:, i * heads:(i + 1) * heads] for i in range(3)]
    ).reshape(4, spans * heads)
    segc, segr = segment_ids[:, None], segment_ids[None, :]

    comb, lse, reads, m0, err = mix_forward(qkvg, pkey, pvalue, segc, segr, coef, heads)
    comb_tok = lax.all_to_all(comb, "col", split_axis=0, concat_axis=1, tiled=True)
    result, dmid, dcomb_tok, go, gg, gu, gd, dgain_f, sums = ffn_block(
        comb_tok, tokens_in, grad_out, full_out, full_gate, full_up, full_down, gain_f)
    dcomb = lax.all_to_all(dcomb_tok, "col", split_axis=1, concat_axis=0, tiled=True)
    dqkvg, dpk, dpv = mix_backward(
        qkvg, dcomb, pkey, pvalue, segc, segr, coef, lse, reads, m0, err, heads)

    g_wide = tn(normed, dqkvg).astype(BF)
    back = nt(dqkvg, wide).astype(BF)
    mine = lax.dynamic_slice_in_dim(back, core * local_tok, local_tok, 0)
    theirs = lax.dynamic_slice_in_dim(back, (1 - core) * local_tok, local_tok, 0)
    theirs = lax.ppermute(theirs, "col", [(0, 1), (1, 0)])
    dnorm = mine.astype(F32) + theirs.astype(F32)
    xf = tokens_in.astype(F32)
    inv = lax.rsqrt(jnp.mean(xf * xf, axis=-1, keepdims=True) + EPS)
    weighted = dnorm * gain_a
    inner = jnp.mean(weighted * xf, axis=-1, keepdims=True)
    grad_in = (dmid.astype(F32) + weighted * inv - xf * (inv * inv * inv) * inner).astype(BF)
    dgain_a = jnp.sum(dnorm * xf * inv, axis=0)

    rows = dim // n
    hidden_rows = full_down.shape[0] // n
    grads = scatter_all(
        n,
        g_wide.reshape(n, rows, 4 * width),
        go.reshape(n, rows, dim),
        gg.reshape(n, rows, -1),
        gu.reshape(n, rows, -1),
        gd.reshape(n, hidden_rows, dim),
    )

    place = jnp.zeros((2 * P_SIZE, dim), F32)
    place = lax.dynamic_update_slice_in_dim(
        place, jnp.concatenate([dpk[:P_SIZE], dpv[:P_SIZE]], axis=0), core * width, 1)
    packed = jnp.concatenate([place, dgain_a[None, :], dgain_f, sums[:3]], axis=0)
    summed = lax.psum(packed, ("dp", "row", "col"))
    entry_count = local_tok * dim * lax.axis_size("dp") * n * lax.axis_size("col")
    rms_stats = jnp.sqrt(jnp.sum(summed[2 * P_SIZE + 2:], axis=1) / entry_count)
    slot = lax.axis_index("row") * 2 + core
    part = lax.dynamic_slice_in_dim(summed, slot * piece, piece, 1)
    return (
        result,
        grad_in,
        grads[0],
        grads[1],
        grads[2],
        grads[3],
        grads[4],
        grads[5],
        grads[6],
        grads[7],
        part[2 * P_SIZE],
        part[2 * P_SIZE + 1],
        part[:P_SIZE],
        part[P_SIZE:2 * P_SIZE],
        rms_stats,
    )


def solution(mesh):
    tokens = P(("dp", "row", "col"), None)
    vector = P(("row", "col"))
    weight = P("row", "col")
    persist = P(None, ("row", "col"))
    table = P(None, "col")
    ids = P(("dp", "row"))
    return jax.shard_map(
        local,
        mesh=mesh,
        in_specs=(tokens, tokens, vector, vector) + (weight,) * 8 + (persist,) * 2 + (table,) * 3 + (ids,) * 2,
        out_specs=(tokens, tokens) + (weight,) * 8 + (vector,) * 2 + (persist,) * 2 + (P(),),
        check_vma=False,
    )
```

time: 2160 us -> 756 us (0.35)
  matrix products: 757 us -> 36 us
  waiting for transfers between devices: 685 us -> 114 us
  Pallas kernels: 0 us -> 502 us
  local copies, waits for them, and re-layouts: 265 us -> 25.8 us
  blocking collectives: 256 us -> 34 us
  other arithmetic: 151 us -> 21.7 us
    dot_general x340 -> x4, matrix products: 756 us -> 36 us  [the longest x1 13.9 us: nt(): lax.dot_general(a, b, (((1,), (1,)), ((), ())), preferred_element_type=F32)]
    reduce_scatter x16 -> x0, waiting for transfers between devices: 663 us -> none  [the longest x1 188 us: local(): lax.psum_scatter(g_ffn_down, 'row', scatter_dimension=0, tiled=True)]
    pallas_call x0 -> x5, Pallas kernels: none -> 502 us  [the longest x1 169 us: scatter_all(): pl.pallas_call(functools.partial(scatter_kernel, n, count), in_specs=[any...]
    psum x1, waiting for transfers between devices: 0.01 us -> 114 us  [local(): summed = lax.psum(packed, ('dp', 'row', 'col'))]
    all_gather x14 -> x1, blocking collectives: 122 us -> 21 us  [local(): small_all = lax.all_gather(small, ('row', 'col'), axis=1, tiled=True)]
    mul x41 -> x0, local copies, waits for them, and re-layouts: 73.9 us -> none  [the longest x2 13.2 us: local(): from_scan(grad_q_mem) * score_scale]
    convert_element_type x35 -> x4, other arithmetic: 84.1 us -> 11.2 us  [the longest x2 5.88 us: local(): normed = (inputs * inverse_a * gain_a).astype(BF)]
    reshape x10 -> x1, local copies, waits for them, and re-layouts: 48.9 us -> 0.07 us  [local(): span_ids = segment_ids.reshape(total // SEQ, SEQ // CH, CH)]
  transfers between devices with their start and end apart: 30 -> 2, of which waited for: 16 -> 1; matrix products, arithmetic and copies ran while one was open for 52% -> 3% of each run, Pallas kernels for 0% -> 23%
where the time goes in v1:
time: 756 us; the launch traced here: 749 us
  Pallas kernels  502 us (66%)
  waiting for transfers between devices  114 us (15%)
  matrix products  36 us (5%)
  blocking collectives  34 us (4%)
  local copies, waits for them, and re-layouts  25.8 us (3%)
  other arithmetic  21.7 us (3%)
  between operations  14.8 us (2%)
    pallas_call x1, Pallas kernels, scatter_all(): pl.pallas_call(functools.partial(scatter_kernel, n, count), in_specs=[any...  169 us
    pallas_call x1, Pallas kernels, gather_all(): pl.pallas_call(functools.partial(gather_kernel, n, 4), in_specs=[any_spec...  139 us
    psum x1, waiting for transfers between devices, local(): summed = lax.psum(packed, ('dp', 'row', 'col'))  114 us
    pallas_call x1, Pallas kernels, ffn_block(): pl.pallas_call(functools.partial(ffn_kernel, tiles), grid=(tiles,), in_sp...  77.7 us
    pallas_call x1, Pallas kernels, mix_backward(): pl.pallas_call(functools.partial(mix_backward_kernel, heads, tiles), grid...  61.8 us
    pallas_call x1, Pallas kernels, mix_forward(): pl.pallas_call(functools.partial(mix_forward_kernel, heads), grid=(tiles,...  54.2 us
    all_gather x1, blocking collectives, local(): small_all = lax.all_gather(small, ('row', 'col'), axis=1, tiled=True)  21 us
  transfers between devices with their start and end apart: 2, of which 1 were waited for; matrix products, arithmetic and copies ran while one was open for 3% of the time, Pallas kernels for 23%

profile of v1, /device:TPU:0, one launch (start us, length us, event | category | flops | bytes accessed | tf_op | source)
XLA Modules:
  0.0 749.0 jit_solution(3717304097411496039)
XLA Ops:
  7.2 0.0 copy-start.13
  7.2 0.0 copy-start.12
  7.2 0.0 all-reduce.4.cloned.1.call-start
  7.3 0.0 copy-start.6
  7.3 139.5 %gather_all.1 = (bf16[8,128,2048]{2,1,0:T(8,128)(2,1)}, bf16[8,128,1024]{2,1,0:T(8,128)(2,1)}, bf16[8,128,2816]{2,1,0:T(8,128)(2,1)}, bf16[8,128,2816]{2,1,0:T(8...) custom-call(bf16[128,512]{1,0:T(8,128)(2,1)} %refs_0_.1, bf16[128,512]{1,0:T(8,128)(2,1)} %refs_1_.1, ...), custom_call_target="tpu_custom_call" | custom-call | tf_op jit(solution)/shard_map/gather_all/pallas_call | solution.py:600
  146.8 3.1 multiply_reduce_fusion
  150.0 21.0 %all-gather = bf16[16,64,34]{1,2,0:T(8,128)(2,1)S(1)} all-gather(bf16[1,64,34]{1,2,0:T(8,128)(2,1)S(1)} %maximum_bitcast_fusion), channel_id=1, replica_groups=mesh['dp'=2,'row'=8,'col'=2] {'row','col'}, dimensions={0}, use_global_device_ids=true | all-gather | bytes 73984 | tf_op jit(solution)/shard_map/all_gather | solution.py:806
  171.1 0.1 reshape.180
  171.2 0.6 slice_convert_fusion
  171.8 0.7 pad.7.pk_ref
  172.5 0.7 pad.8.pv_ref
  173.2 0.2 fusion.10
  173.4 0.1 copy.57
  173.5 0.1 stack.12
  173.6 0.1 copy.58
  173.7 0.1 stack.13
  173.8 0.1 copy.59
  173.9 0.1 stack.14
  174.0 0.1 reshape.166
  174.1 0.2 fusion.11
  174.3 0.1 fusion.18
  174.3 0.1 stack_broadcast_in_dim.13
  174.4 0.1 stack_broadcast_in_dim.14
  174.5 1.4 copy.60.segc_ref
  175.9 2.9 multiply_convert_fusion
  178.9 0.5 copy-done.15
  179.4 10.9 %convolution_convert_fusion.q_ref.k_ref.v_ref.g_ref = bf16[2048,2048]{1,0:T(8,128)(2,1)} fusion(bf16[2048,1024]{1,0:T(8,128)(2,1)S(1)} %bitcast.71, bf16[1024,2048]{1,0:T(8,128)(2,1)S(1)} %bitcast.91), kind=kOutput, calls=%fused_computation.5 | convolution fusion | flops 8594128896 | bytes 16777216 | tf_op jit(solution)/shard_map/dot_general | solution.py:28
  190.3 0.6 pad_maximum_fusion.1.coef_ref
  190.9 54.2 %mix_forward.1 = (bf16[2048,512]{1,0:T(8,128)(2,1)}, f32[2048,128]{1,0:T(8,128)}, bf16[2048,512]{1,0:T(8,128)(2,1)}, bf16[32,4,128,128]{3,2,1,0:T(8,128)(2,1)}, bf16[2048,512]{1,0:T(8,128)(2,1)}) custom-call(bf16[2048,2048]{1,0:T(8,128)(2,1)} %convolution_convert_fusion.q_ref.k_ref.v_ref.g_ref, ...), custom_call_target="tpu_custom_call" | custom-call | tf_op jit(solution)/shard_map/mix_forward/pallas_call | solution.py:124
  245.1 6.6 all_to_all.38
  251.7 1.6 copy.65
  253.4 77.7 %ffn_block.1 = (bf16[1024,1024]{1,0:T(8,128)(2,1)}, bf16[1024,1024]{1,0:T(8,128)(2,1)}, bf16[1024,1024]{1,0:T(8,128)(2,1)}, bf16[1024,1024]{1,0:T(8,128)(2,1)}, ...) custom-call(bf16[1024,1024]{1,0:T(8,128)(2,1)} %bitcast.64, ...), custom_call_target="tpu_custom_call" | custom-call | tf_op jit(solution)/shard_map/ffn_block/pallas_call | solution.py:389
  331.1 1.7 copy.69
  332.9 6.3 all_to_all.39
  339.1 61.8 %mix_backward.1 = (bf16[2048,2048]{1,0:T(8,128)(2,1)}, f32[128,512]{1,0:T(8,128)}, f32[128,512]{1,0:T(8,128)}) custom-call(bf16[2048,2048]{1,0:T(8,128)(2,1)} %convolution_convert_fusion.q_ref.k_ref.v_ref.g_ref, bf16[2048,2048]{1,0:T(8,128)(2,1)} %convolution_convert_fusion.q_ref.k_ref.v_ref.g_ref, ...), custom_call_target="tpu_custom_call" | custom-call | tf_op jit(solution)/shard_map/mix_backward/pallas_call | solution.py:268
  401.0 13.9 %convolution_convert_fusion.2 = bf16[2048,1024]{1,0:T(8,128)(2,1)} fusion(bf16[2048,2048]{1,0:T(8,128)(2,1)} %get-tuple-element.60, bf16[1024,2048]{1,0:T(8,128)(2,1)} %bitcast.90), kind=kOutput, calls=%fused_computation.20 | convolution fusion | flops 8592031744 | bytes 16777216 | tf_op jit(solution)/shard_map/dot_general | solution.py:32
  414.9 3.1 constant_dynamic-slice_fusion.1
  418.0 0.1 collective-permute-start
  418.1 0.8 slice.60
  418.9 0.8 slice.61
  419.6 2.9 fusion.1
  422.6 1.7 copy-done.14
  424.3 11.0 %convolution_convert_fusion.1 = bf16[1024,2048]{1,0:T(8,128)(2,1)} fusion(bf16[2048,1024]{1,0:T(8,128)(2,1)S(1)} %fusion.1, bf16[2048,2048]{1,0:T(8,128)(2,1)S(1)} %copy-done.14), kind=kOutput, calls=%fused_computation.19 | convolution fusion | flops 8592031744 | bytes 16777216 | tf_op jit(solution)/shard_map/dot_general | solution.py:36
  435.3 168.8 %scatter_all.1 = (f32[128,512]{1,0:T(8,128)}, f32[128,512]{1,0:T(8,128)}, f32[128,512]{1,0:T(8,128)}, f32[128,512]{1,0:T(8,128)}, f32[128,512]{1,0:T(8,128)}, /*...) custom-call(bf16[8,128,2048]{2,1,0:T(8,128)(2,1)} %bitcast.72, bf16[8,128,1024]{2,1,0:T(8,128)(2,1)} %bitcast.73, ...), custom_call_target="tpu_custom_call" | custom-call | tf_op jit(solution)/shard_map/scatter_all/pallas_call | solution.py:765
  604.2 0.0 copy-start.8
  604.2 0.5 fusion.2
  604.7 0.0 collective-permute-done
  604.7 3.9 fusion.8
  608.6 0.7 pad_maximum_fusion
  609.3 0.0 all-reduce.4.cloned.1.call-update
  609.4 4.8 fusion.5
  614.2 114.4 %all-reduce.4.cloned.1.call-done = f32[37,1024]{1,0:T(8,128)} async-done(((f32[37,1024]{1,0:T(8,128)}), f32[37,1024]{1,0:T(8,128)}) %all-reduce.4.cloned.1.call-update) | async-done | bytes 151568 | tf_op jit(solution)/shard_map/psum | solution.py:874
  728.6 0.9 slice_reduce_fusion
  729.5 0.5 multiply_sqrt_fusion
  730.0 1.4 fusion.21
  731.4 1.3 dynamic-slice_bitcast_fusion.1
  732.7 1.7 copy.81
  734.4 1.7 copy.82
  736.1 1.7 copy.83
  737.7 0.7 copy.84
  738.4 0.7 copy.85
  739.2 0.9 copy.86
  740.0 0.9 copy.87
  740.9 0.9 copy.88
  (45 shorter events, 0.2 us)
Async XLA Ops:
  7.2 142.8 %copy-start.13 = (bf16[64]{0:T(256)(128)(2,1)S(1)}, bf16[64]{0:T(256)(128)(2,1)}, u32[]{:S(2)}) copy-start(bf16[64]{0:T(256)(128)(2,1)} %param.21) | copy-start | bytes 388
  7.2 142.8 %copy-start.12 = (bf16[64]{0:T(256)(128)(2,1)S(1)}, bf16[64]{0:T(256)(128)(2,1)}, u32[]{:S(2)}) copy-start(bf16[64]{0:T(256)(128)(2,1)} %param.22) | copy-start | bytes 388
  7.2 142.8 %copy-start.10 = (bf16[16,64]{1,0:T(8,128)(2,1)S(1)}, bf16[16,64]{1,0:T(8,128)(2,1)}, u32[]{:S(2)}) copy-start(bf16[16,64]{1,0:T(8,128)(2,1)} %param.31) | copy-start | bytes 6148
  7.2 142.8 %copy-start.9 = (bf16[16,64]{1,0:T(8,128)(2,1)S(1)}, bf16[16,64]{1,0:T(8,128)(2,1)}, u32[]{:S(2)}) copy-start(bf16[16,64]{1,0:T(8,128)(2,1)} %param.32) | copy-start | bytes 6148
  7.2 721.4 %all-reduce.4.cloned.1.call-start = ((), (), s32[]{:S(2)}) async-start(), calls=%async_computation.2 | async-start | bytes 327680 | tf_op jit(solution)/shard_map/psum | solution.py:874
  7.3 165.9 %copy-start.11 = (f32[16,4]{0,1:T(4,128)S(1)}, f32[16,4]{0,1:T(4,128)}, u32[]{:S(2)}) copy-start(f32[16,4]{0,1:T(4,128)} %param.35) | copy-start | bytes 772
  7.3 165.9 %copy-start.16 = (f32[16,4]{0,1:T(4,128)S(1)}, f32[16,4]{0,1:T(4,128)}, u32[]{:S(2)}) copy-start(f32[16,4]{0,1:T(4,128)} %param.34) | copy-start | bytes 772
  7.3 165.9 %copy-start.17 = (f32[16,4]{0,1:T(4,128)S(1)}, f32[16,4]{0,1:T(4,128)}, u32[]{:S(2)}) copy-start(f32[16,4]{0,1:T(4,128)} %param.33) | copy-start | bytes 772
  7.3 165.9 %copy-start.18 = (s32[32]{0:T(128)S(1)}, s32[32]{0:T(128)}, u32[]{:S(2)}) copy-start(s32[32]{0:T(128)} %param.37) | copy-start | bytes 388
  7.3 166.7 %copy-start.6 = (s32[2048]{0:T(1024)S(1)}, s32[2048]{0:T(1024)}, u32[]{:S(2)}) copy-start(s32[2048]{0:T(1024)} %param.36) | copy-start | bytes 24580
  175.9 3.5 copy-start.15
  414.9 4.7 copy-start.7
  418.0 186.7 %collective-permute-start = (bf16[1024,1024]{1,0:T(8,128)(2,1)}, bf16[1024,1024]{1,0:T(8,128)(2,1)}, u32[]{:S(2)}, u32[]{:S(2)}) collective-permute-start(bf16[1024,1024]{1,0:T(8,128)(2,1)} %constant_dynamic-slice_fusion.1), channel_id=1, source_target_pairs={{0,1},{1,0},{2,3},{3,2},{4,5},{5,4},{6,7},{7,6},{8,9},{9,8},{10,11... | collective-permute-start | bytes 6291464 | tf_op jit(solution)/shard_map/ppermute | solution.py:850
  419.6 4.6 copy-start.14
  435.3 168.9 %copy-start = (bf16[1024,1024]{1,0:T(8,128)(2,1)S(1)}, bf16[1024,1024]{1,0:T(8,128)(2,1)}, u32[]{:S(2)}) copy-start(bf16[1024,1024]{1,0:T(8,128)(2,1)} %x_ref.1) | copy-start | bytes 6291460
  604.2 4.4 copy-start.8
  609.4 128.4 %copy-start.5 = (f32[128,512]{1,0:T(8,128)S(1)}, f32[128,512]{1,0:T(8,128)}, u32[]{:S(2)}) copy-start(f32[128,512]{1,0:T(8,128)} %get-tuple-element.114) | copy-start | bytes 786436
  609.4 129.1 %copy-start.4 = (f32[128,512]{1,0:T(8,128)S(1)}, f32[128,512]{1,0:T(8,128)}, u32[]{:S(2)}) copy-start(f32[128,512]{1,0:T(8,128)} %get-tuple-element.115) | copy-start | bytes 786436
  609.4 129.8 %copy-start.3 = (f32[128,1408]{1,0:T(8,128)S(1)}, f32[128,1408]{1,0:T(8,128)}, u32[]{:S(2)}) copy-start(f32[128,1408]{1,0:T(8,128)} %get-tuple-element.116) | copy-start | bytes 2162692
  614.2 125.8 %copy-start.2 = (f32[128,1408]{1,0:T(8,128)S(1)}, f32[128,1408]{1,0:T(8,128)}, u32[]{:S(2)}) copy-start(f32[128,1408]{1,0:T(8,128)} %get-tuple-element.117) | copy-start | bytes 2162692
  614.2 126.7 %copy-start.1 = (f32[352,512]{1,0:T(8,128)S(1)}, f32[352,512]{1,0:T(8,128)}, u32[]{:S(2)}) copy-start(f32[352,512]{1,0:T(8,128)} %get-tuple-element.118) | copy-start | bytes 2162692
Sparse Core Ops, SparseCore 0:
  609.5 119.0 all-reduce.3

commit v2 on v1

--- a/solution.py
+++ b/solution.py
@@ -99,30 +99,88 @@
     lse_ref[...] = lse_all
 
 
-def mix_forward_kernel(heads, q_ref, k_ref, v_ref, g_ref, pk_ref, pv_ref, segc_ref, segr_ref,
-                       coef_ref, comb_ref, lse_ref, reads_ref, m0_ref, err_ref, mem, mom):
+def hop_bound(turn, tiles, hops):
+    return (turn * hops) // tiles
+
+
+def mix_forward_kernel(heads, n, tiles, q_ref, k_ref, v_ref, g_ref, pk_ref, pv_ref, segc_ref,
+                       segr_ref, coef_ref, b0, b1, b2, b3, lse_ref, reads_ref, m0_ref, err_ref,
+                       comb_out, w0, w1, w2, w3, mem, mom, comb_all, csems, *sems):
     tile = pl.program_id(0)
+    core = lax.axis_index("col")
+    blocks, wholes = (b0, b1, b2, b3), (w0, w1, w2, w3)
+    items = [(blk, ref, core * blk.shape[1], True) for blk, ref in zip(blocks, wholes)]
+    g = Gather(n, items, sems)
+    each = range(len(items))
+    width = heads * HD
+    per_core = tiles // 2
+
+    def hops(low, high):
+        def one(s, carry):
+            for m in each:
+                g.advance(m, s)
+            return carry
+
+        lax.fori_loop(low, high, one, 0)
+
+    def place(device, index):
+        return comb_out.at[pl.ds(index * TILE, TILE), pl.ds(device * width, width)]
 
     @pl.when(tile == 0)
     def clear():
+        greet(n, g.right, g.left, True, False)
+        g.begin(each)
         mem[...] = jnp.zeros_like(mem)
         mom[...] = jnp.zeros_like(mom)
+
+    @pl.when(tile > 0)
+    def pass_on():
+        hops(hop_bound(tile - 1, tiles, n - 1), hop_bound(tile, tiles, n - 1))
 
     for part in range(TPS):
         @pl.when(lax.rem(tile, TPS) == part)
         def work():
             mix_forward_tile(heads, part, tile, q_ref, k_ref, v_ref, g_ref, pk_ref, pv_ref,
-                             segc_ref, segr_ref, coef_ref, comb_ref, lse_ref, reads_ref, m0_ref,
-                             err_ref, mem, mom)
-
-
-def mix_forward(qkvg, pkey, pvalue, segc, segr, coef, heads):
+                             segc_ref, segr_ref, coef_ref, comb_all.at[tile], lse_ref, reads_ref,
+                             m0_ref, err_ref, mem, mom)
+
+    def stay(index):
+        return pltpu.make_async_copy(
+            comb_all.at[core * per_core + index], place(core, index), csems.at[0, index])
+
+    def leave(index):
+        return pltpu.make_async_remote_copy(
+            src_ref=comb_all.at[(1 - core) * per_core + index], dst_ref=place(core, index),
+            send_sem=csems.at[1, index], recv_sem=csems.at[2, index],
+            device_id={"col": 1 - core}, device_id_type=MESH)
+
+    index = lax.rem(tile, per_core)
+
+    @pl.when(tile // per_core == core)
+    def mine():
+        stay(index).start()
+
+    @pl.when(tile // per_core != core)
+    def theirs():
+        leave(index).start()
+
+    @pl.when(tile == tiles - 1)
+    def end():
+        hops(hop_bound(tiles - 1, tiles, n - 1), n - 1)
+        g.finish(each)
+        for i in range(per_core):
+            stay(i).wait()
+            leave(i).wait()
+
+
+def mix_forward(n, qkvg, pkey, pvalue, segc, segr, coef, heads, blocks):
     total = qkvg.shape[0]
     width = heads * HD
     tiles = total // TILE
     per = TILE // CH
+    any_spec = pl.BlockSpec(memory_space=pl.ANY)
     return pl.pallas_call(
-        functools.partial(mix_forward_kernel, heads),
+        functools.partial(mix_forward_kernel, heads, n, tiles),
         grid=(tiles,),
         in_specs=[
             pl.BlockSpec((TILE, width), lambda t: (t, 0)),
@@ -134,25 +192,30 @@
             pl.BlockSpec((TILE, 1), lambda t: (t, 0)),
             pl.BlockSpec((1, SEG), lambda t: (0, t // TPS)),
             pl.BlockSpec(memory_space=pltpu.SMEM),
-        ],
+        ] + [any_spec] * 4,
         out_specs=[
-            pl.BlockSpec((TILE, width), lambda t: (t, 0)),
             pl.BlockSpec((TILE, HD), lambda t: (t, 0)),
             pl.BlockSpec((TILE, width), lambda t: (t, 0)),
             pl.BlockSpec((per, heads, HD, HD), lambda t: (t, 0, 0, 0)),
             pl.BlockSpec((TILE, width), lambda t: (t, 0)),
-        ],
+        ] + [any_spec] * 5,
         out_shape=[
-            jax.ShapeDtypeStruct((total, width), BF),
             jax.ShapeDtypeStruct((total, HD), F32),
             jax.ShapeDtypeStruct((total, width), BF),
             jax.ShapeDtypeStruct((total // CH, heads, HD, HD), BF),
             jax.ShapeDtypeStruct((total, width), BF),
-        ],
-        scratch_shapes=[pltpu.VMEM((heads, HD, HD), F32), pltpu.VMEM((heads, HD, HD), F32)],
-        compiler_params=pltpu.CompilerParams(vmem_limit_bytes=VMEM_MAX),
+            jax.ShapeDtypeStruct((total // 2, 2 * width), BF),
+        ] + [jax.ShapeDtypeStruct((n, b.shape[0], 2 * b.shape[1]), BF) for b in blocks],
+        scratch_shapes=[
+            pltpu.VMEM((heads, HD, HD), F32),
+            pltpu.VMEM((heads, HD, HD), F32),
+            pltpu.VMEM((tiles, TILE, width), BF),
+            pltpu.SemaphoreType.DMA((3, tiles // 2)),
+        ] + gather_sems(n, 4),
+        compiler_params=pltpu.CompilerParams(
+            collective_id=3, has_side_effects=True, vmem_limit_bytes=VMEM_MAX),
         name="mix_forward",
-    )(qkvg, qkvg, qkvg, qkvg, pkey, pvalue, segc, segr, coef)
+    )(qkvg, qkvg, qkvg, qkvg, pkey, pvalue, segc, segr, coef, *blocks)
 
 
 def mix_backward_tile(heads, part, tile, q_ref, k_ref, v_ref, g_ref, dc_ref, pk_ref, pv_ref,
@@ -238,18 +301,46 @@
             dv_own - jnp.concatenate(dv_mem, axis=0)).astype(BF)
 
 
-def mix_backward_kernel(heads, tiles, q_ref, k_ref, v_ref, g_ref, dc_ref, pk_ref, pv_ref, segc_ref,
-                        segr_ref, coef_ref, lse_ref, reads_ref, m0_ref, err_ref, dout_ref, dpk_ref,
-                        dpv_ref, dmem, dmom, dk_acc, dv_acc):
+def mix_backward_kernel(heads, n, tiles, q_ref, k_ref, v_ref, g_ref, dc_ref, pk_ref, pv_ref,
+                        segc_ref, segr_ref, coef_ref, lse_ref, reads_ref, m0_ref, err_ref, *refs):
+    own_refs, sib_refs = refs[:4], refs[4:8]
+    dout_ref, dpk_ref, dpv_ref = refs[8:11]
+    outs = refs[11:15]
+    dmem, dmom, dk_acc, dv_acc = refs[15:19]
+    scratch = refs[19:39]
+    sems = refs[39:]
     turn = pl.program_id(0)
     tile = tiles - 1 - turn
+    items = [
+        (own_refs[m], 0, outs[m].shape[1], sib_refs[m]) + tuple(scratch[5 * m:5 * m + 5]) + (outs[m],)
+        for m in range(4)
+    ]
+    g = Scatter(n, items, sems)
+    order = (1, 2, 3, 0)
+
+    def hops(low, high):
+        def one(s, carry):
+            for m in order:
+                g.advance(m, s)
+            return carry
+
+        lax.fori_loop(low, high, one, 0)
 
     @pl.when(turn == 0)
     def clear():
+        greet(n, g.right, g.left, False, True)
+        g.begin(order)
         dmem[...] = jnp.zeros_like(dmem)
         dmom[...] = jnp.zeros_like(dmom)
         dpk_ref[...] = jnp.zeros_like(dpk_ref)
         dpv_ref[...] = jnp.zeros_like(dpv_ref)
+        for m in order:
+            g.ready(m)
+            g.start(m)
+
+    @pl.when(turn > 0)
+    def pass_on():
+        hops(1 + hop_bound(turn - 1, tiles - 1, n - 2), 1 + hop_bound(turn, tiles - 1, n - 2))
 
     for part in range(TPS):
         @pl.when(lax.rem(tile, TPS) == part)
@@ -258,15 +349,24 @@
                               segc_ref, segr_ref, coef_ref, lse_ref, reads_ref, m0_ref, err_ref,
                               dout_ref, dmem, dmom, dk_acc, dv_acc, dpk_ref, dpv_ref)
 
-
-def mix_backward(qkvg, dcomb, pkey, pvalue, segc, segr, coef, lse, reads, m0, err, heads):
+    @pl.when(turn == tiles - 1)
+    def end():
+        for m in order:
+            g.settle(m)
+        for m in order:
+            g.finish(m)
+
+
+def mix_backward(n, qkvg, dcomb, pkey, pvalue, segc, segr, coef, lse, reads, m0, err, heads, owns, sibs):
     total = qkvg.shape[0]
     width = heads * HD
     tiles = total // TILE
     per = TILE // CH
     last = tiles - 1
+    any_spec = pl.BlockSpec(memory_space=pl.ANY)
+    arrays = [(a, a.shape[2], True) for a in owns]
     return pl.pallas_call(
-        functools.partial(mix_backward_kernel, heads, tiles),
+        functools.partial(mix_backward_kernel, heads, n, tiles),
         grid=(tiles,),
         in_specs=[
             pl.BlockSpec((TILE, width), lambda t: (last - t, 0)),
@@ -283,39 +383,80 @@
             pl.BlockSpec((TILE, width), lambda t: (last - t, 0)),
             pl.BlockSpec((per, heads, HD, HD), lambda t: (last - t, 0, 0, 0)),
             pl.BlockSpec((TILE, width), lambda t: (last - t, 0)),
-        ],
+        ] + [any_spec] * 8,
         out_specs=[
             pl.BlockSpec((TILE, 4 * width), lambda t: (last - t, 0)),
             pl.BlockSpec((HD, width), lambda t: (0, 0)),
             pl.BlockSpec((HD, width), lambda t: (0, 0)),
-        ],
+        ] + [whole((a.shape[1], w)) for a, w, share in arrays],
         out_shape=[
             jax.ShapeDtypeStruct((total, 4 * width), BF),
             jax.ShapeDtypeStruct((HD, width), F32),
             jax.ShapeDtypeStruct((HD, width), F32),
-        ],
+        ] + [jax.ShapeDtypeStruct((a.shape[1], w), F32) for a, w, share in arrays],
         scratch_shapes=[
             pltpu.VMEM((heads, HD, HD), F32),
             pltpu.VMEM((heads, HD, HD), F32),
             pltpu.VMEM((SEG, width), F32),
             pltpu.VMEM((SEG, width), F32),
-        ],
-        compiler_params=pltpu.CompilerParams(vmem_limit_bytes=VMEM_MAX),
+        ] + scatter_plan(arrays) + scatter_sems(n, 4),
+        compiler_params=pltpu.CompilerParams(
+            collective_id=4, has_side_effects=True, vmem_limit_bytes=VMEM_MAX),
         name="mix_backward",
-    )(qkvg, qkvg, qkvg, qkvg, dcomb, pkey, pvalue, segc, segr, coef, lse, reads, m0, err)
-
-
-def ffn_kernel(tiles, comb_ref, x_ref, dy_ref, wo_ref, wg_ref, wu_ref, wd_ref, gain_ref, out_ref,
-               dmid_ref, dcomb_ref, go_ref, gg_ref, gu_ref, gd_ref, dgain_ref, sums_ref, n2, n2t,
-               mid, acc_out, acc_dn, hid_all, pair_all):
+    )(qkvg, qkvg, qkvg, qkvg, dcomb, pkey, pvalue, segc, segr, coef, lse, reads, m0, err, *owns, *sibs)
+
+
+def whole(shape):
+    return pl.BlockSpec(shape, lambda t: (0,) * len(shape), pipeline_mode=pl.Buffered(1))
+
+
+def ffn_kernel(tiles, comb_ref, x_ref, dy_ref, wo_ref, wg0, wg1, wu0, wu1, wd0, wd1, gain_ref,
+               out_ref, dmid_ref, dgain_ref, sums_ref, dcomb_out, go_own, go_sib, gg_own, gg_sib,
+               gu_own, gu_sib, gd_own, gd_sib, n2, n2t, mid, acc_out, acc_dn, hid_all, pair_all,
+               dcomb_v, go_v, gbuf, ubuf, dbuf, keep_sem, send_sem, recv_sem, end_sem):
     turn = pl.program_id(0)
+    core = lax.axis_index("col")
+    other = 1 - core
     rows_all, dim = x_ref.shape
+    half = dim // 2
     steps = rows_all // TILE
-    ft = wg_ref.shape[1]
+    ft = 2 * HD
     gain = gain_ref[...]
+    slot = lax.rem(turn, 2)
+    hidden_half = gg_own.shape[1]
+
+    def push(src, dst, sem, rsem):
+        return pltpu.make_async_remote_copy(
+            src_ref=src, dst_ref=dst, send_sem=sem, recv_sem=rsem,
+            device_id={"col": other}, device_id_type=MESH)
+
+    def moves(t, s):
+        stay, leave = [], []
+        for i, (buf, own, sib) in enumerate(((gbuf, gg_own, gg_sib), (ubuf, gu_own, gu_sib))):
+            cols = pl.ds(pl.multiple_of(t * HD, HD), HD)
+            stay.append(pltpu.make_async_copy(
+                buf.at[s, core], own.at[:, cols], keep_sem.at[i, s]))
+            leave.append(push(buf.at[s, other], sib.at[:, cols], send_sem.at[i, s], recv_sem.at[i]))
+        for i in range(2):
+            rows = pl.ds(pl.multiple_of(i * hidden_half + t * HD, HD), HD)
+            stay.append(pltpu.make_async_copy(
+                dbuf.at[s, core, pl.ds(i * HD, HD)], gd_own.at[rows, :], keep_sem.at[2 + i, s]))
+            leave.append(push(dbuf.at[s, other, pl.ds(i * HD, HD)], gd_sib.at[rows, :],
+                              send_sem.at[2 + i, s], recv_sem.at[2 + i]))
+        return stay, leave
+
+    def settle(t, s):
+        stay, leave = moves(t, s)
+        for copy in stay:
+            copy.wait()
+        for copy in leave:
+            copy.wait_send()
 
     @pl.when(turn == 0)
     def first():
+        barrier = pltpu.get_barrier_semaphore()
+        pl.semaphore_signal(barrier, inc=1, device_id={"col": other}, device_id_type=MESH)
+        pl.semaphore_wait(barrier, 1)
         sums_ref[...] = jnp.zeros_like(sums_ref)
         dgain_ref[...] = jnp.zeros_like(dgain_ref)
         for i in range(steps):
@@ -333,8 +474,8 @@
             sums_ref[0:1, :] += jnp.sum(xf * xf, axis=0, keepdims=True)
             sums_ref[1:2, :] += jnp.sum(branch * branch, axis=0, keepdims=True)
 
-    wd = wd_ref[...]
-    both = jnp.concatenate([wg_ref[...], wu_ref[...]], axis=1)
+    wd = jnp.concatenate([wd0[...], wd1[...]], axis=0)
+    both = jnp.concatenate([wg0[...], wg1[...], wu0[...], wu1[...]], axis=1)
     for i in range(steps):
         rows = slice(i * TILE, (i + 1) * TILE)
         gateup = nn(n2[rows, :], both)
@@ -350,10 +491,20 @@
         pair_all[rows, :] = pair
         acc_out[rows, :] += nn(hid, wd)
         acc_dn[rows, :] += nt(pair, both)
-    gd_ref[...] = tn(hid_all[...], dy_ref[...]).astype(BF)
-    grads = nn(n2t[...], pair_all[...])
-    gg_ref[...] = grads[:, :ft].astype(BF)
-    gu_ref[...] = grads[:, ft:].astype(BF)
+
+    @pl.when(turn >= 2)
+    def reuse():
+        settle(turn - 2, slot)
+
+    down = tn(hid_all[...], dy_ref[...]).astype(BF)
+    grads = nn(n2t[...], pair_all[...]).astype(BF)
+    for i in range(2):
+        gbuf[slot, i] = grads[:, i * HD:(i + 1) * HD]
+        ubuf[slot, i] = grads[:, ft + i * HD:ft + (i + 1) * HD]
+        dbuf[slot, i] = down[:, i * half:(i + 1) * half]
+    stay, leave = moves(turn, slot)
+    for copy in stay + leave:
+        copy.start()
 
     @pl.when(turn == tiles - 1)
     def last():
@@ -371,21 +522,46 @@
             dmid = dy_ref[rows, :].astype(F32) + weighted * inv - middle * (inv * inv * inv) * inner
             low = dmid.astype(BF)
             dmid_ref[rows, :] = low
-            dcomb_ref[rows, :] = nt(low, wo_ref[...]).astype(BF)
+            dcomb = nt(low, wo_ref[...]).astype(BF)
+            dcomb_v[0, rows, :] = dcomb[:, :half]
+            dcomb_v[1, rows, :] = dcomb[:, half:]
+        home = pl.ds(pl.multiple_of(core * rows_all, TILE), rows_all)
+        stay_c = pltpu.make_async_copy(dcomb_v.at[core], dcomb_out.at[home, :], end_sem.at[0])
+        leave_c = push(dcomb_v.at[other], dcomb_out.at[home, :], end_sem.at[1], end_sem.at[2])
+        stay_c.start()
+        leave_c.start()
         for i in range(dim // TILE):
             part = slice(i * TILE, (i + 1) * TILE)
-            go_ref[part, :] = tn(comb_ref[:, part], dmid_ref[...]).astype(BF)
-
-
-def whole(shape):
-    return pl.BlockSpec(shape, lambda t: (0,) * len(shape), pipeline_mode=pl.Buffered(1))
+            go = tn(comb_ref[:, part], dmid_ref[...]).astype(BF)
+            go_v[0, part, :] = go[:, :half]
+            go_v[1, part, :] = go[:, half:]
+        stay_o = pltpu.make_async_copy(go_v.at[core], go_own, end_sem.at[3])
+        leave_o = push(go_v.at[other], go_sib, end_sem.at[4], end_sem.at[5])
+        stay_o.start()
+        leave_o.start()
+        settle(turn - 1, 1 - slot)
+        settle(turn, slot)
+        for i, sib in enumerate((gg_sib, gu_sib)):
+            push(sib, sib, send_sem.at[i, 0], recv_sem.at[i]).wait_recv()
+        for i in range(2):
+            part = gd_sib.at[pl.ds(i * hidden_half, hidden_half), :]
+            push(part, part, send_sem.at[2 + i, 0], recv_sem.at[2 + i]).wait_recv()
+        stay_c.wait()
+        stay_o.wait()
+        leave_c.wait()
+        leave_o.wait()
 
 
 def ffn_block(comb, x, dy, w_out, w_gate, w_up, w_down, gain):
     rows, dim = x.shape
     hidden = w_gate.shape[1]
-    tiles = hidden // TILE
+    tiles = hidden // (2 * HD)
     full = (rows, dim)
+    half = dim // 2
+    any_spec = pl.BlockSpec(memory_space=pl.ANY)
+    front = pl.BlockSpec((dim, HD), lambda t: (0, t))
+    rear = pl.BlockSpec((dim, HD), lambda t: (0, t + tiles))
+    dma = pltpu.SemaphoreType.DMA
     return pl.pallas_call(
         functools.partial(ffn_kernel, tiles),
         grid=(tiles,),
@@ -394,45 +570,47 @@
             whole(full),
             whole(full),
             whole((dim, dim)),
-            pl.BlockSpec((dim, TILE), lambda t: (0, t)),
-            pl.BlockSpec((dim, TILE), lambda t: (0, t)),
-            pl.BlockSpec((TILE, dim), lambda t: (t, 0)),
+            front,
+            rear,
+            front,
+            rear,
+            pl.BlockSpec((HD, dim), lambda t: (t, 0)),
+            pl.BlockSpec((HD, dim), lambda t: (t + tiles, 0)),
             whole((1, dim)),
         ],
-        out_specs=[
-            whole(full),
-            whole(full),
-            whole(full),
-            whole((dim, dim)),
-            pl.BlockSpec((dim, TILE), lambda t: (0, t)),
-            pl.BlockSpec((dim, TILE), lambda t: (0, t)),
-            pl.BlockSpec((TILE, dim), lambda t: (t, 0)),
-            whole((1, dim)),
-            whole((8, dim)),
-        ],
+        out_specs=[whole(full), whole(full), whole((1, dim)), whole((8, dim))] + [any_spec] * 9,
         out_shape=[
             jax.ShapeDtypeStruct(full, BF),
             jax.ShapeDtypeStruct(full, BF),
-            jax.ShapeDtypeStruct(full, BF),
-            jax.ShapeDtypeStruct((dim, dim), BF),
-            jax.ShapeDtypeStruct((dim, hidden), BF),
-            jax.ShapeDtypeStruct((dim, hidden), BF),
-            jax.ShapeDtypeStruct((hidden, dim), BF),
             jax.ShapeDtypeStruct((1, dim), F32),
             jax.ShapeDtypeStruct((8, dim), F32),
-        ],
+            jax.ShapeDtypeStruct((2 * rows, half), BF),
+        ]
+        + [jax.ShapeDtypeStruct((dim, half), BF)] * 2
+        + [jax.ShapeDtypeStruct((dim, hidden // 2), BF)] * 4
+        + [jax.ShapeDtypeStruct((hidden, half), BF)] * 2,
         scratch_shapes=[
             pltpu.VMEM(full, BF),
             pltpu.VMEM((dim, rows), BF),
             pltpu.VMEM(full, F32),
             pltpu.VMEM(full, F32),
             pltpu.VMEM(full, F32),
-            pltpu.VMEM((rows, TILE), BF),
-            pltpu.VMEM((rows, 2 * TILE), BF),
+            pltpu.VMEM((rows, 2 * HD), BF),
+            pltpu.VMEM((rows, 4 * HD), BF),
+            pltpu.VMEM((2, rows, half), BF),
+            pltpu.VMEM((2, dim, half), BF),
+            pltpu.VMEM((2, 2, dim, HD), BF),
+            pltpu.VMEM((2, 2, dim, HD), BF),
+            pltpu.VMEM((2, 2, 2 * HD, half), BF),
+            dma((4, 2)),
+            dma((4, 2)),
+            dma((4,)),
+            dma((6,)),
         ],
-        compiler_params=pltpu.CompilerParams(vmem_limit_bytes=VMEM_MAX),
+        compiler_params=pltpu.CompilerParams(
+            collective_id=5, has_side_effects=True, vmem_limit_bytes=VMEM_MAX),
         name="ffn_block",
-    )(comb, x, dy, w_out, w_gate, w_up, w_down, gain)
+    )(comb, x, dy, w_out, w_gate, w_gate, w_up, w_up, w_down, w_down, gain)
 
 
 def ring_place(row, n):
@@ -445,6 +623,8 @@
 
 def split_cols(width, flip):
     tiles = width // HD
+    if tiles == 1:
+        return ((0, width),)
     first = (tiles + (0 if flip else 1)) // 2 * HD
     return ((0, first), (first, width - first))
 
@@ -483,6 +663,9 @@
         self.row = lax.axis_index("row")
         self.other = 1 - lax.axis_index("col")
 
+    def ways(self, m):
+        return range(len(split_cols(self.items[m][0].shape[1], m % 2)))
+
     def hop(self, m, d, s):
         block, whole_ref, base, share = self.items[m]
         place = mod(self.me - s, self.n) if d == 0 else mod(self.me + s, self.n)
@@ -511,7 +694,7 @@
 
     def begin(self, ms):
         for m in ms:
-            for d in (0, 1):
+            for d in self.ways(m):
                 self.ring(m, d, 0, first=True).start()
         for m in ms:
             block, whole_ref, base, share = self.items[m]
@@ -520,7 +703,7 @@
                 self.across(m, block, whole_ref.at[self.row, :, pl.ds(base, block.shape[1])]).start()
 
     def advance(self, m, s):
-        for d in (0, 1):
+        for d in self.ways(m):
             self.ring(m, d, s).wait_recv()
 
             @pl.when(s < self.n - 2)
@@ -542,7 +725,7 @@
                 self.across(m, spot, theirs).wait_send()
 
             def sent(s, carry):
-                for d in (0, 1):
+                for d in self.ways(m):
                     self.ring(m, d, s).wait_send()
                 return carry
 
@@ -559,86 +742,77 @@
     ]
 
 
-def gather_kernel(n, first, *refs):
-    blocks = refs[:8]
-    x_ref = refs[8]
-    wide, w_out, w_gate, w_up, w_down, pair = refs[9:15]
-    sems = refs[15:20]
-    xsems = refs[20]
+def gather_kernel(n, *refs):
+    blocks = refs[:5]
+    x_ref = refs[5]
+    wide, small, pair = refs[6:9]
+    sems = refs[9:14]
+    xsems = refs[14]
     core = lax.axis_index("col")
     items = [(blocks[m], wide, m * blocks[m].shape[1], False) for m in range(4)]
-    items += [(blocks[m], ref, core * blocks[m].shape[1], True)
-              for m, ref in zip(range(4, 8), (w_out, w_gate, w_up, w_down))]
+    items.append((blocks[4], small, core * blocks[4].shape[1], True))
     g = Gather(n, items, sems)
     greet(n, g.right, g.left, True, False)
-    g.begin(range(4))
+    g.begin(range(5))
     mine = pltpu.make_async_copy(x_ref, pair.at[core], xsems.at[0])
     mine.start()
     theirs = pltpu.make_async_remote_copy(
         src_ref=x_ref, dst_ref=pair.at[core], send_sem=xsems.at[1], recv_sem=xsems.at[2],
         device_id={"col": 1 - core}, device_id_type=MESH)
     theirs.start()
-    g.begin(range(4, 8))
 
     def step(s, carry):
-        for m in range(8):
+        for m in range(5):
             g.advance(m, s)
         return carry
 
     lax.fori_loop(0, n - 1, step, 0)
-    g.finish(range(8))
+    g.finish(range(5))
     mine.wait()
     theirs.wait()
 
 
-def gather_all(n, blocks, x):
-    rows = [block.shape[0] for block in blocks]
-    width = blocks[0].shape[1]
+def gather_first(n, blocks, small, x):
+    rows, width = blocks[0].shape
     any_spec = pl.BlockSpec(memory_space=pl.ANY)
-    shapes = [(n, rows[0], 4 * width)] + [(n, rows[m], 2 * blocks[m].shape[1]) for m in range(4, 8)]
-    shapes.append((2,) + x.shape)
+    shapes = [(n, rows, 4 * width), (n, small.shape[0], 2 * small.shape[1]), (2,) + x.shape]
     return pl.pallas_call(
-        functools.partial(gather_kernel, n, 4),
-        in_specs=[any_spec] * 9,
-        out_specs=[any_spec] * 6,
+        functools.partial(gather_kernel, n),
+        in_specs=[any_spec] * 6,
+        out_specs=[any_spec] * 3,
         out_shape=[jax.ShapeDtypeStruct(shape, BF) for shape in shapes],
-        scratch_shapes=gather_sems(n, 8) + [pltpu.SemaphoreType.DMA((3,))],
+        scratch_shapes=gather_sems(n, 5) + [pltpu.SemaphoreType.DMA((3,))],
         compiler_params=pltpu.CompilerParams(collective_id=1, has_side_effects=True),
-        name="gather_all",
-    )(*blocks, x)
+        name="gather_first",
+    )(*blocks, small, x)
 
 
 class Scatter:
     def __init__(self, n, items, sems):
         self.n = n
         self.items = items
-        self.send, self.recv, self.local, self.csend, self.crecv, self.dsend, self.drecv = sems
+        self.send, self.recv, self.local, self.sib, self.dsend, self.drecv = sems
         self.me, self.right, self.left = neighbours(n)
-        self.row = lax.axis_index("row")
-        self.core = lax.axis_index("col")
         self.twin = 1 - lax.axis_index("dp")
 
-    def load(self, m):
-        whole_ref, base, width, share, own = self.items[m][:5]
-        return pltpu.make_async_copy(whole_ref.at[:, :, pl.ds(base, width)], own, self.local.at[m])
-
-    def across(self, m):
-        whole_ref, base, width, share, own, sib = self.items[m][:6]
-        return pltpu.make_async_remote_copy(
-            src_ref=whole_ref.at[:, :, pl.ds((1 - self.core) * width, width)], dst_ref=sib,
-            send_sem=self.csend.at[m], recv_sem=self.crecv.at[m],
-            device_id={"col": 1 - self.core}, device_id_type=MESH)
+    def ways(self, m):
+        return range(len(split_cols(self.items[m][2], m % 2)))
+
+    def loads(self, m):
+        ref, base, width, other, own, sib = self.items[m][:6]
+        copies = [pltpu.make_async_copy(ref.at[:, :, pl.ds(base, width)], own, self.local.at[m])]
+        if other is not None:
+            copies.append(pltpu.make_async_copy(other, sib, self.sib.at[m]))
+        return copies
 
     def begin(self, ms):
         for m in ms:
-            if self.items[m][3]:
-                self.across(m).start()
-            self.load(m).start()
+            for copy in self.loads(m):
+                copy.start()
 
     def ready(self, m):
-        self.load(m).wait()
-        if self.items[m][3]:
-            self.across(m).wait_recv()
+        for copy in self.loads(m):
+            copy.wait()
 
     def part(self, m, d, s):
         place = mod(self.me - 1 - s, self.n) if d == 0 else mod(self.me + 1 + s, self.n)
@@ -654,27 +828,27 @@
             device_id={"row": self.right if d == 0 else self.left}, device_id_type=MESH)
 
     def total(self, m, d, s, arrived):
-        whole_ref, base, width, share, own, sib, ring = self.items[m][:7]
+        other, own, sib, ring = self.items[m][3:7]
         owner, cols = self.part(m, d, s)
         value = own[owner, :, cols].astype(F32)
-        if share:
+        if other is not None:
             value = value + sib[owner, :, cols].astype(F32)
         if arrived:
             value = value + ring[s - 1, :, cols].astype(F32)
-        return owner, cols, value
+        return owner, cols, value.astype(own.dtype)
 
     def start(self, m):
-        for d in (0, 1):
-            owner, cols, value = self.total(m, d, 0, False)
-            if self.items[m][3]:
-                self.items[m][4][owner, :, cols] = value.astype(BF)
+        for d in self.ways(m):
+            if self.items[m][3] is not None:
+                owner, cols, value = self.total(m, d, 0, False)
+                self.items[m][4][owner, :, cols] = value
             self.ring(m, d, 0).start()
 
     def advance(self, m, s):
-        for d in (0, 1):
+        for d in self.ways(m):
             self.ring(m, d, s - 1).wait_recv()
             owner, cols, value = self.total(m, d, s, True)
-            self.items[m][4][owner, :, cols] = value.astype(BF)
+            self.items[m][4][owner, :, cols] = value
             self.ring(m, d, s).start()
 
     def swap(self, m):
@@ -684,10 +858,10 @@
             device_id={"dp": self.twin}, device_id_type=MESH)
 
     def settle(self, m):
-        for d in (0, 1):
+        for d in self.ways(m):
             self.ring(m, d, self.n - 2).wait_recv()
             owner, cols, value = self.total(m, d, self.n - 1, True)
-            self.items[m][7][:, cols] = value.astype(BF)
+            self.items[m][7][:, cols] = value
         self.swap(m).start()
 
     def finish(self, m):
@@ -695,11 +869,9 @@
         self.swap(m).wait_recv()
         out[...] = low[...].astype(F32) + twin[...].astype(F32)
         self.swap(m).wait_send()
-        if self.items[m][3]:
-            self.across(m).wait_send()
 
         def sent(s, carry):
-            for d in (0, 1):
+            for d in self.ways(m):
                 self.ring(m, d, s).wait_send()
             return carry
 
@@ -710,68 +882,81 @@
     return [
         pltpu.SemaphoreType.DMA((count, 2, n - 1)),
         pltpu.SemaphoreType.DMA((count, 2, n - 1)),
-    ] + [pltpu.SemaphoreType.DMA((count,))] * 5
+    ] + [pltpu.SemaphoreType.DMA((count,))] * 4
 
 
 def scatter_plan(arrays):
     scratch = []
     for array, width, share in arrays:
         n, rows, full = array.shape
-        scratch.append(pltpu.VMEM((n, rows, width), BF))
-        scratch.append(pltpu.VMEM((n, rows, width) if share else (1, 16, HD), BF))
-        scratch.append(pltpu.VMEM((n - 1, rows, width), BF))
-        scratch.append(pltpu.VMEM((rows, width), BF))
-        scratch.append(pltpu.VMEM((rows, width), BF))
+        kind = array.dtype
+        scratch.append(pltpu.VMEM((n, rows, width), kind))
+        scratch.append(pltpu.VMEM((n, rows, width) if share else (1, 16, HD), kind))
+        scratch.append(pltpu.VMEM((n - 1, rows, width), kind))
+        scratch.append(pltpu.VMEM((rows, width), kind))
+        scratch.append(pltpu.VMEM((rows, width), kind))
     return scratch
 
 
 def scatter_kernel(n, count, *refs):
-    wide, go, gg, gu, gd = refs[:5]
-    outs = refs[5:5 + count]
-    scratch = refs[5 + count:5 + 6 * count]
-    sems = refs[5 + 6 * count:]
+    wide, small = refs[:2]
+    outs = refs[2:2 + count]
+    scratch = refs[2 + count:2 + 6 * count]
+    small_sib, small_sems = refs[2 + 6 * count:4 + 6 * count]
+    sems = refs[4 + 6 * count:]
     core = lax.axis_index("col")
     items = []
     for m in range(count):
-        ref = wide if m < 4 else (go, gg, gu, gd)[m - 4]
         width = outs[m].shape[1]
-        base = m * width if m < 4 else core * width
-        items.append((ref, base, width, m >= 4) + tuple(scratch[5 * m:5 * m + 5]) + (outs[m],))
+        ref, base, other = (wide, m * width, None) if m < 4 else (small, core * width, small_sib)
+        items.append((ref, base, width, other) + tuple(scratch[5 * m:5 * m + 5]) + (outs[m],))
     g = Scatter(n, items, sems)
     greet(n, g.right, g.left, True, True)
-    order = (5, 6, 7, 4, 0, 1, 2, 3)
+    width = outs[4].shape[1]
+    cross = pltpu.make_async_remote_copy(
+        src_ref=small.at[:, :, pl.ds((1 - core) * width, width)], dst_ref=small_sib,
+        send_sem=small_sems.at[0], recv_sem=small_sems.at[1],
+        device_id={"col": 1 - core}, device_id_type=MESH)
+    cross.start()
+    order = range(4)
     g.begin(order)
     for m in order:
         g.ready(m)
         g.start(m)
+    cross.wait()
+    g.begin((4,))
+    g.ready(4)
+    g.start(4)
 
     def step(s, carry):
-        for m in order:
+        for m in range(count):
             g.advance(m, s)
         return carry
 
     lax.fori_loop(1, n - 1, step, 0)
-    for m in order:
+    for m in range(count):
         g.settle(m)
-    for m in order:
+    for m in range(count):
         g.finish(m)
 
 
-def scatter_all(n, wide, go, gg, gu, gd):
+def scatter_last(n, wide, small):
     width = wide.shape[2] // 4
-    arrays = [(wide, width, False)] * 4 + [(a, a.shape[2] // 2, True) for a in (go, gg, gu, gd)]
+    arrays = [(wide, width, False)] * 4 + [(small, HD, True)]
     count = len(arrays)
     any_spec = pl.BlockSpec(memory_space=pl.ANY)
     return pl.pallas_call(
         functools.partial(scatter_kernel, n, count),
-        in_specs=[any_spec] * 5,
+        in_specs=[any_spec] * 2,
         out_specs=[pl.BlockSpec(memory_space=pltpu.VMEM)] * count,
         out_shape=[jax.ShapeDtypeStruct((a.shape[1], w), F32) for a, w, share in arrays],
-        scratch_shapes=scatter_plan(arrays) + scatter_sems(n, count),
+        scratch_shapes=scatter_plan(arrays)
+        + [pltpu.VMEM((n, small.shape[1], HD), F32), pltpu.SemaphoreType.DMA((2,))]
+        + scatter_sems(n, count),
         compiler_params=pltpu.CompilerParams(
             collective_id=2, has_side_effects=True, vmem_limit_bytes=VMEM_MAX),
-        name="scatter_all",
-    )(wide, go, gg, gu, gd)
+        name="scatter_last",
+    )(wide, small)
 
 
 def local(
@@ -803,19 +988,16 @@
     piece = gain_attn.shape[0]
     small = jnp.concatenate(
         [persist_key, persist_value, gain_attn[None, :], gain_ffn[None, :]], axis=0)
-    small_all = lax.all_gather(small, ("row", "col"), axis=1, tiled=True)
+    small = jnp.pad(small, ((0, 48 - small.shape[0]), (0, HD - piece)))
+    wide, small_all, pair = gather_first(n, (w_query, w_key, w_value, w_gate), small, tokens_in)
+    wide = wide.reshape(dim, 4 * width)
+    small_all = small_all.reshape(n, 48, 2, HD)[:, :, :, :piece].transpose(1, 0, 2, 3).reshape(48, dim)
     gain_a = small_all[2 * P_SIZE][None, :].astype(F32)
     gain_f = small_all[2 * P_SIZE + 1][None, :].astype(F32)
     own_small = lax.dynamic_slice_in_dim(small_all, core * width, width, 1)
     pad = ((0, HD - P_SIZE), (0, 0))
     pkey = jnp.pad(own_small[:P_SIZE], pad)
     pvalue = jnp.pad(own_small[P_SIZE:2 * P_SIZE], pad)
-
-    blocks = (w_query, w_key, w_value, w_gate, w_out, w_ffn_gate, w_ffn_up, w_ffn_down)
-    wide, full_out, full_gate, full_up, full_down, pair = gather_all(n, blocks, tokens_in)
-    wide = wide.reshape(dim, 4 * width)
-    full_out, full_gate, full_up = [a.reshape(dim, -1) for a in (full_out, full_gate, full_up)]
-    full_down = full_down.reshape(-1, dim)
 
     inputs = pair.reshape(2 * local_tok, dim).astype(F32)
     inverse_a = lax.rsqrt(jnp.mean(inputs * inputs, axis=-1, keepdims=True) + EPS)
@@ -835,13 +1017,17 @@
     ).reshape(4, spans * heads)
     segc, segr = segment_ids[:, None], segment_ids[None, :]
 
-    comb, lse, reads, m0, err = mix_forward(qkvg, pkey, pvalue, segc, segr, coef, heads)
-    comb_tok = lax.all_to_all(comb, "col", split_axis=0, concat_axis=1, tiled=True)
-    result, dmid, dcomb_tok, go, gg, gu, gd, dgain_f, sums = ffn_block(
+    later = (w_out, w_ffn_gate, w_ffn_up, w_ffn_down)
+    lse, reads, m0, err, comb_tok, full_out, full_gate, full_up, full_down = mix_forward(
+        n, qkvg, pkey, pvalue, segc, segr, coef, heads, later)
+    full_out, full_gate, full_up = [a.reshape(dim, -1) for a in (full_out, full_gate, full_up)]
+    full_down = full_down.reshape(-1, dim)
+    result, dmid, dgain_f, sums, dcomb, *parts = ffn_block(
         comb_tok, tokens_in, grad_out, full_out, full_gate, full_up, full_down, gain_f)
-    dcomb = lax.all_to_all(dcomb_tok, "col", split_axis=1, concat_axis=0, tiled=True)
-    dqkvg, dpk, dpv = mix_backward(
-        qkvg, dcomb, pkey, pvalue, segc, segr, coef, lse, reads, m0, err, heads)
+    parts = [a.reshape(n, a.shape[0] // n, a.shape[1]) for a in parts]
+    dqkvg, dpk, dpv, *grads_late = mix_backward(
+        n, qkvg, dcomb, pkey, pvalue, segc, segr, coef, lse, reads, m0, err, heads,
+        parts[0::2], parts[1::2])
 
     g_wide = tn(normed, dqkvg).astype(BF)
     back = nt(dqkvg, wide).astype(BF)
@@ -856,26 +1042,20 @@
     grad_in = (dmid.astype(F32) + weighted * inv - xf * (inv * inv * inv) * inner).astype(BF)
     dgain_a = jnp.sum(dnorm * xf * inv, axis=0)
 
-    rows = dim // n
-    hidden_rows = full_down.shape[0] // n
-    grads = scatter_all(
-        n,
-        g_wide.reshape(n, rows, 4 * width),
-        go.reshape(n, rows, dim),
-        gg.reshape(n, rows, -1),
-        gu.reshape(n, rows, -1),
-        gd.reshape(n, hidden_rows, dim),
-    )
-
     place = jnp.zeros((2 * P_SIZE, dim), F32)
     place = lax.dynamic_update_slice_in_dim(
         place, jnp.concatenate([dpk[:P_SIZE], dpv[:P_SIZE]], axis=0), core * width, 1)
-    packed = jnp.concatenate([place, dgain_a[None, :], dgain_f, sums[:3]], axis=0)
-    summed = lax.psum(packed, ("dp", "row", "col"))
+    packed = jnp.concatenate([place, dgain_a[None, :], dgain_f], axis=0)
+    packed = packed.reshape(2 * P_SIZE + 2, n, 2, piece).transpose(1, 0, 2, 3)
+    packed = jnp.pad(packed, ((0, 0), (0, 0), (0, 0), (0, HD - piece)))
+    stats = jnp.sum(sums.reshape(8, dim // HD, HD), axis=1)[:6]
+    stats = jnp.broadcast_to(stats[None, :, None, :], (n, 6, 2, HD))
+    packed = jnp.concatenate([packed, stats], axis=1).reshape(n, 2 * P_SIZE + 8, 2 * HD)
+    *grads, part = scatter_last(n, g_wide.reshape(n, dim // n, 4 * width), packed)
+    grads = grads + grads_late
     entry_count = local_tok * dim * lax.axis_size("dp") * n * lax.axis_size("col")
-    rms_stats = jnp.sqrt(jnp.sum(summed[2 * P_SIZE + 2:], axis=1) / entry_count)
-    slot = lax.axis_index("row") * 2 + core
-    part = lax.dynamic_slice_in_dim(summed, slot * piece, piece, 1)
+    rms_stats = jnp.sqrt(jnp.sum(part[2 * P_SIZE + 2:2 * P_SIZE + 5], axis=1) / entry_count)
+    part = part[:, :piece]
     return (
         result,
         grad_in,

time: 756 us -> 548 us (0.72)
  waiting for transfers between devices: 114 us -> 0.01 us
  Pallas kernels: 502 us -> 458 us
  blocking collectives: 34 us -> 0 us
  between operations: 14.8 us -> 1.45 us
    psum x1 -> x0, waiting for transfers between devices: 114 us -> none  [local(): summed = lax.psum(packed, ('dp', 'row', 'col'))]
    pallas_call x4, Pallas kernels: 424 us -> 375 us  [the longest x1 132 us: mix_backward(): pl.pallas_call(functools.partial(mix_backward_kernel, heads, n, tiles), g...]
    all_gather x1 -> x0, blocking collectives: 21 us -> none  [local(): small_all = lax.all_gather(small, ('row', 'col'), axis=1, tiled=True)]
    all_to_all x2 -> x0, blocking collectives: 12.9 us -> none  [the longest x1 6.63 us: local(): lax.all_to_all(comb, 'col', split_axis=0, concat_axis=1, tiled=True)]
  transfers between devices with their start and end apart: 2 -> 1, of which waited for: 1 -> 0; matrix products, arithmetic and copies ran while one was open for 3% -> 4% of each run, Pallas kernels for 23% -> 0%
where the time goes in v2:
time: 548 us; the launch traced here: 543 us
  Pallas kernels  458 us (84%)
  matrix products  39.3 us (7%)
  local copies, waits for them, and re-layouts  22.9 us (4%)
  other arithmetic  21.7 us (4%)
    pallas_call x1, Pallas kernels, mix_backward(): pl.pallas_call(functools.partial(mix_backward_kernel, heads, n, tiles), g...  132 us
    pallas_call x1, Pallas kernels, mix_forward(): pl.pallas_call(functools.partial(mix_forward_kernel, heads, n, tiles), gr...  101 us
    pallas_call x1, Pallas kernels, gather_first(): pl.pallas_call(functools.partial(gather_kernel, n), in_specs=[any_spec] *...  85.3 us
    pallas_call x1, Pallas kernels, ffn_block(): pl.pallas_call(functools.partial(ffn_kernel, tiles), grid=(tiles,), in_sp...  82.5 us
    pallas_call x1, Pallas kernels, scatter_last(): pl.pallas_call(functools.partial(scatter_kernel, n, count), in_specs=[any...  57.7 us
    dot_general x1, matrix products, tn(): lax.dot_general(a, b, (((0,), (0,)), ((), ())), preferred_element_type=F32)  14.4 us
    dot_general x1, matrix products, nt(): lax.dot_general(a, b, (((1,), (1,)), ((), ())), preferred_element_type=F32)  13.9 us
  transfers between devices with their start and end apart: 1, of which 0 were waited for; matrix products, arithmetic and copies ran while one was open for 4% of the time, Pallas kernels for 0%

profile of v2, /device:TPU:0, one launch (start us, length us, event | category | flops | bytes accessed | tf_op | source)
XLA Modules:
  0.0 543.4 jit_solution(5676783176028067618)
XLA Ops:
  0.7 1.4 fusion.21.refs_4_
  2.1 85.3 %gather_first.1 = (bf16[8,128,2048]{2,1,0:T(8,128)(2,1)}, bf16[8,48,256]{2,1,0:T(8,128)(2,1)}, bf16[2,1024,1024]{2,1,0:T(8,128)(2,1)}) custom-call(bf16[128,512]{1,0:T(8,128)(2,1)} %refs_0_.1, bf16[128,512]{1,0:T(8,128)(2,1)} %refs_1_.1, bf16[128,512]{1,0:T(8,128)(2,1)} %refs_2_.1, bf16[128,512]{1,0:T(8,128)(2,1)} %refs_3_.1, ...), custom_call_target="tpu_custom_call" | custom-call | tf_op jit(solution)/shard_map/gather_first/pallas_call | solution.py:779
  87.4 1.0 reshape.213
  88.4 0.1 copy_bitcast_fusion
  88.5 0.2 reshape.215
  88.7 0.1 reshape.232
  88.8 3.1 multiply_reduce_fusion
  91.9 0.7 pad.16.pk_ref
  92.6 0.7 pad.17.pv_ref
  93.3 0.2 fusion.16
  93.5 0.1 copy.47
  93.6 0.1 stack.12
  93.7 0.1 copy.48
  93.8 0.1 stack.13
  93.9 0.1 copy.49
  94.0 0.1 stack.14
  94.1 0.1 reshape.216
  94.2 0.2 fusion.17
  94.4 0.1 fusion.31
  94.4 0.1 stack_broadcast_in_dim.13
  94.5 0.1 stack_broadcast_in_dim.14
  94.6 1.3 copy.50.segc_ref
  96.0 0.7 reshape.234.gain_ref
  96.7 2.9 multiply_convert_fusion
  99.6 0.5 copy-done.16
  100.1 10.9 %convolution_convert_fusion.q_ref.k_ref.v_ref.g_ref = bf16[2048,2048]{1,0:T(8,128)(2,1)} fusion(bf16[2048,1024]{1,0:T(8,128)(2,1)S(1)} %bitcast.59, bf16[1024,2048]{1,0:T(8,128)(2,1)S(1)} %bitcast.78), kind=kOutput, calls=%fused_computation.5 | convolution fusion | flops 8594128896 | bytes 16777216 | tf_op jit(solution)/shard_map/dot_general | solution.py:28
  111.0 0.6 pad_maximum_fusion.coef_ref
  111.6 100.7 %mix_forward.1 = (f32[2048,128]{1,0:T(8,128)}, bf16[2048,512]{1,0:T(8,128)(2,1)}, bf16[32,4,128,128]{3,2,1,0:T(8,128)(2,1)}, bf16[2048,512]{1,0:T(8,128)(2,1)}, ...) custom-call(bf16[2048,2048]{1,0:T(8,128)(2,1)} %convolution_convert_, ...), custom_call_target="tpu_custom_call" | custom-call | tf_op jit(solution)/shard_map/mix_forward/pallas_call | solution.py:182
  212.3 82.5 %ffn_block.1 = (bf16[1024,1024]{1,0:T(8,128)(2,1)}, bf16[1024,1024]{1,0:T(8,128)(2,1)}, f32[1,1024]{1,0:T(1,128)}, f32[8,1024]{1,0:T(8,128)}, bf16[2048,512]{1,0...) custom-call(bf16[1024,1024]{1,0:T(8,128)(2,1)} %get-tuple-element.55, ...), custom_call_target="tpu_custom_call" | custom-call | tf_op jit(solution)/shard_map/ffn_block/pallas_call | solution.py:565
  294.8 131.8 %mix_backward.1 = (bf16[2048,2048]{1,0:T(8,128)(2,1)}, f32[128,512]{1,0:T(8,128)}, f32[128,512]{1,0:T(8,128)}, f32[128,512]{1,0:T(8,128)}, f32[128,1408]{1,0:T(8...) custom-call(bf16[2048,2048]{1,0:T(8,128)(2,1)} %convolution_convert_fusion.q_ref.k_ref.v_ref.g_ref, ...), custom_call_target="tpu_custom_call" | custom-call | tf_op jit(solution)/shard_map/mix_backward/pallas_call | solution.py:368
  426.6 13.9 %convolution_convert_fusion.2 = bf16[2048,1024]{1,0:T(8,128)(2,1)} fusion(bf16[2048,2048]{1,0:T(8,128)(2,1)} %get-tuple-element.75, bf16[1024,2048]{1,0:T(8,128)(2,1)} %bitcast.77), kind=kOutput, calls=%fused_computation.20 | convolution fusion | flops 8592031744 | bytes 16777216 | tf_op jit(solution)/shard_map/dot_general | solution.py:32
  440.5 3.2 constant_dynamic-slice_fusion.1
  443.7 0.0 collective-permute-start
  443.7 0.5 fusion.2
  444.2 0.8 slice.71
  444.9 0.8 slice.72
  445.7 2.5 fusion.1
  448.3 0.2 concatenate.31
  448.5 0.5 broadcast.100
  449.0 0.7 reduce.6
  449.7 0.1 concatenate.33
  449.8 14.4 %convolution_convert_fusion.1 = bf16[1024,2048]{1,0:T(8,128)(2,1)} fusion(bf16[2048,1024]{1,0:T(8,128)(2,1)} %fusion.1, bf16[2048,2048]{1,0:T(8,128)(2,1)} %get-tuple-element.75), kind=kOutput, calls=%fused_computation.19 | convolution fusion | flops 8592031744 | bytes 16777216 | tf_op jit(solution)/shard_map/dot_general | solution.py:36
  464.2 0.0 collective-permute-done
  464.2 3.3 fusion.8
  467.5 0.1 concatenate.32
  467.6 0.1 maximum_bitcast_fusion
  467.7 0.1 fusion.10
  467.9 0.3 reshape.236
  468.2 0.8 copy.53.refs_1_
  469.0 57.7 %scatter_last.1 = (f32[128,512]{1,0:T(8,128)}, f32[128,512]{1,0:T(8,128)}, f32[128,512]{1,0:T(8,128)}, f32[128,512]{1,0:T(8,128)}, f32[40,128]{1,0:T(8,128)}) custom-call(bf16[8,128,2048]{2,1,0:T(8,128)(2,1)} %bitcast.58, f32[8,40,256]{2,1,0:T(8,128)} %copy.53.refs_1_), custom_call_target="tpu_custom_call" | custom-call | tf_op jit(solution)/shard_map/scatter_last/pallas_call | solution.py:948
  526.7 1.3 fusion.35
  528.0 1.3 slice_bitcast_fusion
  529.3 0.8 slice_reduce_fusion
  530.1 0.5 multiply_sqrt_fusion
  530.6 4.8 fusion.5
  535.5 1.3 copy.69
  536.8 0.7 copy.70
  537.5 0.7 copy.71
  538.2 0.7 copy.72
  538.9 0.7 copy.73
  539.6 0.7 copy.74
  540.3 0.9 copy.75
  541.2 0.9 copy.76
  542.1 0.9 copy.77
  (51 shorter events, 0.2 us)
Async XLA Ops:
  0.7 92.6 %copy-start.15 = (f32[16,4]{0,1:T(4,128)S(1)}, f32[16,4]{0,1:T(4,128)}, u32[]{:S(2)}) copy-start(f32[16,4]{0,1:T(4,128)} %param.35) | copy-start | bytes 772
  0.7 92.6 %copy-start.17 = (f32[16,4]{0,1:T(4,128)S(1)}, f32[16,4]{0,1:T(4,128)}, u32[]{:S(2)}) copy-start(f32[16,4]{0,1:T(4,128)} %param.34) | copy-start | bytes 772
  0.7 92.6 %copy-start.18 = (f32[16,4]{0,1:T(4,128)S(1)}, f32[16,4]{0,1:T(4,128)}, u32[]{:S(2)}) copy-start(f32[16,4]{0,1:T(4,128)} %param.33) | copy-start | bytes 772
  0.7 92.6 %copy-start.19 = (s32[32]{0:T(128)S(1)}, s32[32]{0:T(128)}, u32[]{:S(2)}) copy-start(s32[32]{0:T(128)} %param.37) | copy-start | bytes 388
  2.1 92.0 %copy-start.12 = (s32[2048]{0:T(1024)S(1)}, s32[2048]{0:T(1024)}, u32[]{:S(2)}) copy-start(s32[2048]{0:T(1024)} %param.36) | copy-start | bytes 24580
  96.6 3.5 copy-start.16
  440.4 3.2 copy-start
  440.5 5.3 copy-start.1
  443.7 20.5 %collective-permute-start = (bf16[1024,1024]{1,0:T(8,128)(2,1)}, bf16[1024,1024]{1,0:T(8,128)(2,1)}, u32[]{:S(2)}, u32[]{:S(2)}) collective-permute-start(bf16[1024,1024]{1,0:T(8,128)(2,1)} %constant_dynamic-slice_fusion.1), channel_id=1, source_target_pairs={{0,1},{1,0},{2,3},{3,2},{4,5},{5,4},{6,7},{7,6},{8,9},{9,8},{10,11... | collective-permute-start | bytes 6291464 | tf_op jit(solution)/shard_map/ppermute | solution.py:1036
  445.7 2.6 copy-start.13
  445.7 3.3 copy-start.14
  449.8 14.4 %copy-start.2 = (bf16[2048,1024]{1,0:T(8,128)(2,1)S(1)}, bf16[2048,1024]{1,0:T(8,128)(2,1)}, u32[]{:S(2)}) copy-start(bf16[2048,1024]{1,0:T(8,128)(2,1)} %convolution_convert_fusion.2) | copy-start | bytes 12582916
  530.6 4.9 copy-start.3
  535.4 1.4 copy-start.11
  535.4 2.1 copy-start.10
  535.4 2.8 copy-start.9
  535.4 3.5 copy-start.8
  535.4 4.2 copy-start.7
  535.4 4.9 copy-start.6
  535.5 5.7 %copy-start.5 = (f32[128,1408]{1,0:T(8,128)S(1)}, f32[128,1408]{1,0:T(8,128)}, u32[]{:S(2)}) copy-start(f32[128,1408]{1,0:T(8,128)} %get-tuple-element.129) | copy-start | bytes 2162692
  535.5 6.6 %copy-start.4 = (f32[352,512]{1,0:T(8,128)S(1)}, f32[352,512]{1,0:T(8,128)}, u32[]{:S(2)}) copy-start(f32[352,512]{1,0:T(8,128)} %get-tuple-element.130) | copy-start | bytes 2162692

commit v3 on v2

--- a/solution.py
+++ b/solution.py
@@ -109,7 +109,9 @@
     tile = pl.program_id(0)
     core = lax.axis_index("col")
     blocks, wholes = (b0, b1, b2, b3), (w0, w1, w2, w3)
-    items = [(blk, ref, core * blk.shape[1], True) for blk, ref in zip(blocks, wholes)]
+    planes = (None, 0, 1, None)
+    items = [(blk, ref, core * blk.shape[1], True, plane)
+             for blk, ref, plane in zip(blocks, wholes, planes)]
     g = Gather(n, items, sems)
     each = range(len(items))
     width = heads * HD
@@ -128,7 +130,7 @@
 
     @pl.when(tile == 0)
     def clear():
-        greet(n, g.right, g.left, True, False)
+        greet(n, g.right, g.left, True, True)
         g.begin(each)
         mem[...] = jnp.zeros_like(mem)
         mom[...] = jnp.zeros_like(mom)
@@ -192,7 +194,7 @@
             pl.BlockSpec((TILE, 1), lambda t: (t, 0)),
             pl.BlockSpec((1, SEG), lambda t: (0, t // TPS)),
             pl.BlockSpec(memory_space=pltpu.SMEM),
-        ] + [any_spec] * 4,
+        ] + [whole(b.shape) for b in blocks],
         out_specs=[
             pl.BlockSpec((TILE, HD), lambda t: (t, 0)),
             pl.BlockSpec((TILE, width), lambda t: (t, 0)),
@@ -307,12 +309,12 @@
     dout_ref, dpk_ref, dpv_ref = refs[8:11]
     outs = refs[11:15]
     dmem, dmom, dk_acc, dv_acc = refs[15:19]
-    scratch = refs[19:39]
-    sems = refs[39:]
+    scratch = refs[19:31]
+    sems = refs[31:]
     turn = pl.program_id(0)
     tile = tiles - 1 - turn
     items = [
-        (own_refs[m], 0, outs[m].shape[1], sib_refs[m]) + tuple(scratch[5 * m:5 * m + 5]) + (outs[m],)
+        (own_refs[m], 0, outs[m].shape[1], sib_refs[m]) + tuple(scratch[3 * m:3 * m + 3]) + (outs[m], None, None)
         for m in range(4)
     ]
     g = Scatter(n, items, sems)
@@ -328,7 +330,7 @@
 
     @pl.when(turn == 0)
     def clear():
-        greet(n, g.right, g.left, False, True)
+        greet(n, g.right, g.left, False, False)
         g.begin(order)
         dmem[...] = jnp.zeros_like(dmem)
         dmom[...] = jnp.zeros_like(dmom)
@@ -354,7 +356,7 @@
         for m in order:
             g.settle(m)
         for m in order:
-            g.finish(m)
+            g.drain(m)
 
 
 def mix_backward(n, qkvg, dcomb, pkey, pvalue, segc, segr, coef, lse, reads, m0, err, heads, owns, sibs):
@@ -393,13 +395,13 @@
             jax.ShapeDtypeStruct((total, 4 * width), BF),
             jax.ShapeDtypeStruct((HD, width), F32),
             jax.ShapeDtypeStruct((HD, width), F32),
-        ] + [jax.ShapeDtypeStruct((a.shape[1], w), F32) for a, w, share in arrays],
+        ] + [jax.ShapeDtypeStruct((a.shape[1], w), BF) for a, w, share in arrays],
         scratch_shapes=[
             pltpu.VMEM((heads, HD, HD), F32),
             pltpu.VMEM((heads, HD, HD), F32),
             pltpu.VMEM((SEG, width), F32),
             pltpu.VMEM((SEG, width), F32),
-        ] + scatter_plan(arrays) + scatter_sems(n, 4),
+        ] + scatter_plan(arrays, False) + scatter_sems(n, 4),
         compiler_params=pltpu.CompilerParams(
             collective_id=4, has_side_effects=True, vmem_limit_bytes=VMEM_MAX),
         name="mix_backward",
@@ -658,29 +660,34 @@
     def __init__(self, n, items, sems):
         self.n = n
         self.items = items
-        self.send, self.recv, self.local, self.csend, self.crecv = sems
+        self.send, self.recv, self.local, self.csend, self.crecv, self.xsend = sems
         self.me, self.right, self.left = neighbours(n)
         self.row = lax.axis_index("row")
         self.other = 1 - lax.axis_index("col")
+        self.plane = lax.axis_index("dp")
 
     def ways(self, m):
         return range(len(split_cols(self.items[m][0].shape[1], m % 2)))
 
     def hop(self, m, d, s):
-        block, whole_ref, base, share = self.items[m]
+        block, whole_ref, base = self.items[m][:3]
         place = mod(self.me - s, self.n) if d == 0 else mod(self.me + s, self.n)
         owner = ring_row(place, self.n)
         start, size = split_cols(block.shape[1], m % 2)[d]
-        spot = whole_ref.at[owner, :, pl.ds(base + start, size)]
-        return owner, start, size, spot
+        return start, size, whole_ref.at[owner, :, pl.ds(base + start, size)]
 
     def ring(self, m, d, s, first=False):
-        block = self.items[m][0]
-        owner, start, size, spot = self.hop(m, d, s)
-        source = block.at[:, pl.ds(start, size)] if first else spot
+        start, size, spot = self.hop(m, d, s)
+        source = self.items[m][0].at[:, pl.ds(start, size)] if first else spot
         return pltpu.make_async_remote_copy(
             src_ref=source, dst_ref=spot, send_sem=self.send.at[m, d, s], recv_sem=self.recv.at[m, d, s],
             device_id={"row": self.right if d == 0 else self.left}, device_id_type=MESH)
+
+    def over(self, m, d, s):
+        spot = self.hop(m, d, s + 1)[2]
+        return pltpu.make_async_remote_copy(
+            src_ref=spot, dst_ref=spot, send_sem=self.xsend.at[m, d, s], recv_sem=self.recv.at[m, d, s],
+            device_id={"dp": 1 - self.plane}, device_id_type=MESH)
 
     def across(self, m, source, spot):
         return pltpu.make_async_remote_copy(
@@ -688,35 +695,67 @@
             device_id={"col": self.other}, device_id_type=MESH)
 
     def keep(self, m):
-        block, whole_ref, base, share = self.items[m]
+        block, whole_ref, base = self.items[m][:3]
         return pltpu.make_async_copy(
             block, whole_ref.at[self.row, :, pl.ds(base, block.shape[1])], self.local.at[m])
 
+    def when(self, m, inside, action):
+        plane = self.items[m][4]
+        if plane is None:
+            if inside:
+                action()
+        else:
+            pl.when((self.plane == plane) if inside else (self.plane != plane))(action)
+
     def begin(self, ms):
         for m in ms:
-            for d in self.ways(m):
-                self.ring(m, d, 0, first=True).start()
+            def launch(m=m):
+                for d in self.ways(m):
+                    self.ring(m, d, 0, first=True).start()
+
+            self.when(m, True, launch)
         for m in ms:
-            block, whole_ref, base, share = self.items[m]
+            block, whole_ref, base, share = self.items[m][:4]
             self.keep(m).start()
             if share:
                 self.across(m, block, whole_ref.at[self.row, :, pl.ds(base, block.shape[1])]).start()
 
+    def hand(self, m, d, s):
+        if self.items[m][3]:
+            spot = self.hop(m, d, s + 1)[2]
+            self.across(m, spot, spot).start()
+
+    def arrive(self, m, s):
+        for d in self.ways(m):
+            self.over(m, d, s).wait_recv()
+            self.hand(m, d, s)
+
     def advance(self, m, s):
-        for d in self.ways(m):
-            self.ring(m, d, s).wait_recv()
-
-            @pl.when(s < self.n - 2)
-            def on():
-                self.ring(m, d, s + 1).start()
-
-            if self.items[m][3]:
-                spot = self.hop(m, d, s + 1)[3]
-                self.across(m, spot, spot).start()
+        def inside():
+            for d in self.ways(m):
+                self.ring(m, d, s).wait_recv()
+
+                @pl.when(s < self.n - 2)
+                def on():
+                    self.ring(m, d, s + 1).start()
+
+                if self.items[m][4] is not None:
+                    self.over(m, d, s).start()
+                self.hand(m, d, s)
+
+        def outside():
+            @pl.when(s > 0)
+            def late():
+                self.arrive(m, s - 1)
+
+        self.when(m, True, inside)
+        self.when(m, False, outside)
 
     def finish(self, ms):
         for m in ms:
-            block, whole_ref, base, share = self.items[m]
+            self.when(m, False, functools.partial(self.arrive, m, self.n - 2))
+        for m in ms:
+            block, whole_ref, base, share, plane = self.items[m]
             self.keep(m).wait()
             if share:
                 spot = whole_ref.at[:, :, pl.ds(base, block.shape[1])]
@@ -724,33 +763,33 @@
                 self.across(m, spot, theirs).wait_recv()
                 self.across(m, spot, theirs).wait_send()
 
-            def sent(s, carry):
-                for d in self.ways(m):
-                    self.ring(m, d, s).wait_send()
-                return carry
-
-            lax.fori_loop(0, self.n - 1, sent, 0)
+            def drain(m=m, plane=plane):
+                def sent(s, carry):
+                    for d in self.ways(m):
+                        self.ring(m, d, s).wait_send()
+                        if plane is not None:
+                            self.over(m, d, s).wait_send()
+                    return carry
+
+                lax.fori_loop(0, self.n - 1, sent, 0)
+
+            self.when(m, True, drain)
 
 
 def gather_sems(n, count):
-    return [
-        pltpu.SemaphoreType.DMA((count, 2, n - 1)),
-        pltpu.SemaphoreType.DMA((count, 2, n - 1)),
-        pltpu.SemaphoreType.DMA((count,)),
-        pltpu.SemaphoreType.DMA((count,)),
-        pltpu.SemaphoreType.DMA((count,)),
-    ]
+    dma = pltpu.SemaphoreType.DMA
+    return [dma((count, 2, n - 1))] * 2 + [dma((count,))] * 3 + [dma((count, 2, n - 1))]
 
 
 def gather_kernel(n, *refs):
     blocks = refs[:5]
     x_ref = refs[5]
     wide, small, pair = refs[6:9]
-    sems = refs[9:14]
-    xsems = refs[14]
+    sems = refs[9:15]
+    xsems = refs[15]
     core = lax.axis_index("col")
-    items = [(blocks[m], wide, m * blocks[m].shape[1], False) for m in range(4)]
-    items.append((blocks[4], small, core * blocks[4].shape[1], True))
+    items = [(blocks[m], wide, m * blocks[m].shape[1], False, None) for m in range(4)]
+    items.append((blocks[4], small, core * blocks[4].shape[1], True, None))
     g = Gather(n, items, sems)
     greet(n, g.right, g.left, True, False)
     g.begin(range(5))
@@ -775,14 +814,16 @@
 def gather_first(n, blocks, small, x):
     rows, width = blocks[0].shape
     any_spec = pl.BlockSpec(memory_space=pl.ANY)
+    vmem_spec = pl.BlockSpec(memory_space=pltpu.VMEM)
     shapes = [(n, rows, 4 * width), (n, small.shape[0], 2 * small.shape[1]), (2,) + x.shape]
     return pl.pallas_call(
         functools.partial(gather_kernel, n),
-        in_specs=[any_spec] * 6,
+        in_specs=[vmem_spec] * 6,
         out_specs=[any_spec] * 3,
         out_shape=[jax.ShapeDtypeStruct(shape, BF) for shape in shapes],
         scratch_shapes=gather_sems(n, 5) + [pltpu.SemaphoreType.DMA((3,))],
-        compiler_params=pltpu.CompilerParams(collective_id=1, has_side_effects=True),
+        compiler_params=pltpu.CompilerParams(
+            collective_id=1, has_side_effects=True, vmem_limit_bytes=VMEM_MAX),
         name="gather_first",
     )(*blocks, small, x)
 
@@ -862,14 +903,17 @@
             self.ring(m, d, self.n - 2).wait_recv()
             owner, cols, value = self.total(m, d, self.n - 1, True)
             self.items[m][7][:, cols] = value
-        self.swap(m).start()
+        if self.items[m][8] is not None:
+            self.swap(m).start()
 
     def finish(self, m):
         low, twin, out = self.items[m][7:10]
         self.swap(m).wait_recv()
         out[...] = low[...].astype(F32) + twin[...].astype(F32)
         self.swap(m).wait_send()
-
+        self.drain(m)
+
+    def drain(self, m):
         def sent(s, carry):
             for d in self.ways(m):
                 self.ring(m, d, s).wait_send()
@@ -885,7 +929,7 @@
     ] + [pltpu.SemaphoreType.DMA((count,))] * 4
 
 
-def scatter_plan(arrays):
+def scatter_plan(arrays, swap=True):
     scratch = []
     for array, width, share in arrays:
         n, rows, full = array.shape
@@ -893,70 +937,168 @@
         scratch.append(pltpu.VMEM((n, rows, width), kind))
         scratch.append(pltpu.VMEM((n, rows, width) if share else (1, 16, HD), kind))
         scratch.append(pltpu.VMEM((n - 1, rows, width), kind))
-        scratch.append(pltpu.VMEM((rows, width), kind))
-        scratch.append(pltpu.VMEM((rows, width), kind))
+        if swap:
+            scratch.append(pltpu.VMEM((rows, width), kind))
+            scratch.append(pltpu.VMEM((rows, width), kind))
     return scratch
 
 
-def scatter_kernel(n, count, *refs):
-    wide, small = refs[:2]
-    outs = refs[2:2 + count]
-    scratch = refs[2 + count:2 + 6 * count]
-    small_sib, small_sems = refs[2 + 6 * count:4 + 6 * count]
-    sems = refs[4 + 6 * count:]
+def post_kernel(n, normed_ref, d_ref, w_ref, x_ref, dmid_ref, gain_ref, small, *refs):
+    late = refs[:4]
+    own_w = refs[4:8]
+    gin_ref = refs[8]
+    outs = refs[9:14]
+    late_outs = refs[14:18]
+    dgain_ref = refs[18]
+    turned, back, leave, came, dg_own, dg_sib, small_sib = refs[19:26]
+    late_in = refs[26:30]
+    scratch = refs[30:55]
+    side, late_send, late_recv = refs[55:58]
+    sems = refs[58:]
+    turn = pl.program_id(0)
     core = lax.axis_index("col")
+    other = 1 - core
+    rows_all, dim = x_ref.shape
+    width = outs[0].shape[1]
+    block = outs[0].shape[0]
     items = []
-    for m in range(count):
-        width = outs[m].shape[1]
-        ref, base, other = (wide, m * width, None) if m < 4 else (small, core * width, small_sib)
-        items.append((ref, base, width, other) + tuple(scratch[5 * m:5 * m + 5]) + (outs[m],))
+    for m in range(5):
+        first, sib = (0, None) if m < 4 else (core * HD, small_sib)
+        items.append((None if m < 4 else small, first, outs[m].shape[1], sib)
+                     + tuple(scratch[5 * m:5 * m + 5]) + (outs[m],))
     g = Scatter(n, items, sems)
-    greet(n, g.right, g.left, True, True)
-    width = outs[4].shape[1]
-    cross = pltpu.make_async_remote_copy(
-        src_ref=small.at[:, :, pl.ds((1 - core) * width, width)], dst_ref=small_sib,
-        send_sem=small_sems.at[0], recv_sem=small_sems.at[1],
-        device_id={"col": 1 - core}, device_id_type=MESH)
-    cross.start()
-    order = range(4)
-    g.begin(order)
-    for m in order:
-        g.ready(m)
-        g.start(m)
-    cross.wait()
-    g.begin((4,))
-    g.ready(4)
-    g.start(4)
-
-    def step(s, carry):
-        for m in range(count):
-            g.advance(m, s)
-        return carry
-
-    lax.fori_loop(1, n - 1, step, 0)
-    for m in range(count):
-        g.settle(m)
-    for m in range(count):
-        g.finish(m)
-
-
-def scatter_last(n, wide, small):
-    width = wide.shape[2] // 4
-    arrays = [(wide, width, False)] * 4 + [(small, HD, True)]
-    count = len(arrays)
+    steps = 2 * rows_all // TILE
+
+    def push(src, dst, at):
+        return pltpu.make_async_remote_copy(
+            src_ref=src, dst_ref=dst, send_sem=side.at[2 * at], recv_sem=side.at[2 * at + 1],
+            device_id={"col": other}, device_id_type=MESH)
+
+    def late_swap(i):
+        return pltpu.make_async_remote_copy(
+            src_ref=late[i], dst_ref=late_in[i], send_sem=late_send.at[i], recv_sem=late_recv.at[i],
+            device_id={"dp": g.twin}, device_id_type=MESH)
+
+    cross = push(small.at[:, :, pl.ds(other * HD, HD)], small_sib, 0)
+    swap_back = push(leave, came, 1)
+    swap_gain = push(dg_own, dg_sib, 2)
+
+    @pl.when(turn == 0)
+    def first_turn():
+        greet(n, g.right, g.left, True, True)
+        cross.start()
+        for i in range(4):
+            late_swap(i).start()
+        for i in range(steps):
+            rows = slice(i * TILE, (i + 1) * TILE)
+            turned[:, rows] = normed_ref[rows, :].T
+            back[rows, :] = jnp.zeros((TILE, dim), F32)
+
+    for m in range(4):
+        @pl.when(turn == m)
+        def this():
+            grad = nn(turned[...], d_ref[...]).astype(BF)
+            for q in range(n):
+                items[m][4][q] = grad[q * block:(q + 1) * block]
+            g.start(m)
+            if m == 0:
+                cross.wait()
+                g.begin((4,))
+                g.ready(4)
+                g.start(4)
+            for i in range(steps):
+                rows = slice(i * TILE, (i + 1) * TILE)
+                back[rows, :] += nt(d_ref[rows, :], w_ref[...])
+
+    @pl.when(turn == 3)
+    def rest():
+        def step(low, high):
+            def one(s, carry):
+                for m in range(5):
+                    g.advance(m, s)
+                return carry
+
+            lax.fori_loop(low, high, one, 0)
+
+        hops = n - 2
+        theirs = pl.multiple_of(other * rows_all, TILE)
+        for i in range(rows_all // TILE):
+            rows = slice(i * TILE, (i + 1) * TILE)
+            leave[rows, :] = back[pl.ds(theirs + i * TILE, TILE), :].astype(BF)
+        swap_back.start()
+        step(1, 1 + hop_bound(1, 3, hops))
+        swap_back.wait()
+        mine = pl.multiple_of(core * rows_all, TILE)
+        gain = gain_ref[...]
+        for i in range(rows_all // TILE):
+            rows = slice(i * TILE, (i + 1) * TILE)
+            xf = x_ref[rows, :].astype(F32)
+            inv = lax.rsqrt(jnp.mean(xf * xf, axis=1, keepdims=True) + EPS)
+            weighted = (back[pl.ds(mine + i * TILE, TILE), :] + came[rows, :].astype(F32)) * gain
+            inner = jnp.mean(weighted * xf, axis=1, keepdims=True)
+            value = dmid_ref[rows, :].astype(F32) + weighted * inv - xf * (inv * inv * inv) * inner
+            gin_ref[rows, :] = value.astype(BF)
+            if i == 1:
+                step(1 + hop_bound(1, 3, hops), 1 + hop_bound(2, 3, hops))
+        step(1 + hop_bound(2, 3, hops), 1 + hops)
+        for m in range(5):
+            g.settle(m)
+        for i in range(4):
+            late_swap(i).wait()
+            late_outs[i][...] = late[i][...].astype(F32) + late_in[i][...].astype(F32)
+        total = jnp.zeros((block, 1), F32)
+        for m in range(4):
+            g.finish(m)
+            total = total + jnp.sum(outs[m][...] * own_w[m][...].astype(F32), axis=1, keepdims=True)
+        dg_own[...] = jnp.broadcast_to(total, (block, HD))
+        swap_gain.start()
+        g.finish(4)
+        swap_gain.wait()
+        dgain_ref[...] = dg_own[...] + dg_sib[...]
+
+
+def post(n, normed, dqkvg, wide, x, dmid, gain, small, late, own_w):
+    total, dim = normed.shape
+    width = wide.shape[1] // 4
+    rows = x.shape[0]
+    block = dim // n
+    arrays = [(jax.ShapeDtypeStruct((n, block, width), BF), width, False)] * 4 + [(small, HD, True)]
     any_spec = pl.BlockSpec(memory_space=pl.ANY)
+    dma = pltpu.SemaphoreType.DMA
+    outs = [((a.shape[1], w), F32) for a, w, share in arrays]
+    late_outs = [(a.shape, F32) for a in late]
+    shapes = [((rows, dim), BF)] + outs + late_outs + [((block, HD), F32)]
     return pl.pallas_call(
-        functools.partial(scatter_kernel, n, count),
-        in_specs=[any_spec] * 2,
-        out_specs=[pl.BlockSpec(memory_space=pltpu.VMEM)] * count,
-        out_shape=[jax.ShapeDtypeStruct((a.shape[1], w), F32) for a, w, share in arrays],
-        scratch_shapes=scatter_plan(arrays)
-        + [pltpu.VMEM((n, small.shape[1], HD), F32), pltpu.SemaphoreType.DMA((2,))]
-        + scatter_sems(n, count),
+        functools.partial(post_kernel, n),
+        grid=(4,),
+        in_specs=[
+            whole((total, dim)),
+            pl.BlockSpec((total, width), lambda t: (0, t)),
+            pl.BlockSpec((dim, width), lambda t: (0, t)),
+            whole((rows, dim)),
+            whole((rows, dim)),
+            whole((1, dim)),
+            any_spec,
+        ] + [whole(a.shape) for a in late] + [whole(a.shape) for a in own_w],
+        out_specs=[whole(shape) for shape, kind in shapes],
+        out_shape=[jax.ShapeDtypeStruct(shape, kind) for shape, kind in shapes],
+        scratch_shapes=[
+            pltpu.VMEM((dim, total), BF),
+            pltpu.VMEM((total, dim), F32),
+            pltpu.VMEM((rows, dim), BF),
+            pltpu.VMEM((rows, dim), BF),
+            pltpu.VMEM((block, HD), F32),
+            pltpu.VMEM((block, HD), F32),
+            pltpu.VMEM((n, small.shape[1], HD), F32),
+        ]
+        + [pltpu.VMEM(a.shape, BF) for a in late]
+        + scatter_plan(arrays)
+        + [dma((6,)), dma((4,)), dma((4,))]
+        + scatter_sems(n, 5),
         compiler_params=pltpu.CompilerParams(
             collective_id=2, has_side_effects=True, vmem_limit_bytes=VMEM_MAX),
-        name="scatter_last",
-    )(wide, small)
+        name="post",
+    )(normed, dqkvg, wide, x, dmid, gain, small, *late, *own_w)
 
 
 def local(
@@ -1029,30 +1171,20 @@
         n, qkvg, dcomb, pkey, pvalue, segc, segr, coef, lse, reads, m0, err, heads,
         parts[0::2], parts[1::2])
 
-    g_wide = tn(normed, dqkvg).astype(BF)
-    back = nt(dqkvg, wide).astype(BF)
-    mine = lax.dynamic_slice_in_dim(back, core * local_tok, local_tok, 0)
-    theirs = lax.dynamic_slice_in_dim(back, (1 - core) * local_tok, local_tok, 0)
-    theirs = lax.ppermute(theirs, "col", [(0, 1), (1, 0)])
-    dnorm = mine.astype(F32) + theirs.astype(F32)
-    xf = tokens_in.astype(F32)
-    inv = lax.rsqrt(jnp.mean(xf * xf, axis=-1, keepdims=True) + EPS)
-    weighted = dnorm * gain_a
-    inner = jnp.mean(weighted * xf, axis=-1, keepdims=True)
-    grad_in = (dmid.astype(F32) + weighted * inv - xf * (inv * inv * inv) * inner).astype(BF)
-    dgain_a = jnp.sum(dnorm * xf * inv, axis=0)
-
     place = jnp.zeros((2 * P_SIZE, dim), F32)
     place = lax.dynamic_update_slice_in_dim(
         place, jnp.concatenate([dpk[:P_SIZE], dpv[:P_SIZE]], axis=0), core * width, 1)
-    packed = jnp.concatenate([place, dgain_a[None, :], dgain_f], axis=0)
+    packed = jnp.concatenate([place, jnp.zeros((1, dim), F32), dgain_f], axis=0)
     packed = packed.reshape(2 * P_SIZE + 2, n, 2, piece).transpose(1, 0, 2, 3)
     packed = jnp.pad(packed, ((0, 0), (0, 0), (0, 0), (0, HD - piece)))
     stats = jnp.sum(sums.reshape(8, dim // HD, HD), axis=1)[:6]
     stats = jnp.broadcast_to(stats[None, :, None, :], (n, 6, 2, HD))
     packed = jnp.concatenate([packed, stats], axis=1).reshape(n, 2 * P_SIZE + 8, 2 * HD)
-    *grads, part = scatter_last(n, g_wide.reshape(n, dim // n, 4 * width), packed)
-    grads = grads + grads_late
+    grad_in, *rest = post(
+        n, normed, dqkvg, wide, tokens_in, dmid, gain_a, packed, grads_late,
+        (w_query, w_key, w_value, w_gate))
+    grads, part, dgain_a = rest[:4] + rest[5:9], rest[4], rest[9]
+    dgain_a = lax.dynamic_slice_in_dim(dgain_a[:, 0], core * piece, piece, 0) / gain_attn.astype(F32)
     entry_count = local_tok * dim * lax.axis_size("dp") * n * lax.axis_size("col")
     rms_stats = jnp.sqrt(jnp.sum(part[2 * P_SIZE + 2:2 * P_SIZE + 5], axis=1) / entry_count)
     part = part[:, :piece]
@@ -1067,7 +1199,7 @@
         grads[5],
         grads[6],
         grads[7],
-        part[2 * P_SIZE],
+        dgain_a,
         part[2 * P_SIZE + 1],
         part[:P_SIZE],
         part[P_SIZE:2 * P_SIZE],

time: 548 us -> 476 us (0.87)
  Pallas kernels: 458 us -> 423 us
  matrix products: 39.3 us -> 11 us
  other arithmetic: 21.7 us -> 12.8 us
    dot_general x2 -> x0, matrix products: 28.3 us -> none  [the longest x1 14.4 us: tn(): lax.dot_general(a, b, (((0,), (0,)), ((), ())), preferred_element_type=F32)]
    pallas_call x1, Pallas kernels: 101 us -> 87.1 us  [mix_forward(): pl.pallas_call(functools.partial(mix_forward_kernel, heads, n, tiles), gr...]
    pallas_call x2, Pallas kernels: 143 us -> 130 us  [the longest x1 79 us: post(): pl.pallas_call(functools.partial(post_kernel, n), grid=(4,), in_specs=[wh...]
    pallas_call x1, Pallas kernels: 132 us -> 123 us  [mix_backward(): pl.pallas_call(functools.partial(mix_backward_kernel, heads, n, tiles), g...]
  transfers between devices with their start and end apart: 1 -> 0, of which waited for: 0 -> 0; matrix products, arithmetic and copies ran while one was open for 4% -> 0% of each run, Pallas kernels for 0% -> 0%
where the time goes in v3:
time: 476 us; the launch traced here: 471 us
  Pallas kernels  423 us (89%)
  local copies, waits for them, and re-layouts  22.8 us (5%)
  other arithmetic  12.8 us (3%)
  matrix products  11 us (2%)
    pallas_call x1, Pallas kernels, mix_backward(): pl.pallas_call(functools.partial(mix_backward_kernel, heads, n, tiles), g...  123 us
    pallas_call x1, Pallas kernels, mix_forward(): pl.pallas_call(functools.partial(mix_forward_kernel, heads, n, tiles), gr...  87.1 us
    pallas_call x1, Pallas kernels, ffn_block(): pl.pallas_call(functools.partial(ffn_kernel, tiles), grid=(tiles,), in_sp...  82.4 us
    pallas_call x1, Pallas kernels, post(): pl.pallas_call(functools.partial(post_kernel, n), grid=(4,), in_specs=[wh...  79 us
    pallas_call x1, Pallas kernels, gather_first(): pl.pallas_call(functools.partial(gather_kernel, n), in_specs=[vmem_spec]...  51.3 us
    dot_general x1, matrix products, nn(): lax.dot_general(a, b, (((1,), (0,)), ((), ())), preferred_element_type=F32)  10.9 us
    unnamed x51, local copies, waits for them, and re-layouts  10.1 us

profile of v3, /device:TPU:0, one launch (start us, length us, event | category | flops | bytes accessed | tf_op | source)
XLA Modules:
  0.0 470.8 jit_solution(8345710496291916224)
XLA Ops:
  0.6 1.3 fusion.13.refs_4_
  2.0 51.3 %gather_first.1 = (bf16[8,128,2048]{2,1,0:T(8,128)(2,1)}, bf16[8,48,256]{2,1,0:T(8,128)(2,1)}, bf16[2,1024,1024]{2,1,0:T(8,128)(2,1)}) custom-call(bf16[128,512]{1,0:T(8,128)(2,1)} %refs_4_.1, bf16[128,512]{1,0:T(8,128)(2,1)} %refs_5_.3, bf16[128,512]{1,0:T(8,128)(2,1)} %refs_6_.1, bf16[128,512]{1,0:T(8,128)(2,1)} %refs_7_.1, ...), custom_call_target="tpu_custom_call" | custom-call | tf_op jit(solution)/shard_map/gather_first/pallas_call | solution.py:819
  53.3 1.0 reshape.199
  54.3 0.1 copy_bitcast_fusion
  54.5 0.1 reshape.218
  54.6 3.2 multiply_reduce_fusion
  57.8 0.2 copy-done
  58.0 1.1 multiply_convert_fusion
  59.1 1.1 copy-done.1
  60.2 0.0 copy-start.12
  60.2 10.9 %convolution_convert_fusion.q_ref.k_ref.v_ref.g_ref = bf16[2048,2048]{1,0:T(8,128)(2,1)} fusion(bf16[2048,1024]{1,0:T(8,128)(2,1)S(1)} %bitcast.52, bf16[1024,2048]{1,0:T(8,128)(2,1)S(1)} %bitcast.54), kind=kOutput, calls=%fused_computation.5 | convolution fusion | flops 8594128896 | bytes 16777216 | tf_op jit(solution)/shard_map/dot_general | solution.py:28
  71.1 0.2 reshape.201
  71.3 0.7 pad.16.pk_ref
  72.0 0.7 pad.17.pv_ref
  72.6 0.2 fusion.8
  72.8 0.1 copy.46
  72.9 0.1 stack.12
  73.1 0.1 copy.47
  73.1 0.1 stack.13
  73.3 0.1 copy.48
  73.3 0.1 stack.14
  73.4 0.0 copy-done.12
  73.5 0.1 reshape.202
  73.5 0.2 fusion.9
  73.7 0.1 fusion.23
  73.8 0.1 stack_broadcast_in_dim.13
  73.9 0.1 stack_broadcast_in_dim.14
  74.0 0.6 pad_maximum_fusion.1.coef_ref
  74.6 1.3 copy.49.segc_ref
  75.9 87.1 %mix_forward.1 = (f32[2048,128]{1,0:T(8,128)}, bf16[2048,512]{1,0:T(8,128)(2,1)}, bf16[32,4,128,128]{3,2,1,0:T(8,128)(2,1)}, bf16[2048,512]{1,0:T(8,128)(2,1)}, ...) custom-call(bf16[2048,2048]{1,0:T(8,128)(2,1)} %convolution_convert_, ...), custom_call_target="tpu_custom_call" | custom-call | tf_op jit(solution)/shard_map/mix_forward/pallas_call | solution.py:184
  163.1 0.7 reshape.220.gain_ref
  163.7 82.4 %ffn_block.1 = (bf16[1024,1024]{1,0:T(8,128)(2,1)}, bf16[1024,1024]{1,0:T(8,128)(2,1)}, f32[1,1024]{1,0:T(1,128)}, f32[8,1024]{1,0:T(8,128)}, bf16[2048,512]{1,0...) custom-call(bf16[1024,1024]{1,0:T(8,128)(2,1)} %get-tuple-element.61, ...), custom_call_target="tpu_custom_call" | custom-call | tf_op jit(solution)/shard_map/ffn_block/pallas_call | solution.py:567
  246.2 123.3 %mix_backward.1 = (bf16[2048,2048]{1,0:T(8,128)(2,1)}, f32[128,512]{1,0:T(8,128)}, f32[128,512]{1,0:T(8,128)}, bf16[128,512]{1,0:T(8,128)(2,1)}, bf16[128,1408]{...) custom-call(bf16[2048,2048]{1,0:T(8,128)(2,1)} %convolution_convert_fusion.q_ref.k_ref.v_ref.g_ref, ...), custom_call_target="tpu_custom_call" | custom-call | tf_op jit(solution)/shard_map/mix_backward/pallas_call | solution.py:370
  369.5 0.8 slice.70
  370.2 0.8 slice.71
  371.0 0.1 pad.22.clone
  371.1 0.1 pad_maximum_fusion
  371.2 0.2 reshape.215
  371.4 0.1 fusion.2
  371.6 0.3 reshape.223
  371.9 0.8 copy.52.small
  372.7 4.1 fusion.1.normed_ref
  376.8 0.7 reshape.222.gain_ref
  377.5 79.0 %post.1 = (bf16[1024,1024]{1,0:T(8,128)(2,1)}, f32[128,512]{1,0:T(8,128)}, f32[128,512]{1,0:T(8,128)}, f32[128,512]{1,0:T(8,128)}, f32[128,512]{1,0:T(8,128)}, /...) custom-call(bf16[2048,1024]{1,0:T(8,128)(2,1)} %fusion.1.normed_ref,, ...), custom_call_target="tpu_custom_call" | custom-call | tf_op jit(solution)/shard_map/post/pallas_call | solution.py:1071
  456.5 1.3 fusion.27
  457.8 1.0 dynamic-slice_reduce_fusion
  458.8 0.0 copy-done.16
  458.8 0.5 convert_divide_fusion
  459.3 0.8 slice_reduce_fusion
  460.1 0.5 multiply_sqrt_fusion
  460.7 1.2 slice_bitcast_fusion
  461.9 0.0 copy-done.2
  461.9 1.3 copy.69
  463.2 1.3 copy.70
  464.5 0.7 copy.71
  465.2 0.7 copy.72
  466.0 0.7 copy.73
  466.7 0.0 copy-done.8
  466.7 0.7 copy.74
  467.4 0.7 copy.75
  468.1 0.0 copy-done.6
  468.1 0.9 copy.76
  468.9 0.9 copy.77
  469.8 0.9 copy.78
  (42 shorter events, 0.2 us)
Async XLA Ops:
  54.6 3.4 copy-start
  58.0 2.2 copy-start.1
  60.2 12.4 %copy-start.15 = (f32[16,4]{0,1:T(4,128)S(1)}, f32[16,4]{0,1:T(4,128)}, u32[]{:S(2)}) copy-start(f32[16,4]{0,1:T(4,128)} %param.35) | copy-start | bytes 772
  60.2 12.4 %copy-start.17 = (f32[16,4]{0,1:T(4,128)S(1)}, f32[16,4]{0,1:T(4,128)}, u32[]{:S(2)}) copy-start(f32[16,4]{0,1:T(4,128)} %param.34) | copy-start | bytes 772
  60.2 12.4 %copy-start.18 = (f32[16,4]{0,1:T(4,128)S(1)}, f32[16,4]{0,1:T(4,128)}, u32[]{:S(2)}) copy-start(f32[16,4]{0,1:T(4,128)} %param.33) | copy-start | bytes 772
  60.2 12.4 %copy-start.19 = (s32[32]{0:T(128)S(1)}, s32[32]{0:T(128)}, u32[]{:S(2)}) copy-start(s32[32]{0:T(128)} %param.37) | copy-start | bytes 388
  60.2 13.2 %copy-start.12 = (s32[2048]{0:T(1024)S(1)}, s32[2048]{0:T(1024)}, u32[]{:S(2)}) copy-start(s32[2048]{0:T(1024)} %param.36) | copy-start | bytes 24580
  246.1 124.9 %copy-start.14 = (f32[1,1024]{1,0:T(1,128)S(1)}, f32[1,1024]{1,0:T(1,128)}, u32[]{:S(2)}) copy-start(f32[1,1024]{1,0:T(1,128)} %get-tuple-element.84) | copy-start | bytes 12292
  246.1 125.2 %copy-start.13 = (f32[8,1024]{1,0:T(8,128)S(1)}, f32[8,1024]{1,0:T(8,128)}, u32[]{:S(2)}) copy-start(f32[8,1024]{1,0:T(8,128)} %get-tuple-element.85) | copy-start | bytes 98308
  377.5 81.3 %copy-start.16 = (bf16[64]{0:T(256)(128)(2,1)S(1)}, bf16[64]{0:T(256)(128)(2,1)}, u32[]{:S(2)}) copy-start(bf16[64]{0:T(256)(128)(2,1)} %param.21) | copy-start | bytes 388
  377.5 84.4 %copy-start.2 = (bf16[1024,1024]{1,0:T(8,128)(2,1)S(1)}, bf16[1024,1024]{1,0:T(8,128)(2,1)}, u32[]{:S(2)}) copy-start(bf16[1024,1024]{1,0:T(8,128)(2,1)} %get-tuple-element.127) | copy-start | bytes 6291460
  457.8 5.4 %copy-start.3 = (bf16[1024,1024]{1,0:T(8,128)(2,1)S(1)}, bf16[1024,1024]{1,0:T(8,128)(2,1)}, u32[]{:S(2)}) copy-start(bf16[1024,1024]{1,0:T(8,128)(2,1)} %get-tuple-element.128) | copy-start | bytes 6291460
  461.9 2.7 copy-start.11
  461.9 3.4 copy-start.10
  461.9 4.1 copy-start.9
  461.9 4.8 %copy-start.8 = (f32[128,512]{1,0:T(8,128)S(1)}, f32[128,512]{1,0:T(8,128)}, u32[]{:S(2)}) copy-start(f32[128,512]{1,0:T(8,128)} %get-tuple-element.132) | copy-start | bytes 786436
  463.2 4.2 copy-start.7
  463.2 4.9 %copy-start.6 = (f32[128,1408]{1,0:T(8,128)S(1)}, f32[128,1408]{1,0:T(8,128)}, u32[]{:S(2)}) copy-start(f32[128,1408]{1,0:T(8,128)} %get-tuple-element.134) | copy-start | bytes 2162692
  463.2 5.7 %copy-start.5 = (f32[128,1408]{1,0:T(8,128)S(1)}, f32[128,1408]{1,0:T(8,128)}, u32[]{:S(2)}) copy-start(f32[128,1408]{1,0:T(8,128)} %get-tuple-element.135) | copy-start | bytes 2162692
  463.2 6.6 %copy-start.4 = (f32[352,512]{1,0:T(8,128)S(1)}, f32[352,512]{1,0:T(8,128)}, u32[]{:S(2)}) copy-start(f32[352,512]{1,0:T(8,128)} %get-tuple-element.136) | copy-start | bytes 2162692

commit v4 on v3

--- a/solution.py
+++ b/solution.py
@@ -49,58 +49,69 @@
     width = (part + 1) * TILE
     base = part * TILE
     bias = token_bias(segc_ref[...], segr_ref[...], part)
-    pcol = lax.broadcasted_iota(jnp.int32, (TILE, HD), 1)
     lane = lax.broadcasted_iota(jnp.int32, (TILE, HD), 1)
     lse_all = jnp.zeros((TILE, HD), F32)
     blocks = TILE // CH
-    for head in range(heads):
+    reads = [[None] * blocks for head in range(heads)]
+    per_turn = -(-heads // blocks)
+    attention = {}
+
+    def memory(step, head):
+        cols = slice(head * HD, (head + 1) * HD)
+        rows = slice(step * CH, (step + 1) * CH)
+        at = (tile * blocks + step) * heads + head
+        keep = coef_ref[0, at]
+        rate = coef_ref[1, at]
+        moment = coef_ref[2, at]
+        stay = coef_ref[3, at]
+        start = mem[head] * keep
+        low_start = start.astype(BF)
+        m0_ref[step, head] = low_start
+        key = k_ref[base + step * CH:base + (step + 1) * CH, cols]
+        value = v_ref[base + step * CH:base + (step + 1) * CH, cols]
+        both = jnp.concatenate([q_ref[rows, cols], key], axis=0)
+        got = nn(both, low_start)
+        reads[head][step] = got[:CH] * SCALE
+        err = (got[CH:] * SCALE - value.astype(F32)).astype(BF)
+        err_ref[rows, cols] = err
+        speed = (moment * keep) * mom[head] - (rate * SCALE) * tn(key, err)
+        mom[head] = speed
+        mem[head] = stay * start + speed
+
+    def attend(head):
         cols = slice(head * HD, (head + 1) * HD)
         query = q_ref[:, cols]
-        state = mem[head]
-        speed = mom[head]
-        reads = []
-        for step in range(blocks):
-            rows = slice(step * CH, (step + 1) * CH)
-            at = tile * blocks + step
-            keep = coef_ref[0, at * heads + head]
-            rate = coef_ref[1, at * heads + head]
-            moment = coef_ref[2, at * heads + head]
-            stay = coef_ref[3, at * heads + head]
-            start = state * keep
-            low_start = start.astype(BF)
-            m0_ref[step, head] = low_start
-            rest = (start - low_start.astype(F32)).astype(BF)
-            key = k_ref[base + step * CH:base + (step + 1) * CH, cols]
-            value = v_ref[base + step * CH:base + (step + 1) * CH, cols]
-            both = jnp.concatenate([query[rows], key], axis=0)
-            got = nn(both, low_start) + nn(both, rest)
-            reads.append(got[:CH] * SCALE)
-            err = (got[CH:] * SCALE - value.astype(F32)).astype(BF)
-            err_ref[rows, cols] = err
-            slope = tn(key, err)
-            speed = (moment * keep) * speed - (rate * SCALE) * slope
-            state = stay * start + speed
-        mem[head] = state
-        mom[head] = speed
-        read = jnp.concatenate(reads, axis=0)
-        reads_ref[:, cols] = read.astype(BF)
         tok = nt(query, k_ref[:width, cols]) * (SCALE * LOG2E) + bias
         per = nt(query, pk_ref[:, cols]) * (SCALE * LOG2E)
-        per = jnp.where(pcol < P_SIZE, per, NEG)
+        per = jnp.where(lane < P_SIZE, per, NEG)
         top = jnp.maximum(jnp.max(tok, axis=1, keepdims=True), jnp.max(per, axis=1, keepdims=True))
         tok_e = jnp.exp2(tok - top)
         per_e = jnp.exp2(per - top)
         total = jnp.sum(tok_e, axis=1, keepdims=True) + jnp.sum(per_e, axis=1, keepdims=True)
         att = nn(tok_e.astype(BF), v_ref[:width, cols]) + nn(per_e.astype(BF), pv_ref[:, cols])
-        att = att / total
-        lse_all = jnp.where(lane == head, top + jnp.log2(total), lse_all)
+        attention[head] = att / total
+        return top + jnp.log2(total)
+
+    for step in range(blocks):
+        for head in range(heads):
+            memory(step, head)
+        for head in range(step * per_turn, min(heads, (step + 1) * per_turn)):
+            lse_all = jnp.where(lane == head, attend(head), lse_all)
+    for head in range(heads):
+        cols = slice(head * HD, (head + 1) * HD)
+        read = jnp.concatenate(reads[head], axis=0)
+        reads_ref[:, cols] = read.astype(BF)
         gate = jax.nn.sigmoid(g_ref[:, cols].astype(F32))
-        comb_ref[:, cols] = (att + gate * read).astype(BF)
+        comb_ref[:, cols] = (attention[head] + gate * read).astype(BF)
     lse_ref[...] = lse_all
 
 
 def hop_bound(turn, tiles, hops):
     return (turn * hops) // tiles
+
+
+def hop_early(turn, tiles, hops):
+    return jnp.minimum(hops, (turn * hops + tiles - 1) // tiles)
 
 
 def mix_forward_kernel(heads, n, tiles, q_ref, k_ref, v_ref, g_ref, pk_ref, pv_ref, segc_ref,
@@ -230,43 +241,45 @@
     pcol = lax.broadcasted_iota(jnp.int32, (TILE, HD), 1)
     blocks = TILE // CH
     lse_all = lse_ref[...]
-    for head in range(heads):
+    dreads = {}
+    mem_q, mem_k, mem_v = {}, {}, {}
+
+    def gates(head):
+        cols = slice(head * HD, (head + 1) * HD)
+        upf = dc_ref[:, cols].astype(F32)
+        gate = jax.nn.sigmoid(g_ref[:, cols].astype(F32))
+        dreads[head] = (upf * gate).astype(BF)
+        dgate = upf * reads_ref[:, cols].astype(F32) * gate * (1.0 - gate)
+        dout_ref[:, 3 * wide + head * HD:3 * wide + (head + 1) * HD] = dgate.astype(BF)
+
+    def memory(step, head):
+        cols = slice(head * HD, (head + 1) * HD)
+        rows = slice(step * CH, (step + 1) * CH)
+        at = (tile * blocks + step) * heads + head
+        keep = coef_ref[0, at]
+        rate = coef_ref[1, at]
+        moment = coef_ref[2, at]
+        stay = coef_ref[3, at]
+        key = k_ref[base + step * CH:base + (step + 1) * CH, cols]
+        start = m0_ref[step, head]
+        err = err_ref[rows, cols]
+        dstate = dmem[head]
+        dspeed = dmom[head] + dstate
+        dslope = (dspeed * (-rate)).astype(BF)
+        derr = nn(key, dslope) * SCALE
+        top = jnp.concatenate([dreads[head][rows], derr.astype(BF)], axis=0)
+        both = jnp.concatenate([q_ref[rows, cols], key], axis=0)
+        dmem[head] = keep * (stay * dstate + SCALE * tn(both, top))
+        dmom[head] = (moment * keep) * dspeed
+        back = nt(top, start)
+        mem_q[head, step] = back[:CH]
+        mem_k[head, step] = back[CH:] + nt(err, dslope)
+        mem_v[head, step] = derr
+
+    def attend(head):
         cols = slice(head * HD, (head + 1) * HD)
         query = q_ref[:, cols]
         up = dc_ref[:, cols]
-        upf = up.astype(F32)
-        gate = jax.nn.sigmoid(g_ref[:, cols].astype(F32))
-        dread = (upf * gate).astype(BF)
-        dgate = upf * reads_ref[:, cols].astype(F32) * gate * (1.0 - gate)
-        dout_ref[:, 3 * wide + head * HD:3 * wide + (head + 1) * HD] = dgate.astype(BF)
-        dstate = dmem[head]
-        dspeed = dmom[head]
-        dq_mem, dk_mem, dv_mem = [None] * blocks, [None] * blocks, [None] * blocks
-        for step in reversed(range(blocks)):
-            rows = slice(step * CH, (step + 1) * CH)
-            at = tile * blocks + step
-            keep = coef_ref[0, at * heads + head]
-            rate = coef_ref[1, at * heads + head]
-            moment = coef_ref[2, at * heads + head]
-            stay = coef_ref[3, at * heads + head]
-            key = k_ref[base + step * CH:base + (step + 1) * CH, cols]
-            start = m0_ref[step, head]
-            err = err_ref[rows, cols]
-            dspeed = dspeed + dstate
-            dslope = (dspeed * (-rate)).astype(BF)
-            derr = nn(key, dslope) * SCALE
-            derr_low = derr.astype(BF)
-            top = jnp.concatenate([dread[rows], derr_low], axis=0)
-            both = jnp.concatenate([query[rows], key], axis=0)
-            dstart = stay * dstate + SCALE * tn(both, top)
-            back = nt(top, start)
-            dq_mem[step] = back[:CH]
-            dk_mem[step] = back[CH:] + nt(err, dslope)
-            dv_mem[step] = derr
-            dspeed = (moment * keep) * dspeed
-            dstate = keep * dstart
-        dmem[head] = dstate
-        dmom[head] = dspeed
         tok = nt(query, k_ref[:width, cols]) * (SCALE * LOG2E) + bias
         per = nt(query, pk_ref[:, cols]) * (SCALE * LOG2E)
         per = jnp.where(pcol < P_SIZE, per, NEG)
@@ -280,27 +293,43 @@
         tok_ds = (tok_p * (tok_dp - inner)).astype(BF)
         per_ds = (per_p * (per_dp - inner)).astype(BF)
         dquery = nn(tok_ds, k_ref[:width, cols]) + nn(per_ds, pk_ref[:, cols])
-        dquery = (dquery + jnp.concatenate(dq_mem, axis=0)) * SCALE
-        dout_ref[:, cols] = dquery.astype(BF)
+        dpk_acc[:, cols] += tn(per_ds, query) * SCALE
+        dpv_acc[:, cols] += tn(per_p.astype(BF), up)
         dkey = tn(tok_ds, query)
         dval = tn(tok_p.astype(BF), up)
-        dpk_acc[:, cols] += tn(per_ds, query) * SCALE
-        dpv_acc[:, cols] += tn(per_p.astype(BF), up)
         own = slice(base, base + TILE)
         if part == TPS - 1:
-            dk_acc[:base, cols] = dkey[:base]
-            dv_acc[:base, cols] = dval[:base]
-            dk_own, dv_own = dkey[base:], dval[base:]
+            dk_acc[:, cols] = dkey
+            dv_acc[:, cols] = dval
         else:
-            if part:
-                dk_acc[:base, cols] += dkey[:base]
-                dv_acc[:base, cols] += dval[:base]
-            dk_own = dk_acc[own, cols] + dkey[base:]
-            dv_own = dv_acc[own, cols] + dval[base:]
+            dk_acc[:base + TILE, cols] += dkey
+            dv_acc[:base + TILE, cols] += dval
+        return dquery
+
+    def finish(head, dquery):
+        cols = slice(head * HD, (head + 1) * HD)
+        own = slice(base, base + TILE)
+
+        def rows_of(parts):
+            return jnp.concatenate([parts[head, step] for step in range(blocks)], axis=0)
+
+        dout_ref[:, cols] = ((dquery + rows_of(mem_q)) * SCALE).astype(BF)
         dout_ref[:, wide + head * HD:wide + (head + 1) * HD] = (
-            (dk_own + jnp.concatenate(dk_mem, axis=0)) * SCALE).astype(BF)
+            (dk_acc[own, cols] + rows_of(mem_k)) * SCALE).astype(BF)
         dout_ref[:, 2 * wide + head * HD:2 * wide + (head + 1) * HD] = (
-            dv_own - jnp.concatenate(dv_mem, axis=0)).astype(BF)
+            dv_acc[own, cols] - rows_of(mem_v)).astype(BF)
+
+    for head in range(heads):
+        gates(head)
+    per_turn = -(-heads // blocks)
+    dqueries = {}
+    for turn in range(blocks):
+        for head in range(heads):
+            memory(blocks - 1 - turn, head)
+        for head in range(turn * per_turn, min(heads, (turn + 1) * per_turn)):
+            dqueries[head] = attend(head)
+    for head in range(heads):
+        finish(head, dqueries[head])
 
 
 def mix_backward_kernel(heads, n, tiles, q_ref, k_ref, v_ref, g_ref, dc_ref, pk_ref, pv_ref,
@@ -310,11 +339,13 @@
     outs = refs[11:15]
     dmem, dmom, dk_acc, dv_acc = refs[15:19]
     scratch = refs[19:31]
-    sems = refs[31:]
+    planes = (None, 0, 1, None)
+    inbox = (None, refs[31], refs[32], None)
+    sems = refs[33:]
     turn = pl.program_id(0)
     tile = tiles - 1 - turn
     items = [
-        (own_refs[m], 0, outs[m].shape[1], sib_refs[m]) + tuple(scratch[3 * m:3 * m + 3]) + (outs[m], None, None)
+        (own_refs[m], 0, outs[m].shape[1], sib_refs[m]) + tuple(scratch[3 * m:3 * m + 3]) + (outs[m], None, None, planes[m], inbox[m])
         for m in range(4)
     ]
     g = Scatter(n, items, sems)
@@ -330,7 +361,7 @@
 
     @pl.when(turn == 0)
     def clear():
-        greet(n, g.right, g.left, False, False)
+        greet(n, g.right, g.left, False, True)
         g.begin(order)
         dmem[...] = jnp.zeros_like(dmem)
         dmom[...] = jnp.zeros_like(dmom)
@@ -342,7 +373,12 @@
 
     @pl.when(turn > 0)
     def pass_on():
-        hops(1 + hop_bound(turn - 1, tiles - 1, n - 2), 1 + hop_bound(turn, tiles - 1, n - 2))
+        hops(1 + hop_early(turn - 1, tiles - 2, n - 2), 1 + hop_early(turn, tiles - 2, n - 2))
+
+    @pl.when(turn == tiles - 1)
+    def settle():
+        for m in order:
+            g.settle(m)
 
     for part in range(TPS):
         @pl.when(lax.rem(tile, TPS) == part)
@@ -353,8 +389,6 @@
 
     @pl.when(turn == tiles - 1)
     def end():
-        for m in order:
-            g.settle(m)
         for m in order:
             g.drain(m)
 
@@ -401,7 +435,7 @@
             pltpu.VMEM((heads, HD, HD), F32),
             pltpu.VMEM((SEG, width), F32),
             pltpu.VMEM((SEG, width), F32),
-        ] + scatter_plan(arrays, False) + scatter_sems(n, 4),
+        ] + scatter_plan(arrays, False) + [pltpu.VMEM(a.shape, BF) for a in owns[1:3]] + scatter_sems(n, 4, True),
         compiler_params=pltpu.CompilerParams(
             collective_id=4, has_side_effects=True, vmem_limit_bytes=VMEM_MAX),
         name="mix_backward",
@@ -832,9 +866,10 @@
     def __init__(self, n, items, sems):
         self.n = n
         self.items = items
-        self.send, self.recv, self.local, self.sib, self.dsend, self.drecv = sems
+        self.send, self.recv, self.local, self.sib, self.dsend, self.drecv, self.xsend, self.xrecv = sems
         self.me, self.right, self.left = neighbours(n)
-        self.twin = 1 - lax.axis_index("dp")
+        self.plane = lax.axis_index("dp")
+        self.twin = 1 - self.plane
 
     def ways(self, m):
         return range(len(split_cols(self.items[m][2], m % 2)))
@@ -868,29 +903,68 @@
             send_sem=self.send.at[m, d, s], recv_sem=self.recv.at[m, d, s],
             device_id={"row": self.right if d == 0 else self.left}, device_id_type=MESH)
 
-    def total(self, m, d, s, arrived):
+    def plane_of(self, m):
+        return self.items[m][10] if len(self.items[m]) > 10 else None
+
+    def inside(self, m, action):
+        plane = self.plane_of(m)
+        if plane is None:
+            action()
+        else:
+            pl.when(self.plane == plane)(action)
+
+    def over(self, m, d, s):
+        own, inbox = self.items[m][4], self.items[m][11]
+        owner, cols = self.part(m, d, s)
+        return pltpu.make_async_remote_copy(
+            src_ref=own.at[owner, :, cols], dst_ref=inbox.at[owner, :, cols],
+            send_sem=self.xsend.at[m, d, s], recv_sem=self.xrecv.at[m, d, s],
+            device_id={"dp": self.twin}, device_id_type=MESH)
+
+    def send_over(self, m):
+        def one(s, carry):
+            for d in self.ways(m):
+                owner, cols, value = self.total(m, d, s, False, False)
+                self.items[m][4][owner, :, cols] = value
+                self.over(m, d, s).start()
+            return carry
+
+        lax.fori_loop(0, self.n, one, 0)
+
+    def total(self, m, d, s, arrived, dp=True):
         other, own, sib, ring = self.items[m][3:7]
         owner, cols = self.part(m, d, s)
         value = own[owner, :, cols].astype(F32)
         if other is not None:
             value = value + sib[owner, :, cols].astype(F32)
+        if dp and self.plane_of(m) is not None:
+            self.over(m, d, s).wait_recv()
+            value = value + self.items[m][11][owner, :, cols].astype(F32)
         if arrived:
             value = value + ring[s - 1, :, cols].astype(F32)
         return owner, cols, value.astype(own.dtype)
 
     def start(self, m):
-        for d in self.ways(m):
-            if self.items[m][3] is not None:
-                owner, cols, value = self.total(m, d, 0, False)
+        def go():
+            for d in self.ways(m):
+                if self.items[m][3] is not None:
+                    owner, cols, value = self.total(m, d, 0, False)
+                    self.items[m][4][owner, :, cols] = value
+                self.ring(m, d, 0).start()
+
+        self.inside(m, go)
+        if self.plane_of(m) is not None:
+            pl.when(self.plane != self.plane_of(m))(lambda: self.send_over(m))
+
+    def advance(self, m, s):
+        def go():
+            for d in self.ways(m):
+                self.ring(m, d, s - 1).wait_recv()
+                owner, cols, value = self.total(m, d, s, True)
                 self.items[m][4][owner, :, cols] = value
-            self.ring(m, d, 0).start()
-
-    def advance(self, m, s):
-        for d in self.ways(m):
-            self.ring(m, d, s - 1).wait_recv()
-            owner, cols, value = self.total(m, d, s, True)
-            self.items[m][4][owner, :, cols] = value
-            self.ring(m, d, s).start()
+                self.ring(m, d, s).start()
+
+        self.inside(m, go)
 
     def swap(self, m):
         low, twin = self.items[m][7:9]
@@ -899,12 +973,15 @@
             device_id={"dp": self.twin}, device_id_type=MESH)
 
     def settle(self, m):
-        for d in self.ways(m):
-            self.ring(m, d, self.n - 2).wait_recv()
-            owner, cols, value = self.total(m, d, self.n - 1, True)
-            self.items[m][7][:, cols] = value
-        if self.items[m][8] is not None:
-            self.swap(m).start()
+        def go():
+            for d in self.ways(m):
+                self.ring(m, d, self.n - 2).wait_recv()
+                owner, cols, value = self.total(m, d, self.n - 1, True)
+                self.items[m][7][:, cols] = value
+            if self.items[m][8] is not None:
+                self.swap(m).start()
+
+        self.inside(m, go)
 
     def finish(self, m):
         low, twin, out = self.items[m][7:10]
@@ -919,14 +996,24 @@
                 self.ring(m, d, s).wait_send()
             return carry
 
-        lax.fori_loop(0, self.n - 1, sent, 0)
-
-
-def scatter_sems(n, count):
-    return [
-        pltpu.SemaphoreType.DMA((count, 2, n - 1)),
-        pltpu.SemaphoreType.DMA((count, 2, n - 1)),
-    ] + [pltpu.SemaphoreType.DMA((count,))] * 4
+        def ring_done():
+            lax.fori_loop(0, self.n - 1, sent, 0)
+
+        self.inside(m, ring_done)
+        if self.plane_of(m) is not None:
+            def given(s, carry):
+                for d in self.ways(m):
+                    self.over(m, d, s).wait_send()
+                return carry
+
+            @pl.when(self.plane != self.plane_of(m))
+            def given_done():
+                lax.fori_loop(0, self.n, given, 0)
+
+
+def scatter_sems(n, count, planes=False):
+    dma = pltpu.SemaphoreType.DMA
+    return [dma((count, 2, n - 1))] * 2 + [dma((count,))] * 4 + [dma((count, 2, n) if planes else (1,))] * 2
 
 
 def scatter_plan(arrays, swap=True):
@@ -979,6 +1066,29 @@
             src_ref=late[i], dst_ref=late_in[i], send_sem=late_send.at[i], recv_sem=late_recv.at[i],
             device_id={"dp": g.twin}, device_id_type=MESH)
 
+    planes = (None, 0, 1, None)
+
+    def late_start(i):
+        if planes[i] is None:
+            late_swap(i).start()
+        else:
+            pl.when(g.plane == planes[i])(lambda: late_swap(i).start())
+
+    def late_end(i):
+        if planes[i] is None:
+            late_swap(i).wait()
+            late_outs[i][...] = late[i][...].astype(F32) + late_in[i][...].astype(F32)
+        else:
+            @pl.when(g.plane == planes[i])
+            def given():
+                late_swap(i).wait_send()
+                late_outs[i][...] = late[i][...].astype(F32)
+
+            @pl.when(g.plane != planes[i])
+            def taken():
+                late_swap(i).wait_recv()
+                late_outs[i][...] = late_in[i][...].astype(F32)
+
     cross = push(small.at[:, :, pl.ds(other * HD, HD)], small_sib, 0)
     swap_back = push(leave, came, 1)
     swap_gain = push(dg_own, dg_sib, 2)
@@ -988,19 +1098,39 @@
         greet(n, g.right, g.left, True, True)
         cross.start()
         for i in range(4):
-            late_swap(i).start()
+            late_start(i)
         for i in range(steps):
             rows = slice(i * TILE, (i + 1) * TILE)
             turned[:, rows] = normed_ref[rows, :].T
             back[rows, :] = jnp.zeros((TILE, dim), F32)
 
+    rate = (n + 5) // 7
+
+    def slot(u):
+        for m in range(5):
+            v = u - 2 * (m % 4)
+            if v < 1:
+                continue
+            low, high = max(1, rate * (v - 1) + 1), min(n - 1, rate * v + 1)
+            if low < high:
+                def one(s, carry, m=m):
+                    g.advance(m, s)
+                    return carry
+
+                lax.fori_loop(low, high, one, 0)
+            elif rate * (v - 1) + 1 < n - 1 + rate:
+                g.settle(m)
+
     for m in range(4):
         @pl.when(turn == m)
         def this():
-            grad = nn(turned[...], d_ref[...]).astype(BF)
-            for q in range(n):
-                items[m][4][q] = grad[q * block:(q + 1) * block]
+            for part in range(2):
+                cols = slice(part * (width // 2), (part + 1) * (width // 2))
+                grad = nn(turned[...], d_ref[:, cols]).astype(BF)
+                for q in range(n):
+                    items[m][4][q, :, cols] = grad[q * block:(q + 1) * block]
             g.start(m)
+            slot(2 * m)
             if m == 0:
                 cross.wait()
                 g.begin((4,))
@@ -1009,24 +1139,17 @@
             for i in range(steps):
                 rows = slice(i * TILE, (i + 1) * TILE)
                 back[rows, :] += nt(d_ref[rows, :], w_ref[...])
+            slot(2 * m + 1)
 
     @pl.when(turn == 3)
     def rest():
-        def step(low, high):
-            def one(s, carry):
-                for m in range(5):
-                    g.advance(m, s)
-                return carry
-
-            lax.fori_loop(low, high, one, 0)
-
-        hops = n - 2
         theirs = pl.multiple_of(other * rows_all, TILE)
         for i in range(rows_all // TILE):
             rows = slice(i * TILE, (i + 1) * TILE)
             leave[rows, :] = back[pl.ds(theirs + i * TILE, TILE), :].astype(BF)
         swap_back.start()
-        step(1, 1 + hop_bound(1, 3, hops))
+        slot(8)
+        slot(9)
         swap_back.wait()
         mine = pl.multiple_of(core * rows_all, TILE)
         gain = gain_ref[...]
@@ -1038,14 +1161,12 @@
             inner = jnp.mean(weighted * xf, axis=1, keepdims=True)
             value = dmid_ref[rows, :].astype(F32) + weighted * inv - xf * (inv * inv * inv) * inner
             gin_ref[rows, :] = value.astype(BF)
-            if i == 1:
-                step(1 + hop_bound(1, 3, hops), 1 + hop_bound(2, 3, hops))
-        step(1 + hop_bound(2, 3, hops), 1 + hops)
-        for m in range(5):
-            g.settle(m)
+            if i < 2:
+                slot(10 + i)
+        for u in range(12, 15):
+            slot(u)
         for i in range(4):
-            late_swap(i).wait()
-            late_outs[i][...] = late[i][...].astype(F32) + late_in[i][...].astype(F32)
+            late_end(i)
         total = jnp.zeros((block, 1), F32)
         for m in range(4):
             g.finish(m)

time: 476 us -> 454 us (0.954)
  Pallas kernels: 423 us -> 401 us
    pallas_call x1, Pallas kernels: 123 us -> 106 us  [mix_backward(): pl.pallas_call(functools.partial(mix_backward_kernel, heads, n, tiles), g...]
where the time goes in v4:
time: 454 us; the launch traced here: 449 us
  Pallas kernels  401 us (88%)
  local copies, waits for them, and re-layouts  22.8 us (5%)
  other arithmetic  12.8 us (3%)
  matrix products  11 us (2%)
    pallas_call x1, Pallas kernels, mix_backward(): pl.pallas_call(functools.partial(mix_backward_kernel, heads, n, tiles), g...  106 us
    pallas_call x1, Pallas kernels, mix_forward(): pl.pallas_call(functools.partial(mix_forward_kernel, heads, n, tiles), gr...  83.3 us
    pallas_call x1, Pallas kernels, ffn_block(): pl.pallas_call(functools.partial(ffn_kernel, tiles), grid=(tiles,), in_sp...  82.4 us
    pallas_call x1, Pallas kernels, post(): pl.pallas_call(functools.partial(post_kernel, n), grid=(4,), in_specs=[wh...  77.9 us
    pallas_call x1, Pallas kernels, gather_first(): pl.pallas_call(functools.partial(gather_kernel, n), in_specs=[vmem_spec]...  51.3 us
    dot_general x1, matrix products, nn(): lax.dot_general(a, b, (((1,), (0,)), ((), ())), preferred_element_type=F32)  10.9 us
    unnamed x51, local copies, waits for them, and re-layouts  10.1 us

profile of v4, /device:TPU:0, one launch (start us, length us, event | category | flops | bytes accessed | tf_op | source)
XLA Modules:
  0.0 449.1 jit_solution(6766414659670230526)
XLA Ops:
  0.6 1.3 fusion.13.refs_4_
  2.0 51.3 %gather_first.1 = (bf16[8,128,2048]{2,1,0:T(8,128)(2,1)}, bf16[8,48,256]{2,1,0:T(8,128)(2,1)}, bf16[2,1024,1024]{2,1,0:T(8,128)(2,1)}) custom-call(bf16[128,512]{1,0:T(8,128)(2,1)} %refs_4_.1, bf16[128,512]{1,0:T(8,128)(2,1)} %refs_5_.3, bf16[128,512]{1,0:T(8,128)(2,1)} %refs_6_.1, bf16[128,512]{1,0:T(8,128)(2,1)} %refs_7_.1, ...), custom_call_target="tpu_custom_call" | custom-call | tf_op jit(solution)/shard_map/gather_first/pallas_call | solution.py:853
  53.3 1.0 reshape.199
  54.3 0.1 copy_bitcast_fusion
  54.5 0.1 reshape.218
  54.6 3.2 multiply_reduce_fusion
  57.8 0.2 copy-done
  58.0 1.1 multiply_convert_fusion
  59.1 1.1 copy-done.1
  60.2 0.0 copy-start.12
  60.2 10.9 %convolution_convert_fusion.q_ref.k_ref.v_ref.g_ref = bf16[2048,2048]{1,0:T(8,128)(2,1)} fusion(bf16[2048,1024]{1,0:T(8,128)(2,1)S(1)} %bitcast.52, bf16[1024,2048]{1,0:T(8,128)(2,1)S(1)} %bitcast.54), kind=kOutput, calls=%fused_computation.5 | convolution fusion | flops 8594128896 | bytes 16777216 | tf_op jit(solution)/shard_map/dot_general | solution.py:28
  71.1 0.2 reshape.201
  71.3 0.7 pad.16.pk_ref
  72.0 0.7 pad.17.pv_ref
  72.6 0.0 copy-done.15
  72.6 0.0 copy-done.18
  72.6 0.2 fusion.8
  72.8 0.1 copy.46
  72.9 0.1 stack.12
  73.1 0.1 copy.47
  73.1 0.1 stack.13
  73.3 0.1 copy.48
  73.3 0.1 stack.14
  73.5 0.1 reshape.202
  73.5 0.2 fusion.9
  73.7 0.1 fusion.23
  73.8 0.1 stack_broadcast_in_dim.13
  73.9 0.1 stack_broadcast_in_dim.14
  74.0 0.6 pad_maximum_fusion.1.coef_ref
  74.6 1.3 copy.49.segc_ref
  75.9 83.3 %mix_forward.1 = (f32[2048,128]{1,0:T(8,128)}, bf16[2048,512]{1,0:T(8,128)(2,1)}, bf16[32,4,128,128]{3,2,1,0:T(8,128)(2,1)}, bf16[2048,512]{1,0:T(8,128)(2,1)}, ...) custom-call(bf16[2048,2048]{1,0:T(8,128)(2,1)} %convolution_convert_, ...), custom_call_target="tpu_custom_call" | custom-call | tf_op jit(solution)/shard_map/mix_forward/pallas_call | solution.py:195
  159.2 0.7 reshape.220.gain_ref
  159.9 82.4 %ffn_block.1 = (bf16[1024,1024]{1,0:T(8,128)(2,1)}, bf16[1024,1024]{1,0:T(8,128)(2,1)}, f32[1,1024]{1,0:T(1,128)}, f32[8,1024]{1,0:T(8,128)}, bf16[2048,512]{1,0...) custom-call(bf16[1024,1024]{1,0:T(8,128)(2,1)} %get-tuple-element.61, ...), custom_call_target="tpu_custom_call" | custom-call | tf_op jit(solution)/shard_map/ffn_block/pallas_call | solution.py:601
  242.3 106.5 %mix_backward.1 = (bf16[2048,2048]{1,0:T(8,128)(2,1)}, f32[128,512]{1,0:T(8,128)}, f32[128,512]{1,0:T(8,128)}, bf16[128,512]{1,0:T(8,128)(2,1)}, bf16[128,1408]{...) custom-call(bf16[2048,2048]{1,0:T(8,128)(2,1)} %convolution_convert_fusion.q_ref.k_ref.v_ref.g_ref, ...), custom_call_target="tpu_custom_call" | custom-call | tf_op jit(solution)/shard_map/mix_backward/pallas_call | solution.py:404
  348.8 0.8 slice.70
  349.6 0.8 slice.71
  350.4 0.1 pad.22.clone
  350.5 0.0 copy-done.14
  350.5 0.1 pad_maximum_fusion
  350.5 0.2 reshape.215
  350.8 0.1 fusion.2
  351.0 0.3 reshape.223
  351.2 0.8 copy.52.small
  352.1 4.1 fusion.1.normed_ref
  356.2 0.7 reshape.222.gain_ref
  356.8 77.9 %post.1 = (bf16[1024,1024]{1,0:T(8,128)(2,1)}, f32[128,512]{1,0:T(8,128)}, f32[128,512]{1,0:T(8,128)}, f32[128,512]{1,0:T(8,128)}, f32[128,512]{1,0:T(8,128)}, /...) custom-call(bf16[2048,1024]{1,0:T(8,128)(2,1)} %fusion.1.normed_ref,, ...), custom_call_target="tpu_custom_call" | custom-call | tf_op jit(solution)/shard_map/post/pallas_call | solution.py:1192
  434.8 1.3 fusion.27
  436.1 1.0 dynamic-slice_reduce_fusion
  437.1 0.5 convert_divide_fusion
  437.6 0.8 slice_reduce_fusion
  438.4 0.5 multiply_sqrt_fusion
  439.0 1.2 slice_bitcast_fusion
  440.2 0.0 copy-start.8
  440.2 1.3 copy.69
  441.5 0.0 copy-start.4
  441.5 1.3 copy.70
  442.8 0.7 copy.71
  443.5 0.7 copy.72
  444.2 0.7 copy.73
  445.0 0.7 copy.74
  445.7 0.7 copy.75
  446.4 0.9 copy.76
  447.2 0.9 copy.77
  448.1 0.9 copy.78
  (42 shorter events, 0.2 us)
Async XLA Ops:
  54.6 3.4 copy-start
  58.0 2.2 copy-start.1
  60.2 12.4 %copy-start.15 = (f32[16,4]{0,1:T(4,128)S(1)}, f32[16,4]{0,1:T(4,128)}, u32[]{:S(2)}) copy-start(f32[16,4]{0,1:T(4,128)} %param.35) | copy-start | bytes 772
  60.2 12.4 %copy-start.17 = (f32[16,4]{0,1:T(4,128)S(1)}, f32[16,4]{0,1:T(4,128)}, u32[]{:S(2)}) copy-start(f32[16,4]{0,1:T(4,128)} %param.34) | copy-start | bytes 772
  60.2 12.4 %copy-start.18 = (f32[16,4]{0,1:T(4,128)S(1)}, f32[16,4]{0,1:T(4,128)}, u32[]{:S(2)}) copy-start(f32[16,4]{0,1:T(4,128)} %param.33) | copy-start | bytes 772
  60.2 12.4 %copy-start.19 = (s32[32]{0:T(128)S(1)}, s32[32]{0:T(128)}, u32[]{:S(2)}) copy-start(s32[32]{0:T(128)} %param.37) | copy-start | bytes 388
  60.2 13.2 %copy-start.12 = (s32[2048]{0:T(1024)S(1)}, s32[2048]{0:T(1024)}, u32[]{:S(2)}) copy-start(s32[2048]{0:T(1024)} %param.36) | copy-start | bytes 24580
  242.3 108.2 %copy-start.14 = (f32[1,1024]{1,0:T(1,128)S(1)}, f32[1,1024]{1,0:T(1,128)}, u32[]{:S(2)}) copy-start(f32[1,1024]{1,0:T(1,128)} %get-tuple-element.84) | copy-start | bytes 12292
  242.3 108.4 %copy-start.13 = (f32[8,1024]{1,0:T(8,128)S(1)}, f32[8,1024]{1,0:T(8,128)}, u32[]{:S(2)}) copy-start(f32[8,1024]{1,0:T(8,128)} %get-tuple-element.85) | copy-start | bytes 98308
  356.8 80.3 %copy-start.16 = (bf16[64]{0:T(256)(128)(2,1)S(1)}, bf16[64]{0:T(256)(128)(2,1)}, u32[]{:S(2)}) copy-start(bf16[64]{0:T(256)(128)(2,1)} %param.21) | copy-start | bytes 388
  356.8 83.3 %copy-start.2 = (bf16[1024,1024]{1,0:T(8,128)(2,1)S(1)}, bf16[1024,1024]{1,0:T(8,128)(2,1)}, u32[]{:S(2)}) copy-start(bf16[1024,1024]{1,0:T(8,128)(2,1)} %get-tuple-element.127) | copy-start | bytes 6291460
  436.1 5.4 %copy-start.3 = (bf16[1024,1024]{1,0:T(8,128)(2,1)S(1)}, bf16[1024,1024]{1,0:T(8,128)(2,1)}, u32[]{:S(2)}) copy-start(bf16[1024,1024]{1,0:T(8,128)(2,1)} %get-tuple-element.128) | copy-start | bytes 6291460
  440.1 2.7 copy-start.11
  440.2 3.4 copy-start.10
  440.2 4.1 copy-start.9
  440.2 4.8 %copy-start.8 = (f32[128,512]{1,0:T(8,128)S(1)}, f32[128,512]{1,0:T(8,128)}, u32[]{:S(2)}) copy-start(f32[128,512]{1,0:T(8,128)} %get-tuple-element.132) | copy-start | bytes 786436
  441.5 4.2 copy-start.7
  441.5 4.9 %copy-start.6 = (f32[128,1408]{1,0:T(8,128)S(1)}, f32[128,1408]{1,0:T(8,128)}, u32[]{:S(2)}) copy-start(f32[128,1408]{1,0:T(8,128)} %get-tuple-element.134) | copy-start | bytes 2162692
  441.5 5.7 %copy-start.5 = (f32[128,1408]{1,0:T(8,128)S(1)}, f32[128,1408]{1,0:T(8,128)}, u32[]{:S(2)}) copy-start(f32[128,1408]{1,0:T(8,128)} %get-tuple-element.135) | copy-start | bytes 2162692
  441.5 6.6 %copy-start.4 = (f32[352,512]{1,0:T(8,128)S(1)}, f32[352,512]{1,0:T(8,128)}, u32[]{:S(2)}) copy-start(f32[352,512]{1,0:T(8,128)} %get-tuple-element.136) | copy-start | bytes 2162692

commit v5 on v4

--- a/solution.py
+++ b/solution.py
@@ -115,12 +115,12 @@
 
 
 def mix_forward_kernel(heads, n, tiles, q_ref, k_ref, v_ref, g_ref, pk_ref, pv_ref, segc_ref,
-                       segr_ref, coef_ref, b0, b1, b2, b3, lse_ref, reads_ref, m0_ref, err_ref,
-                       comb_out, w0, w1, w2, w3, mem, mom, comb_all, csems, *sems):
+                       segr_ref, coef_ref, b0, b1, b2, lse_ref, reads_ref, m0_ref, err_ref,
+                       comb_out, w0, w1, w2, mem, mom, comb_all, csems, *sems):
     tile = pl.program_id(0)
     core = lax.axis_index("col")
-    blocks, wholes = (b0, b1, b2, b3), (w0, w1, w2, w3)
-    planes = (None, 0, 1, None)
+    blocks, wholes = (b0, b1, b2), (w0, w1, w2)
+    planes = (0, 1, None)
     items = [(blk, ref, core * blk.shape[1], True, plane)
              for blk, ref, plane in zip(blocks, wholes, planes)]
     g = Gather(n, items, sems)
@@ -211,7 +211,7 @@
             pl.BlockSpec((TILE, width), lambda t: (t, 0)),
             pl.BlockSpec((per, heads, HD, HD), lambda t: (t, 0, 0, 0)),
             pl.BlockSpec((TILE, width), lambda t: (t, 0)),
-        ] + [any_spec] * 5,
+        ] + [any_spec] * 4,
         out_shape=[
             jax.ShapeDtypeStruct((total, HD), F32),
             jax.ShapeDtypeStruct((total, width), BF),
@@ -224,7 +224,7 @@
             pltpu.VMEM((heads, HD, HD), F32),
             pltpu.VMEM((tiles, TILE, width), BF),
             pltpu.SemaphoreType.DMA((3, tiles // 2)),
-        ] + gather_sems(n, 4),
+        ] + gather_sems(n, 3),
         compiler_params=pltpu.CompilerParams(
             collective_id=3, has_side_effects=True, vmem_limit_bytes=VMEM_MAX),
         name="mix_forward",
@@ -349,7 +349,7 @@
         for m in range(4)
     ]
     g = Scatter(n, items, sems)
-    order = (1, 2, 3, 0)
+    order = (3, 0, 1, 2)
 
     def hops(low, high):
         def one(s, carry):
@@ -370,6 +370,10 @@
         for m in order:
             g.ready(m)
             g.start(m)
+        for m in (1, 2):
+            g.give(m)
+        for m in (1, 2):
+            g.inside(m, functools.partial(g.launch, m))
 
     @pl.when(turn > 0)
     def pass_on():
@@ -815,17 +819,19 @@
     return [dma((count, 2, n - 1))] * 2 + [dma((count,))] * 3 + [dma((count, 2, n - 1))]
 
 
-def gather_kernel(n, *refs):
-    blocks = refs[:5]
-    x_ref = refs[5]
-    wide, small, pair = refs[6:9]
-    sems = refs[9:15]
-    xsems = refs[15]
+def pre_kernel(n, *refs):
+    blocks, x_ref = refs[:6], refs[6]
+    wide_out, small_out, full_out, normed_out, qkvg_out, gain_a_ref, gain_f_ref = refs[7:14]
+    wide, small, pair, normed_v, qkvg_v, xsems, osems = refs[14:21]
+    sems = refs[21:]
     core = lax.axis_index("col")
-    items = [(blocks[m], wide, m * blocks[m].shape[1], False, None) for m in range(4)]
-    items.append((blocks[4], small, core * blocks[4].shape[1], True, None))
+    dim = x_ref.shape[1]
+    planes = (0, 1, None, None)
+    items = [(blocks[m], wide, m * blocks[m].shape[1], False, planes[m]) for m in range(4)]
+    items.append((blocks[4], small, core * HD, True, None))
+    items.append((blocks[5], full_out, core * blocks[5].shape[1], True, None))
     g = Gather(n, items, sems)
-    greet(n, g.right, g.left, True, False)
+    greet(n, g.right, g.left, True, True)
     g.begin(range(5))
     mine = pltpu.make_async_copy(x_ref, pair.at[core], xsems.at[0])
     mine.start()
@@ -834,32 +840,98 @@
         device_id={"col": 1 - core}, device_id_type=MESH)
     theirs.start()
 
-    def step(s, carry):
+    def hops(ms, low, high):
+        def step(s, carry):
+            for m in ms:
+                g.advance(m, s)
+            return carry
+
+        lax.fori_loop(low, high, step, 0)
+
+    lag = n // 2 - 1
+    hops(range(5), 0, lag)
+    g.begin((5,))
+
+    def both(s, carry):
         for m in range(5):
             g.advance(m, s)
+        g.advance(5, s - lag)
         return carry
 
-    lax.fori_loop(0, n - 1, step, 0)
+    lax.fori_loop(lag, n - 1, both, 0)
+    done = n - 1 - lag
     g.finish(range(5))
     mine.wait()
     theirs.wait()
-
-
-def gather_first(n, blocks, small, x):
+    copies = [pltpu.make_async_copy(wide, wide_out, osems.at[0]),
+              pltpu.make_async_copy(small, small_out, osems.at[1])]
+    for copy in copies:
+        copy.start()
+    gains = jnp.zeros((16, HD), F32)
+    for q in range(n):
+        for i in range(2):
+            gains = gains + small[q, 2 * P_SIZE:, i * HD:(i + 1) * HD].astype(F32)
+    tiles = dim // HD
+    gain = jnp.concatenate([gains[i:i + 1] for i in range(tiles)], axis=1)
+    gain_a_ref[...] = gain
+    gain_f_ref[...] = jnp.concatenate([gains[tiles + i:tiles + i + 1] for i in range(tiles)], axis=1)
+    chunk = normed_v.shape[1]
+    count = normed_v.shape[0]
+    per_core = count // 2
+    width = qkvg_v.shape[2] // 2
+    slots = 2 * count - 1
+    for i in range(count):
+        rows = slice((i % per_core) * chunk, (i % per_core + 1) * chunk)
+        xf = pair[i // per_core, rows, :].astype(F32)
+        inv = lax.rsqrt(jnp.mean(xf * xf, axis=1, keepdims=True) + EPS)
+        normed_v[i] = (xf * inv * gain).astype(BF)
+        copies.append(pltpu.make_async_copy(
+            normed_v.at[i], normed_out.at[pl.ds(i * chunk, chunk)], osems.at[2 + i]))
+        copies[-1].start()
+        for j in range(2):
+            cols = slice(j * width, (j + 1) * width)
+            weight = wide[:, :, cols].reshape(dim, width)
+            qkvg_v[i, :, cols] = nn(normed_v[i], weight).astype(BF)
+            u = 2 * i + j
+            if u < slots:
+                hops((5,), done + u * lag // slots, done + (u + 1) * lag // slots)
+        copies.append(pltpu.make_async_copy(
+            qkvg_v.at[i], qkvg_out.at[pl.ds(i * chunk, chunk)], osems.at[2 + count + i]))
+        copies[-1].start()
+    g.finish((5,))
+    for copy in copies:
+        copy.wait()
+
+
+def pre(n, blocks, small, w_out, x):
     rows, width = blocks[0].shape
+    tokens, dim = x.shape
+    count = 2 * tokens // 512
     any_spec = pl.BlockSpec(memory_space=pl.ANY)
     vmem_spec = pl.BlockSpec(memory_space=pltpu.VMEM)
-    shapes = [(n, rows, 4 * width), (n, small.shape[0], 2 * small.shape[1]), (2,) + x.shape]
+    dma = pltpu.SemaphoreType.DMA
+    wide = (n, rows, 4 * width)
+    smalls = (n, small.shape[0], 2 * small.shape[1])
+    shapes = [wide, smalls, (n, rows, 2 * w_out.shape[1]), (2 * tokens, dim), (2 * tokens, 4 * width)]
     return pl.pallas_call(
-        functools.partial(gather_kernel, n),
-        in_specs=[vmem_spec] * 6,
-        out_specs=[any_spec] * 3,
-        out_shape=[jax.ShapeDtypeStruct(shape, BF) for shape in shapes],
-        scratch_shapes=gather_sems(n, 5) + [pltpu.SemaphoreType.DMA((3,))],
+        functools.partial(pre_kernel, n),
+        in_specs=[vmem_spec] * 7,
+        out_specs=[any_spec] * 5 + [vmem_spec] * 2,
+        out_shape=[jax.ShapeDtypeStruct(shape, BF) for shape in shapes]
+        + [jax.ShapeDtypeStruct((1, dim), F32)] * 2,
+        scratch_shapes=[
+            pltpu.VMEM(wide, BF),
+            pltpu.VMEM(smalls, BF),
+            pltpu.VMEM((2,) + x.shape, BF),
+            pltpu.VMEM((count, 512, dim), BF),
+            pltpu.VMEM((count, 512, 4 * width), BF),
+            dma((3,)),
+            dma((2 + 2 * count,)),
+        ] + gather_sems(n, 6),
         compiler_params=pltpu.CompilerParams(
             collective_id=1, has_side_effects=True, vmem_limit_bytes=VMEM_MAX),
-        name="gather_first",
-    )(*blocks, small, x)
+        name="pre",
+    )(*blocks, small, w_out, x)
 
 
 class Scatter:
@@ -944,17 +1016,19 @@
             value = value + ring[s - 1, :, cols].astype(F32)
         return owner, cols, value.astype(own.dtype)
 
+    def launch(self, m):
+        for d in self.ways(m):
+            if self.items[m][3] is not None:
+                owner, cols, value = self.total(m, d, 0, False)
+                self.items[m][4][owner, :, cols] = value
+            self.ring(m, d, 0).start()
+
+    def give(self, m):
+        pl.when(self.plane != self.plane_of(m))(lambda: self.send_over(m))
+
     def start(self, m):
-        def go():
-            for d in self.ways(m):
-                if self.items[m][3] is not None:
-                    owner, cols, value = self.total(m, d, 0, False)
-                    self.items[m][4][owner, :, cols] = value
-                self.ring(m, d, 0).start()
-
-        self.inside(m, go)
-        if self.plane_of(m) is not None:
-            pl.when(self.plane != self.plane_of(m))(lambda: self.send_over(m))
+        if self.plane_of(m) is None:
+            self.launch(m)
 
     def advance(self, m, s):
         def go():
@@ -1249,23 +1323,22 @@
     heads = mem_rate.shape[1]
     width = heads * HD
     piece = gain_attn.shape[0]
-    small = jnp.concatenate(
-        [persist_key, persist_value, gain_attn[None, :], gain_ffn[None, :]], axis=0)
-    small = jnp.pad(small, ((0, 48 - small.shape[0]), (0, HD - piece)))
-    wide, small_all, pair = gather_first(n, (w_query, w_key, w_value, w_gate), small, tokens_in)
+    slot = lax.axis_index("row") * 2 + core
+
+    def spread(part):
+        return lax.dynamic_update_slice(jnp.zeros((dim,), BF), part, (slot * piece,)).reshape(dim // HD, HD)
+
+    persist = jnp.pad(jnp.concatenate([persist_key, persist_value], axis=0), ((0, 0), (0, HD - piece)))
+    small = jnp.concatenate([persist, spread(gain_attn), spread(gain_ffn)], axis=0)
+    wide, small_all, full_out, normed, qkvg, gain_a, gain_f = pre(
+        n, (w_query, w_key, w_value, w_gate), small, w_out, tokens_in)
     wide = wide.reshape(dim, 4 * width)
-    small_all = small_all.reshape(n, 48, 2, HD)[:, :, :, :piece].transpose(1, 0, 2, 3).reshape(48, dim)
-    gain_a = small_all[2 * P_SIZE][None, :].astype(F32)
-    gain_f = small_all[2 * P_SIZE + 1][None, :].astype(F32)
+    small_all = small_all[:, :2 * P_SIZE].reshape(n, 2 * P_SIZE, 2, HD)[:, :, :, :piece]
+    small_all = small_all.transpose(1, 0, 2, 3).reshape(2 * P_SIZE, dim)
     own_small = lax.dynamic_slice_in_dim(small_all, core * width, width, 1)
     pad = ((0, HD - P_SIZE), (0, 0))
     pkey = jnp.pad(own_small[:P_SIZE], pad)
     pvalue = jnp.pad(own_small[P_SIZE:2 * P_SIZE], pad)
-
-    inputs = pair.reshape(2 * local_tok, dim).astype(F32)
-    inverse_a = lax.rsqrt(jnp.mean(inputs * inputs, axis=-1, keepdims=True) + EPS)
-    normed = (inputs * inverse_a * gain_a).astype(BF)
-    qkvg = nn(normed, wide).astype(BF)
 
     total = qkvg.shape[0]
     spans = total // CH
@@ -1280,8 +1353,8 @@
     ).reshape(4, spans * heads)
     segc, segr = segment_ids[:, None], segment_ids[None, :]
 
-    later = (w_out, w_ffn_gate, w_ffn_up, w_ffn_down)
-    lse, reads, m0, err, comb_tok, full_out, full_gate, full_up, full_down = mix_forward(
+    later = (w_ffn_gate, w_ffn_up, w_ffn_down)
+    lse, reads, m0, err, comb_tok, full_gate, full_up, full_down = mix_forward(
         n, qkvg, pkey, pvalue, segc, segr, coef, heads, later)
     full_out, full_gate, full_up = [a.reshape(dim, -1) for a in (full_out, full_gate, full_up)]
     full_down = full_down.reshape(-1, dim)

time: 454 us -> 430 us (0.947)
  matrix products: 11 us -> 0.19 us
  other arithmetic: 12.8 us -> 4.26 us
  Pallas kernels: 401 us -> 395 us
    pallas_call x1, Pallas kernels: 83.3 us -> 69 us  [mix_forward(): pl.pallas_call(functools.partial(mix_forward_kernel, heads, n, tiles), gr...]
    pallas_call x1, Pallas kernels: 51.3 us -> 62.8 us  [pre(): pl.pallas_call(functools.partial(pre_kernel, n), in_specs=[vmem_spec] * 7...]
    dot_general x1 -> x0, matrix products: 10.9 us -> none  [nn(): lax.dot_general(a, b, (((1,), (0,)), ((), ())), preferred_element_type=F32)]
    pallas_call x1, Pallas kernels: 77.9 us -> 71.6 us  [post(): pl.pallas_call(functools.partial(post_kernel, n), grid=(4,), in_specs=[wh...]
    convert_element_type x3 -> x0, other arithmetic: 5.22 us -> none  [the longest x2 5.21 us: local(): normed = (inputs * inverse_a * gain_a).astype(BF)]
    unnamed x51 -> x46, local copies, waits for them, and re-layouts: 10.1 us -> 8.8 us
where the time goes in v5:
time: 430 us; the launch traced here: 422 us
  Pallas kernels  395 us (92%)
  local copies, waits for them, and re-layouts  21.7 us (5%)
    pallas_call x1, Pallas kernels, mix_backward(): pl.pallas_call(functools.partial(mix_backward_kernel, heads, n, tiles), g...  109 us
    pallas_call x1, Pallas kernels, ffn_block(): pl.pallas_call(functools.partial(ffn_kernel, tiles), grid=(tiles,), in_sp...  82.4 us
    pallas_call x1, Pallas kernels, post(): pl.pallas_call(functools.partial(post_kernel, n), grid=(4,), in_specs=[wh...  71.6 us
    pallas_call x1, Pallas kernels, mix_forward(): pl.pallas_call(functools.partial(mix_forward_kernel, heads, n, tiles), gr...  69 us
    pallas_call x1, Pallas kernels, pre(): pl.pallas_call(functools.partial(pre_kernel, n), in_specs=[vmem_spec] * 7...  62.8 us
    unnamed x46, local copies, waits for them, and re-layouts  8.8 us

profile of v5, /device:TPU:0, one launch (start us, length us, event | category | flops | bytes accessed | tf_op | source)
XLA Modules:
  0.0 422.5 jit_solution(10570740082481739676)
XLA Ops:
  0.6 0.0 copy-start.13
  0.7 0.0 copy-start.15
  0.7 0.0 copy-start.14
  0.7 0.0 copy-start.16
  0.7 0.0 copy-start.10
  0.7 0.8 dynamic_update_slice.9
  1.6 0.8 dynamic_update_slice.10
  2.4 0.7 fusion.5
  3.1 0.6 pad_maximum_fusion.1.refs_4_
  3.7 62.8 %pre.1 = (bf16[8,128,2048]{2,1,0:T(8,128)(2,1)}, bf16[8,48,256]{2,1,0:T(8,128)(2,1)}, bf16[8,128,1024]{2,1,0:T(8,128)(2,1)}, bf16[2048,1024]{1,0:T(8,128)(2,1)},...) custom-call(bf16[128,512]{1,0:T(8,128)(2,1)} %refs_4_.1, bf16[128,512]{1,0:T(8,128)(2,1)} %refs_5_.3, ...), custom_call_target="tpu_custom_call" | custom-call | tf_op jit(solution)/shard_map/pre/pallas_call | solution.py:916
  66.6 0.9 slice.55
  67.5 0.1 copy_bitcast_fusion
  67.6 0.1 reshape.144
  67.8 0.7 pad.16.pk_ref
  68.4 0.7 pad.17.pv_ref
  69.1 0.0 copy-done.13
  69.1 0.0 copy-done.15
  69.1 0.0 copy-done.14
  69.1 0.0 copy-done.16
  69.1 0.2 fusion.3
  69.3 0.1 copy.46
  69.4 0.1 stack.12
  69.5 0.1 copy.47
  69.6 0.1 stack.13
  69.7 0.1 copy.48
  69.8 0.1 stack.14
  69.9 0.0 copy-done.10
  70.0 0.1 reshape.145
  70.0 0.2 fusion.4
  70.2 0.1 fusion.12
  70.3 0.1 stack_broadcast_in_dim.13
  70.4 0.1 stack_broadcast_in_dim.14
  70.5 0.6 pad_maximum_fusion.2.coef_ref
  71.1 1.3 copy.49.segc_ref
  72.4 69.0 %mix_forward.1 = (f32[2048,128]{1,0:T(8,128)}, bf16[2048,512]{1,0:T(8,128)(2,1)}, bf16[32,4,128,128]{3,2,1,0:T(8,128)(2,1)}, bf16[2048,512]{1,0:T(8,128)(2,1)}, ...) custom-call(bf16[2048,2048]{1,0:T(8,128)(2,1)} %get-tuple-element.61, ...), custom_call_target="tpu_custom_call" | custom-call | tf_op jit(solution)/shard_map/mix_forward/pallas_call | solution.py:195
  141.5 82.4 %ffn_block.1 = (bf16[1024,1024]{1,0:T(8,128)(2,1)}, bf16[1024,1024]{1,0:T(8,128)(2,1)}, f32[1,1024]{1,0:T(1,128)}, f32[8,1024]{1,0:T(8,128)}, bf16[2048,512]{1,0...) custom-call(bf16[1024,1024]{1,0:T(8,128)(2,1)} %get-tuple-element.63, ...), custom_call_target="tpu_custom_call" | custom-call | tf_op jit(solution)/shard_map/ffn_block/pallas_call | solution.py:605
  223.9 109.4 %mix_backward.1 = (bf16[2048,2048]{1,0:T(8,128)(2,1)}, f32[128,512]{1,0:T(8,128)}, f32[128,512]{1,0:T(8,128)}, bf16[128,512]{1,0:T(8,128)(2,1)}, bf16[128,1408]{...) custom-call(bf16[2048,2048]{1,0:T(8,128)(2,1)} %get-tuple-element.61.q_ref.k_ref.v_ref.g_ref, ...), custom_call_target="tpu_custom_call" | custom-call | tf_op jit(solution)/shard_map/mix_backward/pallas_call | solution.py:408
  333.3 0.8 slice.64
  334.0 0.8 slice.65
  334.8 0.1 pad.22.clone
  334.9 0.0 copy-done.12
  334.9 0.1 pad_maximum_fusion
  335.0 0.2 reshape.159
  335.2 0.1 fusion
  335.4 0.3 reshape.163
  335.7 0.8 copy.52.small
  336.5 71.6 %post.1 = (bf16[1024,1024]{1,0:T(8,128)(2,1)}, f32[128,512]{1,0:T(8,128)}, f32[128,512]{1,0:T(8,128)}, f32[128,512]{1,0:T(8,128)}, f32[128,512]{1,0:T(8,128)}, /...) custom-call(bf16[2048,1024]{1,0:T(8,128)(2,1)} %get-tuple-element.70, ...), custom_call_target="tpu_custom_call" | custom-call | tf_op jit(solution)/shard_map/post/pallas_call | solution.py:1266
  408.1 1.3 fusion.15
  409.4 1.0 dynamic-slice_reduce_fusion
  410.5 0.5 convert_divide_fusion
  411.0 0.8 slice_reduce_fusion
  411.8 0.5 multiply_sqrt_fusion
  412.3 1.2 slice_bitcast_fusion
  413.5 1.3 copy.70
  414.9 1.3 copy.71
  416.2 0.7 copy.72
  416.9 0.7 copy.73
  417.6 0.7 copy.74
  418.3 0.7 copy.75
  419.0 0.7 copy.76
  419.7 0.9 copy.77
  420.6 0.9 copy.78
  421.4 0.0 copy-done.2
  421.4 0.9 copy.79
  (34 shorter events, 0.2 us)
Async XLA Ops:
  0.6 68.5 %copy-start.13 = (f32[16,4]{0,1:T(4,128)S(1)}, f32[16,4]{0,1:T(4,128)}, u32[]{:S(2)}) copy-start(f32[16,4]{0,1:T(4,128)} %param.35) | copy-start | bytes 772
  0.7 68.5 %copy-start.15 = (f32[16,4]{0,1:T(4,128)S(1)}, f32[16,4]{0,1:T(4,128)}, u32[]{:S(2)}) copy-start(f32[16,4]{0,1:T(4,128)} %param.33) | copy-start | bytes 772
  0.7 68.5 %copy-start.14 = (f32[16,4]{0,1:T(4,128)S(1)}, f32[16,4]{0,1:T(4,128)}, u32[]{:S(2)}) copy-start(f32[16,4]{0,1:T(4,128)} %param.34) | copy-start | bytes 772
  0.7 68.4 %copy-start.16 = (s32[32]{0:T(128)S(1)}, s32[32]{0:T(128)}, u32[]{:S(2)}) copy-start(s32[32]{0:T(128)} %param.37) | copy-start | bytes 388
  0.7 69.3 %copy-start.10 = (s32[2048]{0:T(1024)S(1)}, s32[2048]{0:T(1024)}, u32[]{:S(2)}) copy-start(s32[2048]{0:T(1024)} %param.36) | copy-start | bytes 24580
  223.9 111.0 %copy-start.12 = (f32[1,1024]{1,0:T(1,128)S(1)}, f32[1,1024]{1,0:T(1,128)}, u32[]{:S(2)}) copy-start(f32[1,1024]{1,0:T(1,128)} %get-tuple-element.90) | copy-start | bytes 12292
  223.9 111.3 %copy-start.11 = (f32[8,1024]{1,0:T(8,128)S(1)}, f32[8,1024]{1,0:T(8,128)}, u32[]{:S(2)}) copy-start(f32[8,1024]{1,0:T(8,128)} %get-tuple-element.91) | copy-start | bytes 98308
  336.5 74.0 %copy-start.17 = (bf16[64]{0:T(256)(128)(2,1)S(1)}, bf16[64]{0:T(256)(128)(2,1)}, u32[]{:S(2)}) copy-start(bf16[64]{0:T(256)(128)(2,1)} %param.21) | copy-start | bytes 388
  336.5 77.0 %copy-start = (bf16[1024,1024]{1,0:T(8,128)(2,1)S(1)}, bf16[1024,1024]{1,0:T(8,128)(2,1)}, u32[]{:S(2)}) copy-start(bf16[1024,1024]{1,0:T(8,128)(2,1)} %get-tuple-element.129) | copy-start | bytes 6291460
  409.4 5.4 %copy-start.1 = (bf16[1024,1024]{1,0:T(8,128)(2,1)S(1)}, bf16[1024,1024]{1,0:T(8,128)(2,1)}, u32[]{:S(2)}) copy-start(bf16[1024,1024]{1,0:T(8,128)(2,1)} %get-tuple-element.130) | copy-start | bytes 6291460
  414.8 1.4 copy-start.9
  414.8 2.1 copy-start.8
  414.8 2.8 copy-start.7
  414.8 3.5 copy-start.6
  414.8 4.2 copy-start.5
  414.8 4.9 %copy-start.4 = (f32[128,1408]{1,0:T(8,128)S(1)}, f32[128,1408]{1,0:T(8,128)}, u32[]{:S(2)}) copy-start(f32[128,1408]{1,0:T(8,128)} %get-tuple-element.136) | copy-start | bytes 2162692
  416.2 4.4 %copy-start.3 = (f32[128,1408]{1,0:T(8,128)S(1)}, f32[128,1408]{1,0:T(8,128)}, u32[]{:S(2)}) copy-start(f32[128,1408]{1,0:T(8,128)} %get-tuple-element.137) | copy-start | bytes 2162692
  416.2 5.3 %copy-start.2 = (f32[352,512]{1,0:T(8,128)S(1)}, f32[352,512]{1,0:T(8,128)}, u32[]{:S(2)}) copy-start(f32[352,512]{1,0:T(8,128)} %get-tuple-element.138) | copy-start | bytes 2162692

commit v6 on v5

--- a/solution.py
+++ b/solution.py
@@ -516,8 +516,9 @@
 
     wd = jnp.concatenate([wd0[...], wd1[...]], axis=0)
     both = jnp.concatenate([wg0[...], wg1[...], wu0[...], wu1[...]], axis=1)
-    for i in range(steps):
-        rows = slice(i * TILE, (i + 1) * TILE)
+    chunk = 2 * TILE
+    for i in range(rows_all // chunk):
+        rows = slice(i * chunk, (i + 1) * chunk)
         gateup = nn(n2[rows, :], both)
         gate, up = gateup[:, :ft], gateup[:, ft:]
         dh = nt(dy_ref[rows, :], wd)
@@ -822,8 +823,8 @@
 def pre_kernel(n, *refs):
     blocks, x_ref = refs[:6], refs[6]
     wide_out, small_out, full_out, normed_out, qkvg_out, gain_a_ref, gain_f_ref = refs[7:14]
-    wide, small, pair, normed_v, qkvg_v, xsems, osems = refs[14:21]
-    sems = refs[21:]
+    wide, small, pair, normed_v, turned_v, qkvg_v, xsems, osems = refs[14:22]
+    sems = refs[22:]
     core = lax.axis_index("col")
     dim = x_ref.shape[1]
     planes = (0, 1, None, None)
@@ -885,9 +886,6 @@
         xf = pair[i // per_core, rows, :].astype(F32)
         inv = lax.rsqrt(jnp.mean(xf * xf, axis=1, keepdims=True) + EPS)
         normed_v[i] = (xf * inv * gain).astype(BF)
-        copies.append(pltpu.make_async_copy(
-            normed_v.at[i], normed_out.at[pl.ds(i * chunk, chunk)], osems.at[2 + i]))
-        copies[-1].start()
         for j in range(2):
             cols = slice(j * width, (j + 1) * width)
             weight = wide[:, :, cols].reshape(dim, width)
@@ -895,6 +893,10 @@
             u = 2 * i + j
             if u < slots:
                 hops((5,), done + u * lag // slots, done + (u + 1) * lag // slots)
+        turned_v[i] = normed_v[i].T
+        copies.append(pltpu.make_async_copy(
+            turned_v.at[i], normed_out.at[:, pl.ds(i * chunk, chunk)], osems.at[2 + i]))
+        copies[-1].start()
         copies.append(pltpu.make_async_copy(
             qkvg_v.at[i], qkvg_out.at[pl.ds(i * chunk, chunk)], osems.at[2 + count + i]))
         copies[-1].start()
@@ -912,7 +914,7 @@
     dma = pltpu.SemaphoreType.DMA
     wide = (n, rows, 4 * width)
     smalls = (n, small.shape[0], 2 * small.shape[1])
-    shapes = [wide, smalls, (n, rows, 2 * w_out.shape[1]), (2 * tokens, dim), (2 * tokens, 4 * width)]
+    shapes = [wide, smalls, (n, rows, 2 * w_out.shape[1]), (dim, 2 * tokens), (2 * tokens, 4 * width)]
     return pl.pallas_call(
         functools.partial(pre_kernel, n),
         in_specs=[vmem_spec] * 7,
@@ -924,6 +926,7 @@
             pltpu.VMEM(smalls, BF),
             pltpu.VMEM((2,) + x.shape, BF),
             pltpu.VMEM((count, 512, dim), BF),
+            pltpu.VMEM((count, dim, 512), BF),
             pltpu.VMEM((count, 512, 4 * width), BF),
             dma((3,)),
             dma((2 + 2 * count,)),
@@ -1104,18 +1107,18 @@
     return scratch
 
 
-def post_kernel(n, normed_ref, d_ref, w_ref, x_ref, dmid_ref, gain_ref, small, *refs):
+def post_kernel(n, turned, d_ref, w_ref, x_ref, dmid_ref, gain_ref, small, *refs):
     late = refs[:4]
     own_w = refs[4:8]
     gin_ref = refs[8]
     outs = refs[9:14]
     late_outs = refs[14:18]
     dgain_ref = refs[18]
-    turned, back, leave, came, dg_own, dg_sib, small_sib = refs[19:26]
-    late_in = refs[26:30]
-    scratch = refs[30:55]
-    side, late_send, late_recv = refs[55:58]
-    sems = refs[58:]
+    back, leave, came, dg_own, dg_sib, small_sib = refs[19:25]
+    late_in = refs[25:29]
+    scratch = refs[29:54]
+    side, late_send, late_recv = refs[54:57]
+    sems = refs[57:]
     turn = pl.program_id(0)
     core = lax.axis_index("col")
     other = 1 - core
@@ -1173,10 +1176,6 @@
         cross.start()
         for i in range(4):
             late_start(i)
-        for i in range(steps):
-            rows = slice(i * TILE, (i + 1) * TILE)
-            turned[:, rows] = normed_ref[rows, :].T
-            back[rows, :] = jnp.zeros((TILE, dim), F32)
 
     rate = (n + 5) // 7
 
@@ -1210,9 +1209,12 @@
                 g.begin((4,))
                 g.ready(4)
                 g.start(4)
-            for i in range(steps):
-                rows = slice(i * TILE, (i + 1) * TILE)
-                back[rows, :] += nt(d_ref[rows, :], w_ref[...])
+            for i in range(steps // 2):
+                rows = slice(2 * i * TILE, 2 * (i + 1) * TILE)
+                if m == 0:
+                    back[rows, :] = nt(d_ref[rows, :], w_ref[...])
+                else:
+                    back[rows, :] += nt(d_ref[rows, :], w_ref[...])
             slot(2 * m + 1)
 
     @pl.when(turn == 3)
@@ -1253,7 +1255,7 @@
 
 
 def post(n, normed, dqkvg, wide, x, dmid, gain, small, late, own_w):
-    total, dim = normed.shape
+    dim, total = normed.shape
     width = wide.shape[1] // 4
     rows = x.shape[0]
     block = dim // n
@@ -1267,7 +1269,7 @@
         functools.partial(post_kernel, n),
         grid=(4,),
         in_specs=[
-            whole((total, dim)),
+            whole((dim, total)),
             pl.BlockSpec((total, width), lambda t: (0, t)),
             pl.BlockSpec((dim, width), lambda t: (0, t)),
             whole((rows, dim)),
@@ -1278,7 +1280,6 @@
         out_specs=[whole(shape) for shape, kind in shapes],
         out_shape=[jax.ShapeDtypeStruct(shape, kind) for shape, kind in shapes],
         scratch_shapes=[
-            pltpu.VMEM((dim, total), BF),
             pltpu.VMEM((total, dim), F32),
             pltpu.VMEM((rows, dim), BF),
             pltpu.VMEM((rows, dim), BF),

time: 430 us -> 427 us (level)
  no operation moved by 1% of the time
where the time goes in v6:
time: 427 us; the launch traced here: 419 us
  Pallas kernels  392 us (92%)
  local copies, waits for them, and re-layouts  21.7 us (5%)
    pallas_call x1, Pallas kernels, mix_backward(): pl.pallas_call(functools.partial(mix_backward_kernel, heads, n, tiles), g...  108 us
    pallas_call x1, Pallas kernels, ffn_block(): pl.pallas_call(functools.partial(ffn_kernel, tiles), grid=(tiles,), in_sp...  80.6 us
    pallas_call x1, Pallas kernels, post(): pl.pallas_call(functools.partial(post_kernel, n), grid=(4,), in_specs=[wh...  71 us
    pallas_call x1, Pallas kernels, mix_forward(): pl.pallas_call(functools.partial(mix_forward_kernel, heads, n, tiles), gr...  69 us
    pallas_call x1, Pallas kernels, pre(): pl.pallas_call(functools.partial(pre_kernel, n), in_specs=[vmem_spec] * 7...  63.2 us
    unnamed x46, local copies, waits for them, and re-layouts  8.8 us

profile of v6, /device:TPU:0, one launch (start us, length us, event | category | flops | bytes accessed | tf_op | source)
XLA Modules:
  0.0 419.0 jit_solution(11205450859270240273)
XLA Ops:
  0.6 0.0 copy-start.13
  0.7 0.0 copy-start.15
  0.7 0.0 copy-start.14
  0.7 0.0 copy-start.16
  0.7 0.0 copy-start.10
  0.7 0.8 dynamic_update_slice.9
  1.6 0.8 dynamic_update_slice.10
  2.4 0.7 fusion.5
  3.1 0.6 pad_maximum_fusion.1.refs_4_
  3.7 63.2 %pre.1 = (bf16[8,128,2048]{2,1,0:T(8,128)(2,1)}, bf16[8,48,256]{2,1,0:T(8,128)(2,1)}, bf16[8,128,1024]{2,1,0:T(8,128)(2,1)}, bf16[1024,2048]{1,0:T(8,128)(2,1)},...) custom-call(bf16[128,512]{1,0:T(8,128)(2,1)} %refs_4_.1, bf16[128,512]{1,0:T(8,128)(2,1)} %refs_5_.3, ...), custom_call_target="tpu_custom_call" | custom-call | tf_op jit(solution)/shard_map/pre/pallas_call | solution.py:918
  66.9 0.9 slice.55
  67.9 0.1 copy_bitcast_fusion
  68.0 0.1 reshape.144
  68.1 0.7 pad.16.pk_ref
  68.8 0.7 pad.17.pv_ref
  69.5 0.0 copy-done.13
  69.5 0.0 copy-done.15
  69.5 0.2 fusion.3
  69.7 0.1 copy.46
  69.8 0.1 stack.12
  69.9 0.1 copy.47
  70.0 0.1 stack.13
  70.1 0.1 copy.48
  70.2 0.1 stack.14
  70.3 0.1 reshape.145
  70.4 0.2 fusion.4
  70.6 0.1 fusion.12
  70.6 0.1 stack_broadcast_in_dim.13
  70.7 0.1 stack_broadcast_in_dim.14
  70.8 0.6 pad_maximum_fusion.2.coef_ref
  71.4 1.3 copy.49.segc_ref
  72.8 69.0 %mix_forward.1 = (f32[2048,128]{1,0:T(8,128)}, bf16[2048,512]{1,0:T(8,128)(2,1)}, bf16[32,4,128,128]{3,2,1,0:T(8,128)(2,1)}, bf16[2048,512]{1,0:T(8,128)(2,1)}, ...) custom-call(bf16[2048,2048]{1,0:T(8,128)(2,1)} %get-tuple-element.61, ...), custom_call_target="tpu_custom_call" | custom-call | tf_op jit(solution)/shard_map/mix_forward/pallas_call | solution.py:195
  141.8 80.6 %ffn_block.1 = (bf16[1024,1024]{1,0:T(8,128)(2,1)}, bf16[1024,1024]{1,0:T(8,128)(2,1)}, f32[1,1024]{1,0:T(1,128)}, f32[8,1024]{1,0:T(8,128)}, bf16[2048,512]{1,0...) custom-call(bf16[1024,1024]{1,0:T(8,128)(2,1)} %get-tuple-element.63, ...), custom_call_target="tpu_custom_call" | custom-call | tf_op jit(solution)/shard_map/ffn_block/pallas_call | solution.py:606
  222.5 108.0 %mix_backward.1 = (bf16[2048,2048]{1,0:T(8,128)(2,1)}, f32[128,512]{1,0:T(8,128)}, f32[128,512]{1,0:T(8,128)}, bf16[128,512]{1,0:T(8,128)(2,1)}, bf16[128,1408]{...) custom-call(bf16[2048,2048]{1,0:T(8,128)(2,1)} %get-tuple-element.61.q_ref.k_ref.v_ref.g_ref, ...), custom_call_target="tpu_custom_call" | custom-call | tf_op jit(solution)/shard_map/mix_backward/pallas_call | solution.py:408
  330.5 0.8 slice.64
  331.2 0.8 slice.65
  332.0 0.1 pad.22.clone
  332.1 0.1 pad_maximum_fusion
  332.2 0.2 reshape.159
  332.4 0.0 copy-done.11
  332.4 0.1 fusion
  332.6 0.3 reshape.163
  332.9 0.8 copy.52.small
  333.7 71.0 %post.1 = (bf16[1024,1024]{1,0:T(8,128)(2,1)}, f32[128,512]{1,0:T(8,128)}, f32[128,512]{1,0:T(8,128)}, f32[128,512]{1,0:T(8,128)}, f32[128,512]{1,0:T(8,128)}, /...) custom-call(bf16[1024,2048]{1,0:T(8,128)(2,1)} %get-tuple-element.70, ...), custom_call_target="tpu_custom_call" | custom-call | tf_op jit(solution)/shard_map/post/pallas_call | solution.py:1268
  404.7 1.3 fusion.15
  406.0 1.0 dynamic-slice_reduce_fusion
  407.0 0.0 copy-done.17
  407.0 0.5 convert_divide_fusion
  407.5 0.8 slice_reduce_fusion
  408.3 0.5 multiply_sqrt_fusion
  408.9 1.2 slice_bitcast_fusion
  410.0 1.3 copy.70
  411.4 1.3 copy.71
  412.7 0.0 copy-done.9
  412.7 0.7 copy.72
  413.4 0.0 copy-done.8
  413.4 0.7 copy.73
  414.1 0.7 copy.74
  414.9 0.7 copy.75
  415.6 0.7 copy.76
  416.3 0.9 copy.77
  417.1 0.9 copy.78
  418.0 0.0 copy-done.2
  418.0 0.9 copy.79
  (34 shorter events, 0.2 us)
Async XLA Ops:
  0.6 68.8 %copy-start.13 = (f32[16,4]{0,1:T(4,128)S(1)}, f32[16,4]{0,1:T(4,128)}, u32[]{:S(2)}) copy-start(f32[16,4]{0,1:T(4,128)} %param.35) | copy-start | bytes 772
  0.7 68.8 %copy-start.15 = (f32[16,4]{0,1:T(4,128)S(1)}, f32[16,4]{0,1:T(4,128)}, u32[]{:S(2)}) copy-start(f32[16,4]{0,1:T(4,128)} %param.33) | copy-start | bytes 772
  0.7 68.8 %copy-start.14 = (f32[16,4]{0,1:T(4,128)S(1)}, f32[16,4]{0,1:T(4,128)}, u32[]{:S(2)}) copy-start(f32[16,4]{0,1:T(4,128)} %param.34) | copy-start | bytes 772
  0.7 68.8 %copy-start.16 = (s32[32]{0:T(128)S(1)}, s32[32]{0:T(128)}, u32[]{:S(2)}) copy-start(s32[32]{0:T(128)} %param.37) | copy-start | bytes 388
  0.7 69.6 %copy-start.10 = (s32[2048]{0:T(1024)S(1)}, s32[2048]{0:T(1024)}, u32[]{:S(2)}) copy-start(s32[2048]{0:T(1024)} %param.36) | copy-start | bytes 24580
  222.5 109.6 %copy-start.12 = (f32[1,1024]{1,0:T(1,128)S(1)}, f32[1,1024]{1,0:T(1,128)}, u32[]{:S(2)}) copy-start(f32[1,1024]{1,0:T(1,128)} %get-tuple-element.90) | copy-start | bytes 12292
  222.5 109.9 %copy-start.11 = (f32[8,1024]{1,0:T(8,128)S(1)}, f32[8,1024]{1,0:T(8,128)}, u32[]{:S(2)}) copy-start(f32[8,1024]{1,0:T(8,128)} %get-tuple-element.91) | copy-start | bytes 98308
  333.7 73.3 %copy-start.17 = (bf16[64]{0:T(256)(128)(2,1)S(1)}, bf16[64]{0:T(256)(128)(2,1)}, u32[]{:S(2)}) copy-start(bf16[64]{0:T(256)(128)(2,1)} %param.21) | copy-start | bytes 388
  333.7 76.4 %copy-start = (bf16[1024,1024]{1,0:T(8,128)(2,1)S(1)}, bf16[1024,1024]{1,0:T(8,128)(2,1)}, u32[]{:S(2)}) copy-start(bf16[1024,1024]{1,0:T(8,128)(2,1)} %get-tuple-element.129) | copy-start | bytes 6291460
  406.0 5.4 %copy-start.1 = (bf16[1024,1024]{1,0:T(8,128)(2,1)S(1)}, bf16[1024,1024]{1,0:T(8,128)(2,1)}, u32[]{:S(2)}) copy-start(bf16[1024,1024]{1,0:T(8,128)(2,1)} %get-tuple-element.130) | copy-start | bytes 6291460
  411.4 1.4 copy-start.9
  411.4 2.1 copy-start.8
  411.4 2.8 copy-start.7
  411.4 3.5 copy-start.6
  411.4 4.2 copy-start.5
  411.4 4.9 %copy-start.4 = (f32[128,1408]{1,0:T(8,128)S(1)}, f32[128,1408]{1,0:T(8,128)}, u32[]{:S(2)}) copy-start(f32[128,1408]{1,0:T(8,128)} %get-tuple-element.136) | copy-start | bytes 2162692
  412.7 4.4 %copy-start.3 = (f32[128,1408]{1,0:T(8,128)S(1)}, f32[128,1408]{1,0:T(8,128)}, u32[]{:S(2)}) copy-start(f32[128,1408]{1,0:T(8,128)} %get-tuple-element.137) | copy-start | bytes 2162692
  412.7 5.3 %copy-start.2 = (f32[352,512]{1,0:T(8,128)S(1)}, f32[352,512]{1,0:T(8,128)}, u32[]{:S(2)}) copy-start(f32[352,512]{1,0:T(8,128)} %get-tuple-element.138) | copy-start | bytes 2162692

commit v7 on v6

--- a/solution.py
+++ b/solution.py
@@ -379,11 +379,6 @@
     def pass_on():
         hops(1 + hop_early(turn - 1, tiles - 2, n - 2), 1 + hop_early(turn, tiles - 2, n - 2))
 
-    @pl.when(turn == tiles - 1)
-    def settle():
-        for m in order:
-            g.settle(m)
-
     for part in range(TPS):
         @pl.when(lax.rem(tile, TPS) == part)
         def work():
@@ -393,6 +388,8 @@
 
     @pl.when(turn == tiles - 1)
     def end():
+        for m in order:
+            g.settle(m)
         for m in order:
             g.drain(m)
 

time: 427 us -> 425 us (level)
  no operation moved by 1% of the time
where the time goes in v7:
time: 425 us; the launch traced here: 417 us
  Pallas kernels  390 us (92%)
  local copies, waits for them, and re-layouts  21.7 us (5%)
  other arithmetic  4.26 us (1%)
    pallas_call x1, Pallas kernels, mix_backward(): pl.pallas_call(functools.partial(mix_backward_kernel, heads, n, tiles), g...  106 us
    pallas_call x1, Pallas kernels, ffn_block(): pl.pallas_call(functools.partial(ffn_kernel, tiles), grid=(tiles,), in_sp...  80.6 us
    pallas_call x1, Pallas kernels, post(): pl.pallas_call(functools.partial(post_kernel, n), grid=(4,), in_specs=[wh...  70.8 us
    pallas_call x1, Pallas kernels, mix_forward(): pl.pallas_call(functools.partial(mix_forward_kernel, heads, n, tiles), gr...  69 us
    pallas_call x1, Pallas kernels, pre(): pl.pallas_call(functools.partial(pre_kernel, n), in_specs=[vmem_spec] * 7...  63.2 us
    unnamed x46, local copies, waits for them, and re-layouts  8.8 us

profile of v7, /device:TPU:0, one launch (start us, length us, event | category | flops | bytes accessed | tf_op | source)
XLA Modules:
  0.0 417.4 jit_solution(13380785412018446657)
XLA Ops:
  0.6 0.0 copy-start.13
  0.7 0.0 copy-start.15
  0.7 0.0 copy-start.10
  0.7 0.8 dynamic_update_slice.9
  1.6 0.8 dynamic_update_slice.10
  2.4 0.7 fusion.5
  3.1 0.6 pad_maximum_fusion.1.refs_4_
  3.7 63.2 %pre.1 = (bf16[8,128,2048]{2,1,0:T(8,128)(2,1)}, bf16[8,48,256]{2,1,0:T(8,128)(2,1)}, bf16[8,128,1024]{2,1,0:T(8,128)(2,1)}, bf16[1024,2048]{1,0:T(8,128)(2,1)},...) custom-call(bf16[128,512]{1,0:T(8,128)(2,1)} %refs_4_.1, bf16[128,512]{1,0:T(8,128)(2,1)} %refs_5_.3, ...), custom_call_target="tpu_custom_call" | custom-call | tf_op jit(solution)/shard_map/pre/pallas_call | solution.py:915
  66.9 0.9 slice.55
  67.9 0.1 copy_bitcast_fusion
  68.0 0.1 reshape.144
  68.1 0.7 pad.16.pk_ref
  68.8 0.7 pad.17.pv_ref
  69.5 0.0 copy-done.15
  69.5 0.2 fusion.3
  69.7 0.1 copy.46
  69.8 0.1 stack.12
  69.9 0.1 copy.47
  70.0 0.1 stack.13
  70.1 0.1 copy.48
  70.2 0.1 stack.14
  70.3 0.1 reshape.145
  70.4 0.2 fusion.4
  70.6 0.1 fusion.12
  70.6 0.1 stack_broadcast_in_dim.13
  70.7 0.1 stack_broadcast_in_dim.14
  70.8 0.6 pad_maximum_fusion.2.coef_ref
  71.4 1.3 copy.49.segc_ref
  72.8 69.0 %mix_forward.1 = (f32[2048,128]{1,0:T(8,128)}, bf16[2048,512]{1,0:T(8,128)(2,1)}, bf16[32,4,128,128]{3,2,1,0:T(8,128)(2,1)}, bf16[2048,512]{1,0:T(8,128)(2,1)}, ...) custom-call(bf16[2048,2048]{1,0:T(8,128)(2,1)} %get-tuple-element.61, ...), custom_call_target="tpu_custom_call" | custom-call | tf_op jit(solution)/shard_map/mix_forward/pallas_call | solution.py:195
  141.8 80.6 %ffn_block.1 = (bf16[1024,1024]{1,0:T(8,128)(2,1)}, bf16[1024,1024]{1,0:T(8,128)(2,1)}, f32[1,1024]{1,0:T(1,128)}, f32[8,1024]{1,0:T(8,128)}, bf16[2048,512]{1,0...) custom-call(bf16[1024,1024]{1,0:T(8,128)(2,1)} %get-tuple-element.63, ...), custom_call_target="tpu_custom_call" | custom-call | tf_op jit(solution)/shard_map/ffn_block/pallas_call | solution.py:603
  222.5 0.0 copy-start.12
  222.5 0.0 copy-start.11
  222.5 106.5 %mix_backward.1 = (bf16[2048,2048]{1,0:T(8,128)(2,1)}, f32[128,512]{1,0:T(8,128)}, f32[128,512]{1,0:T(8,128)}, bf16[128,512]{1,0:T(8,128)(2,1)}, bf16[128,1408]{...) custom-call(bf16[2048,2048]{1,0:T(8,128)(2,1)} %get-tuple-element.61.q_ref.k_ref.v_ref.g_ref, ...), custom_call_target="tpu_custom_call" | custom-call | tf_op jit(solution)/shard_map/mix_backward/pallas_call | solution.py:405
  328.9 0.8 slice.64
  329.7 0.8 slice.65
  330.5 0.1 pad.22.clone
  330.6 0.0 copy-done.12
  330.6 0.1 pad_maximum_fusion
  330.7 0.2 reshape.159
  330.9 0.1 fusion
  331.1 0.3 reshape.163
  331.3 0.8 copy.52.small
  332.2 70.8 %post.1 = (bf16[1024,1024]{1,0:T(8,128)(2,1)}, f32[128,512]{1,0:T(8,128)}, f32[128,512]{1,0:T(8,128)}, f32[128,512]{1,0:T(8,128)}, f32[128,512]{1,0:T(8,128)}, /...) custom-call(bf16[1024,2048]{1,0:T(8,128)(2,1)} %get-tuple-element.70, ...), custom_call_target="tpu_custom_call" | custom-call | tf_op jit(solution)/shard_map/post/pallas_call | solution.py:1265
  403.0 1.3 fusion.15
  404.3 1.0 dynamic-slice_reduce_fusion
  405.3 0.0 copy-done.17
  405.3 0.5 convert_divide_fusion
  405.9 0.8 slice_reduce_fusion
  406.7 0.5 multiply_sqrt_fusion
  407.2 1.2 slice_bitcast_fusion
  408.4 1.3 copy.70
  409.7 1.3 copy.71
  411.1 0.0 copy-done.9
  411.1 0.7 copy.72
  411.8 0.0 copy-done.8
  411.8 0.7 copy.73
  412.5 0.7 copy.74
  413.2 0.0 copy-done.6
  413.2 0.7 copy.75
  413.9 0.7 copy.76
  414.6 0.0 copy-done.4
  414.6 0.9 copy.77
  415.5 0.9 copy.78
  416.3 0.9 copy.79
  (34 shorter events, 0.2 us)
Async XLA Ops:
  0.6 68.8 %copy-start.13 = (f32[16,4]{0,1:T(4,128)S(1)}, f32[16,4]{0,1:T(4,128)}, u32[]{:S(2)}) copy-start(f32[16,4]{0,1:T(4,128)} %param.35) | copy-start | bytes 772
  0.7 68.8 %copy-start.15 = (f32[16,4]{0,1:T(4,128)S(1)}, f32[16,4]{0,1:T(4,128)}, u32[]{:S(2)}) copy-start(f32[16,4]{0,1:T(4,128)} %param.33) | copy-start | bytes 772
  0.7 68.8 %copy-start.14 = (f32[16,4]{0,1:T(4,128)S(1)}, f32[16,4]{0,1:T(4,128)}, u32[]{:S(2)}) copy-start(f32[16,4]{0,1:T(4,128)} %param.34) | copy-start | bytes 772
  0.7 68.8 %copy-start.16 = (s32[32]{0:T(128)S(1)}, s32[32]{0:T(128)}, u32[]{:S(2)}) copy-start(s32[32]{0:T(128)} %param.37) | copy-start | bytes 388
  0.7 69.6 %copy-start.10 = (s32[2048]{0:T(1024)S(1)}, s32[2048]{0:T(1024)}, u32[]{:S(2)}) copy-start(s32[2048]{0:T(1024)} %param.36) | copy-start | bytes 24580
  222.5 108.1 %copy-start.12 = (f32[1,1024]{1,0:T(1,128)S(1)}, f32[1,1024]{1,0:T(1,128)}, u32[]{:S(2)}) copy-start(f32[1,1024]{1,0:T(1,128)} %get-tuple-element.90) | copy-start | bytes 12292
  222.5 108.4 %copy-start.11 = (f32[8,1024]{1,0:T(8,128)S(1)}, f32[8,1024]{1,0:T(8,128)}, u32[]{:S(2)}) copy-start(f32[8,1024]{1,0:T(8,128)} %get-tuple-element.91) | copy-start | bytes 98308
  332.2 73.2 %copy-start.17 = (bf16[64]{0:T(256)(128)(2,1)S(1)}, bf16[64]{0:T(256)(128)(2,1)}, u32[]{:S(2)}) copy-start(bf16[64]{0:T(256)(128)(2,1)} %param.21) | copy-start | bytes 388
  332.2 76.2 %copy-start = (bf16[1024,1024]{1,0:T(8,128)(2,1)S(1)}, bf16[1024,1024]{1,0:T(8,128)(2,1)}, u32[]{:S(2)}) copy-start(bf16[1024,1024]{1,0:T(8,128)(2,1)} %get-tuple-element.129) | copy-start | bytes 6291460
  404.3 5.4 %copy-start.1 = (bf16[1024,1024]{1,0:T(8,128)(2,1)S(1)}, bf16[1024,1024]{1,0:T(8,128)(2,1)}, u32[]{:S(2)}) copy-start(bf16[1024,1024]{1,0:T(8,128)(2,1)} %get-tuple-element.130) | copy-start | bytes 6291460
  409.7 1.4 copy-start.9
  409.7 2.1 copy-start.8
  409.7 2.8 copy-start.7
  409.7 3.5 copy-start.6
  409.7 4.2 copy-start.5
  409.7 4.9 %copy-start.4 = (f32[128,1408]{1,0:T(8,128)S(1)}, f32[128,1408]{1,0:T(8,128)}, u32[]{:S(2)}) copy-start(f32[128,1408]{1,0:T(8,128)} %get-tuple-element.136) | copy-start | bytes 2162692
  411.1 4.4 %copy-start.3 = (f32[128,1408]{1,0:T(8,128)S(1)}, f32[128,1408]{1,0:T(8,128)}, u32[]{:S(2)}) copy-start(f32[128,1408]{1,0:T(8,128)} %get-tuple-element.137) | copy-start | bytes 2162692
  411.1 5.3 %copy-start.2 = (f32[352,512]{1,0:T(8,128)S(1)}, f32[352,512]{1,0:T(8,128)}, u32[]{:S(2)}) copy-start(f32[352,512]{1,0:T(8,128)} %get-tuple-element.138) | copy-start | bytes 2162692
